TPU v7x, 32 devices: a whole 2x2x4 slice. The times are simulated.
32 devices in a mesh: section: 2 (over core), dp: 16 (over z, y, x).
Axes of the slice: x: 2, y: 2, z: 4, core: 2. Of those that a mesh axis runs over, the one named last changes fastest.
Arguments:
- inputs: bfloat16 [2, 192, 24, 1024], P('section', 'dp'), may hold values from -6 to 6
- counts: int32 [2, 192], P('section', 'dp'), may hold values from 1 to 24, as said below
- cotangent: bfloat16 [192, 24, 1000], P('dp', None, 'section'), may hold values from -6 to 6
- lstm_master: float32 [2, 2048, 4096], P('section', 'dp'), may hold values from -0.125 to 0.125
- lstm_copy: bfloat16 [2, 2048, 4096], P('section', 'dp')
- lstm_first: float32 [2, 2048, 4096], P('section', 'dp')
- lstm_second: float32 [2, 2048, 4096], P('section', 'dp')
- mats_master: float32 [3, 1024, 2048], P(None, None, ('section', 'dp')), may hold values from -0.1875 to 0.1875
- mats_copy: bfloat16 [3, 1024, 2048], P(None, None, ('section', 'dp')), may hold values from -0.1875 to 0.1875
- mats_first: float32 [3, 1024, 2048], P(None, None, ('section', 'dp'))
- mats_second: float32 [3, 1024, 2048], P(None, None, ('section', 'dp'))
- out_master: float32 [1024, 1000], P('dp', 'section'), may hold values from -0.1875 to 0.1875
- out_copy: bfloat16 [1024, 1000], P('dp', 'section'), may hold values from -0.1875 to 0.1875
- out_first: float32 [1024, 1000], P('dp', 'section')
- out_second: float32 [1024, 1000], P('dp', 'section')
- vec_master: float32 [8, 2048], P(None, ('section', 'dp'))
- vec_first: float32 [8, 2048], P(None, ('section', 'dp'))
- vec_second: float32 [8, 2048], P(None, ('section', 'dp'))
Outputs:
- logits: bfloat16 [192, 24, 1000], P('dp', None, 'section')
- grad_inputs: float32 [2, 192, 24, 1024], P('section', 'dp')
- lstm_new: float32 [2, 2048, 4096], P('section', 'dp')
- lstm_first_new: float32 [2, 2048, 4096], P('section', 'dp')
- lstm_second_new: float32 [2, 2048, 4096], P('section', 'dp')
- lstm_copy_new: bfloat16 [2, 2048, 4096], P('section', 'dp')
- mats_new: float32 [3, 1024, 2048], P(None, None, ('section', 'dp'))
- mats_first_new: float32 [3, 1024, 2048], P(None, None, ('section', 'dp'))
- mats_second_new: float32 [3, 1024, 2048], P(None, None, ('section', 'dp'))
- mats_copy_new: bfloat16 [3, 1024, 2048], P(None, None, ('section', 'dp'))
- out_new: float32 [1024, 1000], P('dp', 'section')
- out_first_new: float32 [1024, 1000], P('dp', 'section')
- out_second_new: float32 [1024, 1000], P('dp', 'section')
- out_copy_new: bfloat16 [1024, 1000], P('dp', 'section')
- vec_new: float32 [8, 2048], P(None, ('section', 'dp'))
- vec_first_new: float32 [8, 2048], P(None, ('section', 'dp'))
- vec_second_new: float32 [8, 2048], P(None, ('section', 'dp'))
Inputs may be any that keep to these rules, and one draw needn't show every extreme that they name: counts[0, u] frames and counts[1, u] labels of utterance u; the first utterance of each aligned block of 12 has 24 of both.
All inputs are finite; a program needn't handle non-finite values.
Results may differ from a plain program's by a relative error of at most 0.012.
The roundings to bfloat16 on the way count: a program that leaves them out, or rounds other values in their place, can miss the bound.
Values may be sent and summed in bfloat16 or wider, within the bound.
A program may use at most 256 MiB of HBM per device.

v0:
```python
import jax
import jax.numpy as jnp
from jax import lax
from jax.sharding import PartitionSpec as P

STEP = 5


NORM_EPS = 1e-05
ENERGY_OFFSET = -4.0
BETA_ONE = 0.9
BETA_TWO = 0.999
ADAM_EPS = 1e-08
WEIGHT_DECAY = 0.01
RATE_LSTM = 0.05
RATE_MATRIX = 0.02
RATE_VECTOR = 0.3
HIGH = lax.Precision.HIGHEST


def shifted(block, axis, distance):
    devices = range(lax.axis_size(axis))
    route = [(i - distance, i) for i in devices if i - distance in devices]
    return lax.ppermute(block, axis, route)


def contract(left, right, left_dim, right_dim):
    return lax.dot_general(
        left, right, (((left_dim,), (right_dim,)), ((), ())), preferred_element_type=jnp.float32
    )


def energies(queries, keys, shifts, weights):

    def single(operands):
        query_rows, key_rows = operands
        squash_all = jnp.tanh(query_rows[:, None, :] + key_rows[None, :, :] + shifts)
        return jnp.einsum("ijk,k->ij", squash_all, weights, precision=HIGH)

    return lax.map(jax.checkpoint(single), (queries, keys))


def align(queries, keys, shifts, weights, frame_mask):
    half_width = queries.shape[-1] // 2
    length = queries.shape[1]
    monotone = (
        energies(
            queries[..., :half_width],
            keys[..., :half_width],
            shifts[:half_width],
            weights[:half_width],
        )
        + ENERGY_OFFSET
    )
    windowed = energies(
        queries[..., half_width:], keys[..., half_width:], shifts[half_width:], weights[half_width:]
    )
    frame_rows = frame_mask[:, None, :]
    select = jax.nn.sigmoid(monotone) * frame_rows
    leave_rate = jax.nn.softplus(monotone) * frame_rows
    row_index = lax.broadcasted_iota(jnp.int32, (length, length), 0)
    col_index = lax.broadcasted_iota(jnp.int32, (length, length), 1)
    before = (row_index < col_index).astype(jnp.float32)
    cumulated = jnp.einsum("uij,jl->uil", leave_rate, before, precision=HIGH)
    below = row_index >= col_index
    spacing = jnp.where(below, cumulated[:, :, :, None] - cumulated[:, :, None, :], 0.0)
    transfer = jnp.exp(-spacing) * below.astype(jnp.float32)
    first_slot = (col_index[0] == 0).astype(jnp.float32)
    initial = jnp.broadcast_to(first_slot, (queries.shape[0], length))

    def align_advance(previous, items):
        moving, probable = items
        waiting = jnp.einsum("ujk,uk->uj", moving, previous, precision=HIGH)
        current = probable * waiting
        return (current, current)

    _, alignments = lax.scan(
        align_advance, initial, (jnp.swapaxes(transfer, 0, 1), jnp.swapaxes(select, 0, 1))
    )
    alignment = jnp.swapaxes(alignments, 0, 1)
    earlier = jnp.concatenate([windowed[..., :1], windowed[..., :-1]], -1)
    later = jnp.concatenate([windowed[..., 1:], windowed[..., -1:]], -1)
    own_factor = jnp.where(col_index[0] == 0, 1.0, jax.nn.sigmoid(windowed - earlier))
    next_alignment = jnp.concatenate([alignment[..., 1:], jnp.zeros_like(alignment[..., :1])], -1)
    return alignment * own_factor + next_alignment * jax.nn.sigmoid(windowed - later)


def recur_forward(sequence, weight, bias):
    batch_size, length, model_width = sequence.shape
    inflow = jnp.dot(
        sequence.reshape(batch_size * length, model_width),
        weight[:model_width],
        preferred_element_type=jnp.float32,
    )
    inflow = inflow.reshape(batch_size, length, -1) + bias
    recurrent = weight[model_width:]

    def recur_advance(carried, inflow_now):
        hidden, cell_state = carried
        gate_sums = inflow_now + jnp.dot(hidden, recurrent, preferred_element_type=jnp.float32)
        cell_new = jax.nn.sigmoid(
            gate_sums[:, model_width : 2 * model_width]
        ) * cell_state + jax.nn.sigmoid(gate_sums[:, :model_width]) * jnp.tanh(
            gate_sums[:, 2 * model_width : 3 * model_width]
        )
        hidden_new = (jax.nn.sigmoid(gate_sums[:, 3 * model_width :]) * jnp.tanh(cell_new)).astype(
            jnp.bfloat16
        )
        return ((hidden_new, cell_new), (gate_sums, cell_new, hidden_new))

    initial = (
        jnp.zeros((batch_size, model_width), jnp.bfloat16),
        jnp.zeros((batch_size, model_width), jnp.float32),
    )
    _, (gate_sums, cell_states, hiddens) = lax.scan(
        recur_advance, initial, jnp.swapaxes(inflow, 0, 1)
    )
    return (gate_sums, cell_states, hiddens)


def recur_backward(sequence, weight, gate_sums, cell_states, hiddens, outer):
    batch_size, length, model_width = sequence.shape
    recurrent = weight[model_width:]
    cells_before = jnp.concatenate([jnp.zeros_like(cell_states[:1]), cell_states[:-1]], 0)

    def retreat(carried, items):
        grad_hidden, grad_cell = carried
        gate_now, cell_now, cell_prior, outer_now = items
        in_gate = jax.nn.sigmoid(gate_now[:, :model_width])
        forget = jax.nn.sigmoid(gate_now[:, model_width : 2 * model_width])
        candidate = jnp.tanh(gate_now[:, 2 * model_width : 3 * model_width])
        out_gate = jax.nn.sigmoid(gate_now[:, 3 * model_width :])
        squash_cell = jnp.tanh(cell_now)
        hidden_total = outer_now + grad_hidden
        cell_total = grad_cell + hidden_total * out_gate * (1.0 - squash_cell * squash_cell)
        gate_grads = jnp.concatenate(
            [
                cell_total * candidate * in_gate * (1.0 - in_gate),
                cell_total * cell_prior * forget * (1.0 - forget),
                cell_total * in_gate * (1.0 - candidate * candidate),
                hidden_total * squash_cell * out_gate * (1.0 - out_gate),
            ],
            -1,
        ).astype(jnp.bfloat16)
        hidden_back = contract(gate_grads, recurrent, 1, 1)
        return ((hidden_back, cell_total * forget), gate_grads)

    initial = (
        jnp.zeros((batch_size, model_width), jnp.float32),
        jnp.zeros((batch_size, model_width), jnp.float32),
    )
    _, gate_grads = lax.scan(
        retreat, initial, (gate_sums, cell_states, cells_before, outer), reverse=True
    )
    flat_grads = gate_grads.reshape(length * batch_size, -1)
    hidden_before = jnp.concatenate([jnp.zeros_like(hiddens[:1]), hiddens[:-1]], 0).reshape(
        length * batch_size, model_width
    )
    sequence_flat = jnp.swapaxes(sequence, 0, 1).reshape(length * batch_size, model_width)
    weight_grad = jnp.concatenate(
        [contract(sequence_flat, flat_grads, 0, 0), contract(hidden_before, flat_grads, 0, 0)], 0
    )
    bias_grad = jnp.sum(flat_grads, 0, dtype=jnp.float32)
    input_grad = contract(flat_grads, weight[:model_width], 1, 1).reshape(
        length, batch_size, model_width
    )
    return (weight_grad, bias_grad, jnp.swapaxes(input_grad, 0, 1))


def adamw(master, first, second, grad, rate):
    first_new = BETA_ONE * first + (1.0 - BETA_ONE) * grad
    second_new = BETA_TWO * second + (1.0 - BETA_TWO) * grad * grad
    first_hat = first_new / (1.0 - BETA_ONE**STEP)
    second_hat = second_new / (1.0 - BETA_TWO**STEP)
    master_new = master - rate * (
        first_hat / (jnp.sqrt(second_hat) + ADAM_EPS) + WEIGHT_DECAY * master
    )
    return (master_new, first_new, second_new)


def local(
    inputs,
    counts,
    cotangent,
    lstm_master,
    lstm_copy,
    lstm_first,
    lstm_second,
    mats_master,
    mats_copy,
    mats_first,
    mats_second,
    out_master,
    out_copy,
    out_first,
    out_second,
    vec_master,
    vec_first,
    vec_second,
):
    section_index = lax.axis_index("section")
    on_encoder = section_index == 0
    lstm_full, out_half = (
        lax.all_gather(lstm_copy, "dp", axis=1, tiled=True),
        lax.all_gather(out_copy, "dp", axis=0, tiled=True),
    )
    mats_full, vectors_low = (
        lax.all_gather(mats_copy, ("section", "dp"), axis=2, tiled=True),
        lax.all_gather(vec_master.astype(jnp.bfloat16), ("section", "dp"), axis=1, tiled=True),
    )
    vectors = vectors_low.astype(jnp.float32)
    weight = lstm_full[0]
    model_width = weight.shape[0] // 2
    vocab_half = out_half.shape[1]
    sequence = inputs[0]
    batch_size, length, _ = sequence.shape
    slot_index = lax.broadcasted_iota(jnp.int32, (batch_size, length), 1)
    slot_mask = (slot_index < counts[0][:, None]).astype(jnp.float32)
    raw_values = sequence.astype(jnp.float32)
    norm_gain = vectors[4, :model_width]
    center = raw_values - jnp.mean(raw_values, -1, keepdims=True)
    spread = lax.rsqrt(jnp.mean(center * center, -1, keepdims=True) + NORM_EPS)
    scaled = center * spread
    normed = jnp.where(
        on_encoder, scaled * norm_gain + vectors[4, model_width:], raw_values
    ).astype(jnp.bfloat16)
    bias_here = lax.dynamic_slice_in_dim(vectors, 2 * section_index, 2, 0).reshape(-1)
    gate_sums, cell_states, hiddens = recur_forward(normed, weight, bias_here)
    states = jnp.swapaxes(hiddens, 0, 1)
    memory_out = (raw_values + states.astype(jnp.float32)).astype(jnp.bfloat16)
    memory_in, frames_low = shifted((memory_out, slot_mask.astype(jnp.bfloat16)), "section", 1)
    frame_mask = frames_low.astype(jnp.float32)

    def attend(operands):
        states_in, memory_now, mask_now = operands
        query_all = jnp.dot(
            states_in.reshape(-1, model_width), mats_full[0], preferred_element_type=jnp.float32
        ).reshape(batch_size, length, -1)
        key_all = jnp.dot(
            memory_now.reshape(-1, model_width), mats_full[1], preferred_element_type=jnp.float32
        ).reshape(batch_size, length, -1)
        beta_low = align(query_all, key_all, vectors[5], vectors[6], mask_now).astype(jnp.bfloat16)
        context = jnp.einsum(
            "uik,ukd->uid", beta_low, memory_now, preferred_element_type=jnp.float32
        ).astype(jnp.bfloat16)
        joined = jnp.concatenate([states_in, context], -1).reshape(-1, 2 * model_width)
        before_tanh = contract(joined, mats_full[2], 1, 1) + vectors[7, :model_width]
        squashed = jnp.tanh(before_tanh).reshape(batch_size, length, model_width)
        return (squashed, beta_low, context, query_all, key_all)

    def attend_spare(operands):
        return (
            jnp.zeros((batch_size, length, model_width), jnp.float32),
            jnp.zeros((batch_size, length, length), jnp.bfloat16),
            jnp.zeros((batch_size, length, model_width), jnp.bfloat16),
            jnp.zeros((batch_size, length, 2 * model_width), jnp.float32),
            jnp.zeros((batch_size, length, 2 * model_width), jnp.float32),
        )

    squashed, beta_low, context, query_all, key_all = lax.cond(
        section_index == 1, attend, attend_spare, (states, memory_in, frame_mask)
    )
    hidden_sent, labels_low = shifted(
        (squashed.astype(jnp.bfloat16), slot_mask.astype(jnp.bfloat16)), "section", -1
    )
    hidden_low = jnp.where(on_encoder, hidden_sent, squashed.astype(jnp.bfloat16))
    label_rows = jnp.where(on_encoder, labels_low.astype(jnp.float32), slot_mask)
    out_bias = lax.dynamic_slice_in_dim(
        vectors[7], model_width + section_index * vocab_half, vocab_half
    )
    flat_hidden = hidden_low.reshape(-1, model_width)
    logits = (
        jnp.dot(flat_hidden, out_half, preferred_element_type=jnp.float32) + out_bias
    ).reshape(batch_size, length, vocab_half)
    grad_logits = (
        (cotangent.astype(jnp.float32) * label_rows[:, :, None])
        .astype(jnp.bfloat16)
        .reshape(-1, vocab_half)
    )
    out_grad = contract(flat_hidden, grad_logits, 0, 0)
    out_bias_grad = jnp.sum(grad_logits, 0, dtype=jnp.float32)
    hidden_part = contract(grad_logits, out_half, 1, 1)
    hidden_other = shifted(hidden_part, "section", 1)
    hidden_grad = hidden_part + hidden_other

    def attend_back(operands):
        (
            grad_now,
            squash_now,
            beta_now,
            context_now,
            query_now,
            key_now,
            states_in,
            memory_now,
            mask_now,
        ) = operands
        squash_flat = squash_now.reshape(-1, model_width)
        grad_before = (grad_now * (1.0 - squash_flat * squash_flat)).astype(jnp.bfloat16)
        joined = jnp.concatenate([states_in, context_now], -1).reshape(-1, 2 * model_width)
        proj_grad = contract(grad_before, joined, 0, 0)
        proj_bias_grad = jnp.sum(grad_before, 0, dtype=jnp.float32)
        joined_grad = jnp.dot(grad_before, mats_full[2], preferred_element_type=jnp.float32)
        states_grad = joined_grad[:, :model_width]
        context_grad = (
            joined_grad[:, model_width:]
            .astype(jnp.bfloat16)
            .reshape(batch_size, length, model_width)
        )
        beta_grad = jnp.einsum(
            "uid,ukd->uik", context_grad, memory_now, preferred_element_type=jnp.float32
        )
        memory_grad = jnp.einsum(
            "uik,uid->ukd", beta_now, context_grad, preferred_element_type=jnp.float32
        )

        def local_align(query_part, key_part, shift_part, vector_part):
            return align(query_part, key_part, shift_part, vector_part, mask_now)

        _, pullback = jax.vjp(local_align, query_now, key_now, vectors[5], vectors[6])
        query_grad, key_grad, shift_grad, vector_grad_part = pullback(beta_grad)
        query_flat = query_grad.astype(jnp.bfloat16).reshape(-1, 2 * model_width)
        key_flat = key_grad.astype(jnp.bfloat16).reshape(-1, 2 * model_width)
        query_weight_grad = contract(states_in.reshape(-1, model_width), query_flat, 0, 0)
        key_weight_grad = contract(memory_now.reshape(-1, model_width), key_flat, 0, 0)
        states_grad = states_grad + contract(query_flat, mats_full[0], 1, 1)
        memory_total = memory_grad.reshape(-1, model_width) + contract(key_flat, mats_full[1], 1, 1)
        mats_grad = jnp.stack([query_weight_grad, key_weight_grad, proj_grad])
        tail_rows = jnp.stack(
            [
                shift_grad,
                vector_grad_part,
                jnp.concatenate([proj_bias_grad, jnp.zeros((model_width,), jnp.float32)]),
            ]
        )
        return (
            mats_grad,
            tail_rows,
            states_grad.reshape(batch_size, length, model_width),
            memory_total.astype(jnp.bfloat16).reshape(batch_size, length, model_width),
        )

    def back_spare(operands):
        return (
            jnp.zeros((3, model_width, 2 * model_width), jnp.float32),
            jnp.zeros((3, 2 * model_width), jnp.float32),
            jnp.zeros((batch_size, length, model_width), jnp.float32),
            jnp.zeros((batch_size, length, model_width), jnp.bfloat16),
        )

    mats_grad, tail_rows, states_grad, memory_grad = lax.cond(
        section_index == 1,
        attend_back,
        back_spare,
        (
            hidden_grad,
            squashed,
            beta_low,
            context,
            query_all,
            key_all,
            states,
            memory_in,
            frame_mask,
        ),
    )
    memory_back = shifted(memory_grad, "section", -1)
    memory_back_f = memory_back.astype(jnp.float32)
    outer = jnp.where(on_encoder, memory_back_f, states_grad)
    weight_grad, bias_grad, input_grad = recur_backward(
        normed, weight, gate_sums, cell_states, hiddens, jnp.swapaxes(outer, 0, 1)
    )
    gain_grad = jnp.sum(input_grad * scaled, (0, 1))
    shift_grad_norm = jnp.sum(input_grad, (0, 1))
    scaled_grad = input_grad * norm_gain
    norm_back = spread * (
        scaled_grad
        - jnp.mean(scaled_grad, -1, keepdims=True)
        - scaled * jnp.mean(scaled_grad * scaled, -1, keepdims=True)
    )
    inputs_grad = jnp.where(on_encoder, norm_back + memory_back_f, input_grad)
    lstm_rows = lax.dynamic_update_slice(
        jnp.zeros((4, 2 * model_width), jnp.float32),
        bias_grad.reshape(2, -1),
        (2 * section_index, 0),
    )
    norm_row = jnp.where(on_encoder, jnp.concatenate([gain_grad, shift_grad_norm]), 0.0)
    logit_row = lax.dynamic_update_slice(
        jnp.zeros((2 * model_width,), jnp.float32),
        out_bias_grad,
        (model_width + section_index * vocab_half,),
    )
    vector_grad = jnp.concatenate(
        [lstm_rows, norm_row[None], tail_rows[:2], (tail_rows[2] + logit_row)[None]], 0
    )
    lstm_sum, out_sum = (
        lax.psum_scatter(weight_grad[None], "dp", scatter_dimension=1, tiled=True),
        lax.psum_scatter(out_grad, "dp", scatter_dimension=0, tiled=True),
    )
    mats_sum, vector_sum = (
        lax.psum_scatter(mats_grad, ("section", "dp"), scatter_dimension=2, tiled=True),
        lax.psum_scatter(vector_grad, ("section", "dp"), scatter_dimension=1, tiled=True),
    )
    lstm_new, lstm_first_new, lstm_second_new = adamw(
        lstm_master, lstm_first, lstm_second, lstm_sum, RATE_LSTM
    )
    mats_new, mats_first_new, mats_second_new = adamw(
        mats_master, mats_first, mats_second, mats_sum, RATE_MATRIX
    )
    out_new, out_first_new, out_second_new = adamw(
        out_master, out_first, out_second, out_sum, RATE_MATRIX
    )
    vec_new, vec_first_new, vec_second_new = adamw(
        vec_master, vec_first, vec_second, vector_sum, RATE_VECTOR
    )
    return (
        logits.astype(jnp.bfloat16),
        inputs_grad[None],
        lstm_new,
        lstm_first_new,
        lstm_second_new,
        lstm_new.astype(jnp.bfloat16),
        mats_new,
        mats_first_new,
        mats_second_new,
        mats_new.astype(jnp.bfloat16),
        out_new,
        out_first_new,
        out_second_new,
        out_new.astype(jnp.bfloat16),
        vec_new,
        vec_first_new,
        vec_second_new,
    )


def solution(mesh):
    return jax.shard_map(
        local,
        mesh=mesh,
        in_specs=(
            P("section", "dp", None, None),
            P("section", "dp"),
            P("dp", None, "section"),
            P("section", "dp", None),
            P("section", "dp", None),
            P("section", "dp", None),
            P("section", "dp", None),
            P(None, None, ("section", "dp")),
            P(None, None, ("section", "dp")),
            P(None, None, ("section", "dp")),
            P(None, None, ("section", "dp")),
            P("dp", "section"),
            P("dp", "section"),
            P("dp", "section"),
            P("dp", "section"),
            P(None, ("section", "dp")),
            P(None, ("section", "dp")),
            P(None, ("section", "dp")),
        ),
        out_specs=(
            P("dp", None, "section"),
            P("section", "dp", None, None),
            P("section", "dp", None),
            P("section", "dp", None),
            P("section", "dp", None),
            P("section", "dp", None),
            P(None, None, ("section", "dp")),
            P(None, None, ("section", "dp")),
            P(None, None, ("section", "dp")),
            P(None, None, ("section", "dp")),
            P("dp", "section"),
            P("dp", "section"),
            P("dp", "section"),
            P("dp", "section"),
            P(None, ("section", "dp")),
            P(None, ("section", "dp")),
            P(None, ("section", "dp")),
        ),
        check_vma=False,
    )
```

profile of v0, /device:TPU:0, one launch (start us, length us, event | category | flops | bytes accessed | tf_op | source)
XLA Modules:
  0.0 2925.8 jit_solution(829591026056509668)
XLA Ops:
  13.0 72.9 %all-gather = bf16[32,64,8]{1,2,0:T(8,128)(2,1)S(1)} all-gather(bf16[1,64,8]{1,2,0:T(8,128)(2,1)S(1)} %convert_bitcast_fusion.1), channel_id=1, replica_groups=mesh['section'=2,'dp'=16] {'section','dp'}, dimensions={0}, use_global_device_ids=true | all-gather | bytes 33792 | tf_op jit(solution)/shard_map/all_gather | solution.py:209
  86.0 49.8 %all_gather.15 = bf16[1024,500]{1,0:T(8,128)(2,1)S(1)} all-gather(bf16[64,500]{1,0:T(8,128)(2,1)S(1)} %copy-done.71), channel_id=1, replica_groups=mesh['section'=2,'dp'=16] {'dp'}, dimensions={0}, use_global_device_ids=true | all-gather | bytes 1088000 | tf_op jit(solution)/shard_map/all_gather | solution.py:205
  142.1 74.8 %all-gather.6.cloned.1.call-done = bf16[1,2048,4096]{2,1,0:T(8,128)(2,1)} async-done(((bf16[1,128,4096]{2,1,0:T(8,128)(2,1)}), bf16[1,2048,4096]{2,1,0:T(8,128)(2,1)}) %all-gather.6.cloned.1.call-update) | async-done | bytes 16777232 | tf_op jit(solution)/shard_map/all_gather | solution.py:204
  216.9 7.8 slice_bitcast_fusion.24
  224.8 8.6 fusion.186
  233.4 184.6 %while.188 = (s32[]{:T(128)}, bf16[12,1024]{1,0:T(8,128)(2,1)S(1)}, f32[12,1024]{1,0:T(8,128)S(1)}, f32[24,12,4096]{2,1,0:T(8,128)}, f32[24,12,1024]{2,1,0:T(8,1...) while((s32[]{:T(128)}, bf16[12,1024]{1,0:T(8,128)(2,1)S(1)}, ...), condition=%wide.region_3.4_spmd.clone, body=%wide.region_2.3_spmd.clone.sunk | while | flops 100909056 | bytes 10035336 | solution.py:115
  273.2 6.1 bitcast_dynamic-update-slice_fusion.17
  297.0 5.6 bitcast_dynamic-update-slice_fusion.17
  423.9 14.8 conditional.2
  439.6 20.5 conditional.3
  441.9 11.6 broadcast.255
  468.7 775.7 %collective-permute-done.5 = bf16[12,24,1024]{2,1,0:T(8,128)(2,1)S(1)} collective-permute-done((bf16[12,24,1024]{2,1,0:T(8,128)(2,1)}, bf16[12,24,1024]{2,1,0:T(8,128)(2,1)S(1)}, u32[]{:S(2)}, u32[]{:S(2)}) %collective-permute-start.5) | collective-permute-done | bytes 589856 | tf_op jit(solution)/shard_map/ppermute | solution.py:24
  1246.4 204.8 %while.189 = (s32[]{:T(128)}, f32[12,1024]{1,0:T(8,128)S(1)}, f32[12,1024]{1,0:T(8,128)S(1)}, bf16[24,12,4096]{2,1,0:T(8,128)(2,1)S(1)}, f32[24,12,1024]{2,1,0:T...) while((s32[]{:T(128)}, f32[12,1024]{1,0:T(8,128)S(1)}, ...), condition=%wide.region_36.37_spmd.clone, body=%wide.region_35.36_spmd.clone.sunk | while | flops 101941248 | bytes 9928867 | solution.py:152
  1257.8 5.6 fusion.329
  1266.4 5.6 fusion.329
  1274.9 5.6 fusion.329
  1283.4 5.6 fusion.329
  1292.0 5.6 fusion.329
  1300.5 5.6 fusion.329
  1309.0 5.6 fusion.329
  1317.6 5.6 fusion.329
  1326.1 5.6 fusion.329
  1334.6 5.6 fusion.329
  1343.2 5.6 fusion.329
  1452.8 9.1 fusion.202
  1477.5 6.9 convolution_bitcast_fusion.4
  1484.4 11.6 maximum_bitcast_fusion
  1502.9 106.7 %reduce-scatter.13.cloned.1.call-done = f32[64,8]{1,0:T(8,128)} async-done(((f32[2048,8]{1,0:T(8,128)}), f32[64,8]{1,0:T(8,128)}) %reduce-scatter.13.cloned.1.call-update) | async-done | bytes 2064
  1611.0 78.5 %reduce-scatter.11.cloned.1.call-done = f32[64,500]{1,0:T(8,128)} async-done(((f32[1024,500]{1,0:T(8,128)}), f32[64,500]{1,0:T(8,128)}) %reduce-scatter.11.cloned.1.call-update) | async-done | bytes 128016 | tf_op jit(solution)/shard_map/reduce_scatter | solution.py:398
  1691.3 529.4 %reduce-scatter.9.cloned.1.call-done = f32[3,1024,64]{1,2,0:T(8,128)} async-done(((f32[3,1024,2048]{1,2,0:T(8,128)}), f32[3,1024,64]{1,2,0:T(8,128)}) %reduce-scatter.9.cloned.1.call-update) | async-done | bytes 786448 | tf_op jit(solution)/shard_map/reduce_scatter | solution.py:401
  2224.3 687.0 %reduce-scatter.7.cloned.1.call-done = f32[1,128,4096]{2,1,0:T(8,128)} async-done(((f32[1,2048,4096]{2,1,0:T(8,128)}), f32[1,128,4096]{2,1,0:T(8,128)}) %reduce-scatter.7.cloned.1.call-update) | async-done | bytes 2097168 | tf_op jit(solution)/shard_map/reduce_scatter | solution.py:397
  2911.4 7.1 fusion.242
  (374 shorter events, 381.6 us)
Async XLA Ops:
  7.2 78.8 %copy-start.71 = (bf16[64,500]{1,0:T(8,128)(2,1)S(1)}, bf16[64,500]{1,0:T(8,128)(2,1)}, u32[]{:S(2)}) copy-start(bf16[64,500]{1,0:T(8,128)(2,1)} %param.56) | copy-start | bytes 192004
  7.2 209.7 %all-gather.6.cloned.1.call-start = ((), (), s32[]{:S(2)}) async-start(), calls=%async_computation.5 | async-start | bytes 17825792 | tf_op jit(solution)/shard_map/all_gather | solution.py:204
  7.9 415.1 %all-gather.4.cloned.1.call-start = ((), (), s32[]{:S(2)}) async-start(), calls=%async_computation.4 | async-start | bytes 12976128 | tf_op jit(solution)/shard_map/all_gather | solution.py:208
  8.7 128.7 %copy-start.94 = (s32[1,12]{1,0:T(1,128)S(1)}, s32[1,12]{1,0:T(1,128)}, u32[]{:S(2)}) copy-start(s32[1,12]{1,0:T(1,128)} %param.45) | copy-start | bytes 148
  8.7 128.8 %copy-start.46 = (bf16[12,24,500]{2,1,0:T(8,128)(2,1)S(1)}, bf16[12,24,500]{2,1,0:T(8,128)(2,1)}, u32[]{:S(2)}) copy-start(bf16[12,24,500]{2,1,0:T(8,128)(2,1)} %param.46) | copy-start | bytes 864004
  8.7 128.7 %collective-permute-start.3 = (bf16[12,24]{1,0:T(8,128)(2,1)S(1)}, bf16[12,24]{1,0:T(8,128)(2,1)S(1)}, u32[]{:S(2)}, u32[]{:S(2)}) collective-permute-start(bf16[12,24]{1,0:T(8,128)(2,1)S(1)} %convert_convert_fusion), channel_id=1, source_target_pairs={{16,0},{17,1},{18,2},{19,3},{20,4},{21,5},{22,6},{23,7},{24,8},{25... | collective-permute-start | bytes 1736 | tf_op jit(solution)/shard_map/ppermute | solution.py:24
  10.2 1599.4 %reduce-scatter.13.cloned.1.call-start = ((), (), s32[]{:S(2)}) async-start(), calls=%async_computation.9 | async-start | bytes 1081344
  12.4 124.9 %copy-start.48 = (f32[12,24]{0,1:T(8,128)}, f32[12,24]{0,1:T(8,128)S(1)}, u32[]{:S(2)}) copy-start(f32[12,24]{0,1:T(8,128)S(1)} %broadcast_multiply_fusion.2) | copy-start | bytes 3460
  12.9 124.4 %copy-start.66 = (f32[12,24]{0,1:T(8,128)}, f32[12,24]{0,1:T(8,128)S(1)}, u32[]{:S(2)}) copy-start(f32[12,24]{0,1:T(8,128)S(1)} %add_rsqrt_fusion) | copy-start | bytes 3460
  86.0 352.8 %copy-start.47 = (f32[2048,8]{0,1:T(8,128)}, f32[2048,8]{0,1:T(8,128)S(1)}, u32[]{:S(2)}) copy-start(f32[2048,8]{0,1:T(8,128)S(1)} %reshape.381) | copy-start | bytes 196612
  86.0 51.3 %copy-start.75 = (f32[1,1024]{1,0:T(1,128)}, f32[1,1024]{1,0:T(1,128)S(1)}, u32[]{:S(2)}) copy-start(f32[1,1024]{1,0:T(1,128)S(1)} %get-tuple-element.2071) | copy-start | bytes 12292
  86.0 51.3 %copy-start.79 = (f32[1,1024]{1,0:T(1,128)}, f32[1,1024]{1,0:T(1,128)S(1)}, u32[]{:S(2)}) copy-start(f32[1,1024]{1,0:T(1,128)S(1)} %get-tuple-element.2072) | copy-start | bytes 12292
  135.8 89.0 %copy-start.13 = (bf16[1024,500]{1,0:T(8,128)(2,1)}, bf16[1024,500]{1,0:T(8,128)(2,1)S(1)}, u32[]{:S(2)}) copy-start(bf16[1024,500]{1,0:T(8,128)(2,1)S(1)} %all_gather.15) | copy-start | bytes 3072004
  138.3 86.5 %copy-start.29 = (bf16[12,24,500]{2,1,0:T(8,128)(2,1)}, bf16[12,24,500]{2,1,0:T(8,128)(2,1)S(1)}, u32[]{:S(2)}) copy-start(bf16[12,24,500]{2,1,0:T(8,128)(2,1)S(1)} %get-tuple-element.1998) | copy-start | bytes 864004
  139.8 298.9 %collective-permute-start.4 = (f32[288,1024]{1,0:T(8,128)}, f32[288,1024]{1,0:T(8,128)}, u32[]{:S(2)}, u32[]{:S(2)}) collective-permute-start(f32[288,1024]{1,0:T(8,128)} %fusion.256), channel_id=1, source_target_pairs={{0,16},{1,17},{2,18},{3,19},{4,20},{5,21},{6,22},{7,23},{8,24},{9,... | collective-permute-start | bytes 3538952 | tf_op jit(solution)/shard_map/ppermute | solution.py:24
  418.1 20.7 copy-start.6
  418.9 4.2 collective-permute-start
  420.9 2.1 collective-permute-start.1
  461.3 783.2 %collective-permute-start.5 = (bf16[12,24,1024]{2,1,0:T(8,128)(2,1)}, bf16[12,24,1024]{2,1,0:T(8,128)(2,1)S(1)}, u32[]{:S(2)}, u32[]{:S(2)}) collective-permute-start(bf16[12,24,1024]{2,1,0:T(8,128)(2,1)} %get-tuple-element.1120), channel_id=1, source_target_pairs={{16,0},{17,1},{18,2},{19,3},{20,4},{21,5},{22,6},{23,7},{24,8},{25... | collective-permute-start | bytes 1769480 | tf_op jit(solution)/shard_map/ppermute | solution.py:24
  465.4 1000.3 %collective-permute-start.2 = (bf16[12,24,1024]{2,1,0:T(8,128)(2,1)}, bf16[12,24,1024]{2,1,0:T(8,128)(2,1)}, u32[]{:S(2)}, u32[]{:S(2)}) collective-permute-start(bf16[12,24,1024]{2,1,0:T(8,128)(2,1)} %get-tuple-element.1128), channel_id=1, source_target_pairs={{16,0},{17,1},{18,2},{19,3},{20,4},{21,5},{22,6},{23,7},{24,8},{25... | collective-permute-start | bytes 1769480 | tf_op jit(solution)/shard_map/ppermute | solution.py:24
  1451.3 21.2 copy-start.5
  1465.6 223.9 %reduce-scatter.11.cloned.1.call-start = ((), (), s32[]{:S(2)}) async-start(), calls=%async_computation.8 | async-start | bytes 2228224 | tf_op jit(solution)/shard_map/reduce_scatter | solution.py:398
  1470.1 750.6 %reduce-scatter.9.cloned.1.call-start = ((), (), s32[]{:S(2)}) async-start(), calls=%async_computation.7 | async-start | bytes 25952256 | tf_op jit(solution)/shard_map/reduce_scatter | solution.py:401
  1470.7 1440.7 %reduce-scatter.7.cloned.1.call-start = ((), (), s32[]{:S(2)}) async-start(), calls=%async_computation.6 | async-start | bytes 35651584 | tf_op jit(solution)/shard_map/reduce_scatter | solution.py:397
  1499.9 110.5 %copy-start.81 = (f32[8,64]{1,0:T(8,128)S(1)}, f32[8,64]{1,0:T(8,128)}, u32[]{:S(2)}) copy-start(f32[8,64]{1,0:T(8,128)} %param.59) | copy-start | bytes 6148
  1500.0 110.4 %copy-start.84 = (f32[8,64]{1,0:T(8,128)S(1)}, f32[8,64]{1,0:T(8,128)}, u32[]{:S(2)}) copy-start(f32[8,64]{1,0:T(8,128)} %param.60) | copy-start | bytes 6148
  1500.0 110.4 %copy-start.85 = (f32[8,64]{1,0:T(8,128)S(1)}, f32[8,64]{1,0:T(8,128)}, u32[]{:S(2)}) copy-start(f32[8,64]{1,0:T(8,128)} %param.61) | copy-start | bytes 6148
  1500.0 189.6 %copy-start.63 = (f32[64,500]{1,0:T(8,128)S(1)}, f32[64,500]{1,0:T(8,128)}, u32[]{:S(2)}) copy-start(f32[64,500]{1,0:T(8,128)} %param.55) | copy-start | bytes 384004
  1500.0 189.6 %copy-start.64 = (f32[64,500]{1,0:T(8,128)S(1)}, f32[64,500]{1,0:T(8,128)}, u32[]{:S(2)}) copy-start(f32[64,500]{1,0:T(8,128)} %param.57) | copy-start | bytes 384004
  1500.0 189.5 %copy-start.65 = (f32[64,500]{1,0:T(8,128)S(1)}, f32[64,500]{1,0:T(8,128)}, u32[]{:S(2)}) copy-start(f32[64,500]{1,0:T(8,128)} %param.58) | copy-start | bytes 384004
  1500.0 720.7 %copy-start.32 = (f32[3,1024,64]{1,2,0:T(8,128)S(1)}, f32[3,1024,64]{1,2,0:T(8,128)}, u32[]{:S(2)}) copy-start(f32[3,1024,64]{1,2,0:T(8,128)} %param.51) | copy-start | bytes 2359300
  1691.3 1220.1 %copy-start.27 = (f32[1,128,4096]{2,1,0:T(8,128)S(1)}, f32[1,128,4096]{2,1,0:T(8,128)}, u32[]{:S(2)}) copy-start(f32[1,128,4096]{2,1,0:T(8,128)} %param.47) | copy-start | bytes 6291460
  (21 other events, 52.7 us)
Sparse Core Ops, SparseCore 0:
  10.8 206.0 all-gather.5
  219.9 95.0 all-gather.3
  1465.7 143.8 reduce-scatter.12
  1612.4 77.1 reduce-scatter.10
  1691.8 528.8 reduce-scatter.8
  2223.0 688.2 reduce-scatter.6
where the time goes:
time: 2960 us; the launch traced here: 2930 us
  waiting for transfers between devices  2250 us (76%)
  matrix products  299 us (10%)
  blocking collectives  123 us (4%)
  local copies, waits for them, and re-layouts  120 us (4%)
  other arithmetic  87.3 us (3%)
    ppermute x6, waiting for transfers between devices, shifted(): return lax.ppermute(block, axis, route)  777 us
    reduce_scatter x1, waiting for transfers between devices, local(): lax.psum_scatter(weight_grad[None], 'dp', scatter_dimension=1, tiled=True)  687 us
    reduce_scatter x1, waiting for transfers between devices, local(): lax.psum_scatter(mats_grad, ('section', 'dp'), scatter_dimension=2, tiled...  529 us
    dot_general x29, matrix products, contract(): lax.dot_general(left, right, (((left_dim,), (right_dim,)), ((), ())), pre...  160 us
    dot_general x24, matrix products, recur_advance(): jnp.dot(hidden, recurrent, preferred_element_type=jnp.float32)  129 us
    unnamed x7, waiting for transfers between devices  108 us
    reduce_scatter x1, waiting for transfers between devices, local(): lax.psum_scatter(out_grad, 'dp', scatter_dimension=0, tiled=True)  78.5 us
    all_gather x1, waiting for transfers between devices, local(): lax.all_gather(lstm_copy, 'dp', axis=1, tiled=True)  74.8 us
  transfers between devices with their start and end apart: 12, of which 7 were waited for; matrix products, arithmetic and copies ran while one was open for 16% of the time, Pallas kernels for 0%

commit v1 on v0

v1 whole, which is shorter than its diff:
```python
import functools
import jax
import jax.numpy as jnp
from jax import lax
from jax.experimental import pallas as pl
from jax.experimental.pallas import tpu as pltpu

ROWS = 16
LANES = 128
ENERGY_OFFSET = -4.0
VMEM_SPEC = pl.BlockSpec(memory_space=pltpu.VMEM)
SMEM_SPEC = pl.BlockSpec(memory_space=pltpu.SMEM)
VMEM_LIMIT = 60 * 1024 * 1024


def contract(left, right, left_dim, right_dim):
    return lax.dot_general(
        left, right, (((left_dim,), (right_dim,)), ((), ())), preferred_element_type=jnp.float32
    )


def lstm_forward_kernel(x_ref, w_ref, b_ref, act_ref, cell_ref, h_ref, state):
    width = x_ref.shape[1]
    steps = x_ref.shape[0] // ROWS
    for q in range(4):
        columns = slice(q * width, (q + 1) * width)
        act_ref[:, columns] = (
            jnp.dot(x_ref[...], w_ref[:width, columns], preferred_element_type=jnp.float32)
            + b_ref[:, columns]
        )
    state[...] = jnp.zeros_like(state)
    cell_ref[:ROWS] = jnp.zeros((ROWS, width), jnp.float32)

    def step(t, carry):
        rows = pl.ds(pl.multiple_of(t * ROWS, ROWS), ROWS)
        after = pl.ds(pl.multiple_of((t + 1) * ROWS, ROWS), ROWS)
        hidden = state[...]

        def gate(q):
            columns = slice(q * width, (q + 1) * width)
            return act_ref[rows, columns] + jnp.dot(
                hidden, w_ref[width:, columns], preferred_element_type=jnp.float32
            )

        in_gate = jax.nn.sigmoid(gate(0))
        forget = jax.nn.sigmoid(gate(1))
        candidate = jnp.tanh(gate(2))
        cell = forget * cell_ref[rows] + in_gate * candidate
        out_gate = jax.nn.sigmoid(gate(3))
        hidden_new = (out_gate * jnp.tanh(cell)).astype(jnp.bfloat16)
        act_ref[rows, :width] = in_gate
        act_ref[rows, width : 2 * width] = forget
        act_ref[rows, 2 * width : 3 * width] = candidate
        act_ref[rows, 3 * width :] = out_gate
        cell_ref[after] = cell
        h_ref[rows] = hidden_new
        state[...] = hidden_new
        return carry

    lax.fori_loop(0, steps, step, 0)


def lstm_forward(x, weight, bias):
    rows, width = x.shape
    return pl.pallas_call(
        lstm_forward_kernel,
        out_shape=(
            jax.ShapeDtypeStruct((rows, 4 * width), jnp.float32),
            jax.ShapeDtypeStruct((rows + ROWS, width), jnp.float32),
            jax.ShapeDtypeStruct((rows, width), jnp.bfloat16),
        ),
        in_specs=[VMEM_SPEC] * 3,
        out_specs=(VMEM_SPEC,) * 3,
        scratch_shapes=[pltpu.VMEM((ROWS, width), jnp.bfloat16)],
        compiler_params=pltpu.CompilerParams(vmem_limit_bytes=VMEM_LIMIT),
    )(x, weight, bias)


def lstm_backward_kernel(act_ref, cell_ref, outer_ref, wt_ref, dpre_ref, state, held):
    width = outer_ref.shape[1]
    steps = outer_ref.shape[0] // ROWS
    state[...] = jnp.zeros_like(state)
    held[...] = jnp.zeros_like(held)

    def step(k, carry):
        t = steps - 1 - k
        rows = pl.ds(pl.multiple_of(t * ROWS, ROWS), ROWS)
        after = pl.ds(pl.multiple_of((t + 1) * ROWS, ROWS), ROWS)
        hidden_total = outer_ref[rows] + jnp.dot(
            state[...], wt_ref[...], preferred_element_type=jnp.float32
        )
        in_gate = act_ref[rows, :width]
        forget = act_ref[rows, width : 2 * width]
        candidate = act_ref[rows, 2 * width : 3 * width]
        out_gate = act_ref[rows, 3 * width :]
        squash = jnp.tanh(cell_ref[after])
        cell_total = held[...] + hidden_total * out_gate * (1.0 - squash * squash)
        held[...] = cell_total * forget
        grads = jnp.concatenate(
            [
                cell_total * candidate * in_gate * (1.0 - in_gate),
                cell_total * cell_ref[rows] * forget * (1.0 - forget),
                cell_total * in_gate * (1.0 - candidate * candidate),
                hidden_total * squash * out_gate * (1.0 - out_gate),
            ],
            -1,
        ).astype(jnp.bfloat16)
        state[...] = grads
        dpre_ref[rows] = grads
        return carry

    lax.fori_loop(0, steps, step, 0)


def lstm_backward(act, cell, outer, weight_t):
    rows, width = outer.shape
    return pl.pallas_call(
        lstm_backward_kernel,
        out_shape=jax.ShapeDtypeStruct((rows, 4 * width), jnp.bfloat16),
        in_specs=[VMEM_SPEC] * 4,
        out_specs=VMEM_SPEC,
        scratch_shapes=[
            pltpu.VMEM((ROWS, 4 * width), jnp.bfloat16),
            pltpu.VMEM((ROWS, width), jnp.float32),
        ],
        compiler_params=pltpu.CompilerParams(vmem_limit_bytes=VMEM_LIMIT),
    )(act, cell, outer, weight_t)


def attention_kernel(
    frames_ref,
    labels_ref,
    mask_ref,
    dec_ref,
    mem_ref,
    m0_ref,
    m1_ref,
    m2_ref,
    vec_ref,
    pull_ref,
    squash_ref,
    context_ref,
    dz_ref,
    dq_ref,
    dk_ref,
    ddec_ref,
    dmem_ref,
    dvec_ref,
    q_s,
    k_s,
    mem_s,
    ctx_s,
    dqa_s,
    dka_s,
    e_s,
    sel_s,
    prob_s,
    pow_s,
    w_s,
    a_s,
    own_s,
    nxt_s,
    g_s,
    d_s,
    bc_s,
):
    rows, width = dec_ref.shape
    utts = frames_ref.shape[0]
    length = rows // utts
    low = jnp.bfloat16
    f32 = jnp.float32
    lane = lax.broadcasted_iota(jnp.int32, (length, LANES), 1)
    lane_block = lax.broadcasted_iota(jnp.int32, (length, 8, LANES), 2)

    q_s[...] = jnp.dot(dec_ref[...], m0_ref[...], preferred_element_type=f32) + vec_ref[5:6]
    k_s[...] = jnp.dot(mem_ref[...], m1_ref[...], preferred_element_type=f32)
    mem_s[...] = mem_ref[...].astype(f32)
    e_s[...] = jnp.zeros_like(e_s)
    d_s[...] = jnp.zeros_like(d_s)

    tile = 256
    group = 4

    for u in range(utts):
        at = u * length

        def energy_step(block, sums, at=at):
            base = block * group
            for offset in range(group):
                j = base + offset
                row = k_s[pl.ds(at + j, 1), :]
                for head in range(2):
                    total = jnp.zeros((length, LANES), f32)
                    for c in range(width // LANES):
                        columns = slice(head * width + c * LANES, head * width + (c + 1) * LANES)
                        total = total + jnp.tanh(
                            q_s[at : at + length, columns] + row[:, columns]
                        ) * vec_ref[6:7, columns]
                    value = jnp.sum(total, -1, keepdims=True)
                    sums = tuple(
                        jnp.where(lane == j, value, s) if h == head else s
                        for h, s in enumerate(sums)
                    )
            return sums

        blocks = (frames_ref[u] + (group - 1)) // group
        zero = jnp.zeros((length, LANES), f32)
        mono, window = lax.fori_loop(0, blocks, energy_step, (zero, zero))
        e_s[0, :, u, :] = mono
        e_s[1, :, u, :] = window

    mask = mask_ref[...][None]
    mono = e_s[0] + ENERGY_OFFSET
    window = e_s[1]
    chosen = jax.nn.sigmoid(mono)
    inside = (lane_block < length).astype(f32)
    sel_s[...] = chosen * mask
    leave = (jnp.maximum(mono, 0.0) + jnp.log1p(jnp.exp(-jnp.abs(mono)))) * mask
    prob = jnp.exp(-leave) * inside
    prob_s[...] = prob

    def right(value, distance):
        return pltpu.roll(value, distance, value.ndim - 1)

    def left(value, distance):
        return pltpu.roll(value, LANES - distance, value.ndim - 1)

    power = jnp.where(lane_block >= 1, right(prob, 1), 0.0) * inside
    for n in range(5):
        pow_s[n] = power
        if n < 4:
            power = jnp.where(lane_block >= 2 ** (n + 1), power * right(power, 2**n), 0.0)

    lane_row = lax.broadcasted_iota(jnp.int32, (8, LANES), 1)

    def align_step(i, before):
        total = before
        for n in range(5):
            total = total + pow_s[n, i] * right(total, 2**n)
        w_s[i] = total
        now = sel_s[i] * total
        a_s[i] = now
        return now

    lax.fori_loop(0, length, align_step, jnp.where(lane_row == 0, 1.0, 0.0).astype(f32))

    aligned = a_s[...]
    own = jnp.where(lane_block == 0, 1.0, jax.nn.sigmoid(window - right(window, 1)))
    nxt = jax.nn.sigmoid(window - left(window, 1))
    own_s[...] = own
    nxt_s[...] = nxt
    beta = aligned * own + jnp.where(lane_block < length - 1, left(aligned, 1), 0.0) * nxt
    g_s[...] = beta

    for u in range(utts):
        at = u * length
        weights = g_s[:, u, :].astype(low)[:, :length]
        ctx_s[at : at + length] = jnp.dot(
            weights, mem_s[at : at + length].astype(low), preferred_element_type=f32
        )
    context_ref[...] = ctx_s[...].astype(low)

    squash = jnp.tanh(
        contract(dec_ref[...], m2_ref[:, :width], 1, 1)
        + contract(context_ref[...], m2_ref[:, width:], 1, 1)
        + vec_ref[7:8, :width]
    )
    squash_ref[...] = squash.astype(low)
    dz = (pull_ref[...] * (1.0 - squash * squash)).astype(low)
    dz_ref[...] = dz
    dvec_ref[...] = jnp.zeros_like(dvec_ref)
    dvec_ref[7:8, :width] = jnp.sum(dz.astype(f32), 0, keepdims=True)
    ddec_ref[...] = jnp.dot(dz, m2_ref[:, :width], preferred_element_type=f32)
    ctx_s[...] = (
        jnp.dot(dz, m2_ref[:, width:], preferred_element_type=f32).astype(low).astype(f32)
    )

    pad = jnp.zeros((length, LANES - length), f32)
    for u in range(utts):
        at = u * length
        weights = g_s[:, u, :].astype(low)[:, :length]
        pulled = ctx_s[at : at + length].astype(low)
        beta_grad = contract(pulled, mem_s[at : at + length].astype(low), 1, 1)
        e_s[0, :, u, :] = jnp.concatenate([beta_grad, pad], -1)
        mem_s[at : at + length] = contract(weights, pulled, 0, 0)

    beta_grad = e_s[0]
    own = own_s[...]
    nxt = nxt_s[...]
    g_s[...] = beta_grad * own + jnp.where(lane_block >= 1, right(beta_grad * nxt, 1), 0.0)
    aligned = a_s[...]
    from_own = jnp.where(lane_block >= 1, beta_grad * aligned * own * (1.0 - own), 0.0)
    from_next = (
        beta_grad
        * jnp.where(lane_block < length - 1, left(aligned, 1), 0.0)
        * nxt
        * (1.0 - nxt)
    )
    d_s[1] = (from_own - left(from_own, 1) + from_next - right(from_next, 1)) * inside

    prob = prob_s[...]
    power = jnp.where(lane_block < length - 1, prob, 0.0)
    for n in range(5):
        pow_s[n] = power
        if n < 4:
            power = power * left(power, 2**n)

    def retreat_step(k, after):
        i = length - 1 - k
        grad_align = g_s[i] + after
        e_s[0, i] = grad_align
        total = sel_s[i] * grad_align
        for n in range(5):
            total = total + pow_s[n, i] * left(total, 2**n)
        e_s[1, i] = total
        return total

    lax.fori_loop(0, length, retreat_step, jnp.zeros((8, LANES), f32))
    reached = w_s[...]
    grad_select = reached * e_s[0]
    grad_prob = reached * jnp.where(lane_block < length - 1, left(e_s[1], 1), 0.0)
    chosen = sel_s[...]
    d_s[0] = grad_select * chosen * (1.0 - chosen) - grad_prob * prob * chosen

    dka_s[...] = jnp.zeros_like(dka_s)

    def energy_back(u, dvec):
        at = pl.multiple_of(u * length, 8)
        for head in range(2):
            grads = d_s[head, :, pl.ds(u, 1), :].reshape(length, LANES)
            for j in range(length):
                bc_s[head, j] = jnp.broadcast_to(grads[:, j : j + 1], (length, LANES))
        count = (frames_ref[u] + 1) // 2
        for c in range(2 * width // tile):
            columns = slice(c * tile, (c + 1) * tile)
            head = c * tile // width
            q_now = q_s[pl.ds(at, length), columns]

            def back_step(block, sums, head=head, columns=columns, q_now=q_now):
                dq, dw = sums
                for offset in range(2):
                    j = block * 2 + offset
                    squash_all = jnp.tanh(q_now + k_s[pl.ds(at + j, 1), columns])
                    grad = bc_s[head, j]
                    grad = jnp.concatenate([grad] * (tile // LANES), -1)
                    scaled = grad * squash_all
                    dw = dw + scaled
                    moved = grad - scaled * squash_all
                    dq = dq + moved
                    dka_s[pl.ds(at + j, 1), columns] = jnp.sum(moved, 0, keepdims=True)
                return (dq, dw)

            zero = jnp.zeros((length, tile), f32)
            dq, dw = lax.fori_loop(0, count, back_step, (zero, zero))
            dq = dq * vec_ref[6:7, columns]
            dqa_s[pl.ds(at, length), columns] = dq
            dvec_ref[5:6, columns] += jnp.sum(dq, 0, keepdims=True)
            dvec_ref[6:7, columns] += jnp.sum(dw, 0, keepdims=True)
        return dvec

    lax.fori_loop(0, utts, energy_back, 0)
    dq_ref[...] = dqa_s[...].astype(low)
    dk_ref[...] = (dka_s[...] * vec_ref[6:7]).astype(low)
    ddec_ref[...] += contract(dq_ref[...], m0_ref[...], 1, 1)
    dmem_ref[...] = (mem_s[...] + contract(dk_ref[...], m1_ref[...], 1, 1)).astype(low)


def attention(frames, labels, decoded, memory, mats, vectors, pull):
    rows, width = decoded.shape
    utts = frames.shape[0]
    length = rows // utts
    lane = lax.broadcasted_iota(jnp.int32, (8, LANES), 1)
    padded = jnp.concatenate([frames, jnp.zeros((8 - utts,), frames.dtype)])
    mask = (lane < padded[:, None]).astype(jnp.float32)
    low, f32 = jnp.bfloat16, jnp.float32
    small = (length, 8, LANES)
    return pl.pallas_call(
        attention_kernel,
        out_shape=(
            jax.ShapeDtypeStruct((rows, width), low),
            jax.ShapeDtypeStruct((rows, width), low),
            jax.ShapeDtypeStruct((rows, width), low),
            jax.ShapeDtypeStruct((rows, 2 * width), low),
            jax.ShapeDtypeStruct((rows, 2 * width), low),
            jax.ShapeDtypeStruct((rows, width), f32),
            jax.ShapeDtypeStruct((rows, width), low),
            jax.ShapeDtypeStruct((8, 2 * width), f32),
        ),
        in_specs=[SMEM_SPEC] * 2 + [VMEM_SPEC] * 8,
        out_specs=(VMEM_SPEC,) * 8,
        scratch_shapes=[
            pltpu.VMEM((rows, 2 * width), f32),
            pltpu.VMEM((rows, 2 * width), f32),
            pltpu.VMEM((rows, width), f32),
            pltpu.VMEM((rows, width), f32),
            pltpu.VMEM((rows, 2 * width), f32),
            pltpu.VMEM((rows, 2 * width), f32),
            pltpu.VMEM((2,) + small, f32),
            pltpu.VMEM(small, f32),
            pltpu.VMEM(small, f32),
            pltpu.VMEM((5,) + small, f32),
            pltpu.VMEM(small, f32),
            pltpu.VMEM(small, f32),
            pltpu.VMEM(small, f32),
            pltpu.VMEM(small, f32),
            pltpu.VMEM(small, f32),
            pltpu.VMEM((2,) + small, f32),
            pltpu.VMEM((2, length, length, LANES), f32),
        ],
        compiler_params=pltpu.CompilerParams(vmem_limit_bytes=VMEM_LIMIT),
    )(frames, labels, mask, decoded, memory, mats[0], mats[1], mats[2], vectors, pull)


from jax.sharding import PartitionSpec as P

STEP = 5
NORM_EPS = 1e-05
BETA_ONE = 0.9
BETA_TWO = 0.999
ADAM_EPS = 1e-08
WEIGHT_DECAY = 0.01
RATE_LSTM = 0.05
RATE_MATRIX = 0.02
RATE_VECTOR = 0.3


def swapped(block):
    return lax.ppermute(block, "section", [(0, 1), (1, 0)])


def adamw(master, first, second, grad, rate):
    first_new = BETA_ONE * first + (1.0 - BETA_ONE) * grad
    second_new = BETA_TWO * second + (1.0 - BETA_TWO) * grad * grad
    first_hat = first_new / (1.0 - BETA_ONE**STEP)
    second_hat = second_new / (1.0 - BETA_TWO**STEP)
    master_new = master - rate * (
        first_hat / (jnp.sqrt(second_hat) + ADAM_EPS) + WEIGHT_DECAY * master
    )
    return (master_new, first_new, second_new)


def slot_major(block):
    batch_size, length, width = block.shape
    padded = jnp.pad(jnp.swapaxes(block, 0, 1), ((0, 0), (0, ROWS - batch_size), (0, 0)))
    return padded.reshape(length * ROWS, width)


def utt_major(block, batch_size):
    width = block.shape[-1]
    return jnp.swapaxes(block.reshape(-1, ROWS, width)[:, :batch_size], 0, 1)


def local(
    inputs,
    counts,
    cotangent,
    lstm_master,
    lstm_copy,
    lstm_first,
    lstm_second,
    mats_master,
    mats_copy,
    mats_first,
    mats_second,
    out_master,
    out_copy,
    out_first,
    out_second,
    vec_master,
    vec_first,
    vec_second,
):
    low, f32 = jnp.bfloat16, jnp.float32
    section_index = lax.axis_index("section")
    on_encoder = section_index == 0
    lstm_full, out_half = (
        lax.all_gather(lstm_copy, "dp", axis=1, tiled=True),
        lax.all_gather(out_copy, "dp", axis=0, tiled=True),
    )
    mats_full, vectors_low = (
        lax.all_gather(mats_copy, ("section", "dp"), axis=2, tiled=True),
        lax.all_gather(vec_master.astype(low), ("section", "dp"), axis=1, tiled=True),
    )
    out_full = lax.all_gather(out_half, "section", axis=1, tiled=True)
    vectors = vectors_low.astype(f32)
    weight = lstm_full[0]
    model_width = weight.shape[0] // 2
    vocab_half = out_half.shape[1]
    sequence = inputs[0]
    batch_size, length, _ = sequence.shape
    half = batch_size // 2

    def traded(block):
        kept = jnp.where(on_encoder, block[:half], block[half:])
        other = swapped(jnp.where(on_encoder, block[half:], block[:half]))
        return jnp.where(on_encoder, kept, other), jnp.where(on_encoder, other, kept)

    def returned(from_encoder, from_decoder):
        kept = jnp.where(on_encoder, from_encoder, from_decoder)
        other = swapped(jnp.where(on_encoder, from_decoder, from_encoder))
        return jnp.where(
            on_encoder,
            jnp.concatenate([kept, other], 0),
            jnp.concatenate([other, kept], 0),
        )

    frames, labels = traded(counts[0])
    label_mask = (
        lax.broadcasted_iota(jnp.int32, (half, length), 1) < labels[:, None]
    ).astype(f32)
    grad_low, grad_high = traded(cotangent)
    grad_logits = jnp.concatenate([grad_low, grad_high], -1) * label_mask[:, :, None].astype(low)
    grad_logits = grad_logits.reshape(half * length, -1)
    pull = contract(grad_logits, out_full, 1, 1)

    raw_values = sequence.astype(f32)
    norm_gain = vectors[4, :model_width]
    center = raw_values - jnp.mean(raw_values, -1, keepdims=True)
    spread = lax.rsqrt(jnp.mean(center * center, -1, keepdims=True) + NORM_EPS)
    scaled = center * spread
    normed = jnp.where(
        on_encoder, scaled * norm_gain + vectors[4, model_width:], raw_values
    ).astype(low)
    bias_here = lax.dynamic_slice_in_dim(vectors, 2 * section_index, 2, 0).reshape(1, -1)
    x_rows = slot_major(normed)
    act, cell, h_rows = lstm_forward(x_rows, weight, bias_here)
    states = utt_major(h_rows, batch_size)
    result = jnp.where(on_encoder, raw_values + states.astype(f32), states.astype(f32)).astype(low)
    memory, decoded = traded(result)
    decoded = decoded.reshape(-1, model_width)
    memory = memory.reshape(-1, model_width)
    squashed, context, dz, dq, dk, ddec, dmem, vec_rows = attention(
        frames, labels, decoded, memory, mats_full, vectors, pull
    )
    vocab = 2 * vocab_half
    logits = (
        jnp.dot(squashed, out_full, preferred_element_type=f32)
        + vectors[7, model_width : model_width + vocab]
    ).astype(low)
    logits = logits.reshape(half, length, vocab)
    logits = returned(logits[..., :vocab_half], logits[..., vocab_half:])
    out_grad = contract(squashed, grad_logits, 0, 0)
    out_bias_grad = jnp.sum(grad_logits, 0, dtype=f32)
    mats_grad = jnp.stack(
        [
            contract(decoded, dq, 0, 0),
            contract(memory, dk, 0, 0),
            jnp.concatenate([contract(dz, decoded, 0, 0), contract(dz, context, 0, 0)], 1),
        ]
    )
    outer = returned(dmem, ddec.astype(low)).reshape(batch_size, length, model_width)
    outer = outer.astype(f32)
    weight_t = jnp.swapaxes(weight[model_width:], 0, 1)
    dpre = lstm_backward(act, cell, slot_major(outer), weight_t)
    h_before = jnp.concatenate([jnp.zeros_like(h_rows[:ROWS]), h_rows[:-ROWS]], 0)
    weight_grad = jnp.concatenate([contract(x_rows, dpre, 0, 0), contract(h_before, dpre, 0, 0)], 0)
    bias_grad = jnp.sum(dpre, 0, dtype=f32)
    input_grad = utt_major(contract(dpre, weight[:model_width], 1, 1), batch_size)
    gain_grad = jnp.sum(input_grad * scaled, (0, 1))
    shift_grad_norm = jnp.sum(input_grad, (0, 1))
    scaled_grad = input_grad * norm_gain
    norm_back = spread * (
        scaled_grad
        - jnp.mean(scaled_grad, -1, keepdims=True)
        - scaled * jnp.mean(scaled_grad * scaled, -1, keepdims=True)
    )
    inputs_grad = jnp.where(on_encoder, norm_back + outer, input_grad)
    lstm_rows = lax.dynamic_update_slice(
        jnp.zeros((4, 2 * model_width), f32), bias_grad.reshape(2, -1), (2 * section_index, 0)
    )
    norm_row = jnp.where(on_encoder, jnp.concatenate([gain_grad, shift_grad_norm]), 0.0)
    logit_row = jnp.pad(out_bias_grad, (model_width, model_width - vocab))
    vector_grad = jnp.concatenate(
        [lstm_rows, norm_row[None], vec_rows[5:7], (vec_rows[7] + logit_row)[None]], 0
    )
    out_grad = out_grad.reshape(model_width, 2, vocab_half)
    lstm_sum = lax.psum_scatter(
        weight_grad.astype(low)[None], "dp", scatter_dimension=1, tiled=True
    ).astype(f32)
    out_sum = lax.psum_scatter(
        jnp.swapaxes(out_grad, 0, 1).astype(low), "section", scatter_dimension=0, tiled=True
    )[0]
    out_sum = lax.psum_scatter(out_sum, "dp", scatter_dimension=0, tiled=True).astype(f32)
    mats_sum = lax.psum_scatter(
        mats_grad.astype(low), ("section", "dp"), scatter_dimension=2, tiled=True
    ).astype(f32)
    vector_sum = lax.psum_scatter(vector_grad, ("section", "dp"), scatter_dimension=1, tiled=True)
    lstm_new, lstm_first_new, lstm_second_new = adamw(
        lstm_master, lstm_first, lstm_second, lstm_sum, RATE_LSTM
    )
    mats_new, mats_first_new, mats_second_new = adamw(
        mats_master, mats_first, mats_second, mats_sum, RATE_MATRIX
    )
    out_new, out_first_new, out_second_new = adamw(
        out_master, out_first, out_second, out_sum, RATE_MATRIX
    )
    vec_new, vec_first_new, vec_second_new = adamw(
        vec_master, vec_first, vec_second, vector_sum, RATE_VECTOR
    )
    return (
        logits,
        inputs_grad[None],
        lstm_new,
        lstm_first_new,
        lstm_second_new,
        lstm_new.astype(low),
        mats_new,
        mats_first_new,
        mats_second_new,
        mats_new.astype(low),
        out_new,
        out_first_new,
        out_second_new,
        out_new.astype(low),
        vec_new,
        vec_first_new,
        vec_second_new,
    )


def solution(mesh):
    lstm = P("section", "dp", None)
    mats = P(None, None, ("section", "dp"))
    out = P("dp", "section")
    vec = P(None, ("section", "dp"))
    logits = P("dp", None, "section")
    rows = P("section", "dp", None, None)
    return jax.shard_map(
        local,
        mesh=mesh,
        in_specs=(rows, P("section", "dp"), logits) + (lstm,) * 4 + (mats,) * 4 + (out,) * 4 + (vec,) * 3,
        out_specs=(logits, rows) + (lstm,) * 4 + (mats,) * 4 + (out,) * 4 + (vec,) * 3,
        check_vma=False,
    )
```

time: 2960 us -> 1450 us (0.49)
  waiting for transfers between devices: 2250 us -> 987 us
  matrix products: 299 us -> 32.2 us
  Pallas kernels: 0 us -> 136 us
  other arithmetic: 87.3 us -> 40.9 us
    reduce_scatter x3, waiting for transfers between devices: 1290 us -> 420 us  [the longest x1 344 us: local(): lax.psum_scatter(weight_grad.astype(low)[None], 'dp', scatter_dimension=1...]
    ppermute x6 -> x5, waiting for transfers between devices: 777 us -> 1.02 us  [swapped(): return lax.ppermute(block, 'section', [(0, 1), (1, 0)])]
    unnamed x7 -> x10, waiting for transfers between devices: 108 us -> 351 us
    dot_general x26 -> x1, matrix products: 139 us -> 0.8 us  [local(): jnp.dot(squashed, out_full, preferred_element_type=f32)]
    pallas_call x0 -> x3, Pallas kernels: none -> 136 us  [the longest x1 57 us: attention(): pl.pallas_call(attention_kernel, out_shape=(jax.ShapeDtypeStruct((rows, w...]
    dot_general x29 -> x9, matrix products: 160 us -> 31.4 us  [contract(): lax.dot_general(left, right, (((left_dim,), (right_dim,)), ((), ())), pre...]
    all_gather x1, waiting for transfers between devices: 74.8 us -> 183 us  [local(): lax.all_gather(lstm_copy, 'dp', axis=1, tiled=True)]
    dynamic_slice x25 -> x0, local copies, waits for them, and re-layouts: 37.9 us -> none  [the longest x24 37.9 us: recur_forward(): lax.scan(recur_advance, initial, jnp.swapaxes(inflow, 0, 1))]
  transfers between devices with their start and end apart: 12 -> 13, of which waited for: 7 -> 7; matrix products, arithmetic and copies ran while one was open for 16% -> 12% of each run, Pallas kernels for 0% -> 6%
where the time goes in v1:
time: 1450 us; the launch traced here: 1440 us
  waiting for transfers between devices  987 us (68%)
  Pallas kernels  136 us (9%)
  blocking collectives  114 us (8%)
  local copies, waits for them, and re-layouts  109 us (8%)
  other arithmetic  40.9 us (3%)
  matrix products  32.2 us (2%)
  between operations  15 us (1%)
    unnamed x10, waiting for transfers between devices  351 us
    reduce_scatter x1, waiting for transfers between devices, local(): lax.psum_scatter(weight_grad.astype(low)[None], 'dp', scatter_dimension=1...  344 us
    all_gather x1, waiting for transfers between devices, local(): lax.all_gather(lstm_copy, 'dp', axis=1, tiled=True)  183 us
    reduce_scatter x1, waiting for transfers between devices, local(): lax.psum_scatter(out_sum, 'dp', scatter_dimension=0, tiled=True).astype(f32)  76 us
    all_gather x1, blocking collectives, local(): lax.all_gather(vec_master.astype(low), ('section', 'dp'), axis=1, tiled=T...  64.9 us
    pallas_call x1, Pallas kernels, attention(): pl.pallas_call(attention_kernel, out_shape=(jax.ShapeDtypeStruct((rows, w...  57 us
    all_gather x1, blocking collectives, local(): lax.all_gather(out_copy, 'dp', axis=0, tiled=True)  49.1 us
    pallas_call x1, Pallas kernels, lstm_forward(): pl.pallas_call(lstm_forward_kernel, out_shape=(jax.ShapeDtypeStruct((rows...  41.8 us
  transfers between devices with their start and end apart: 13, of which 7 were waited for; matrix products, arithmetic and copies ran while one was open for 12% of the time, Pallas kernels for 6%

profile of v1, /device:TPU:0, one launch (start us, length us, event | category | flops | bytes accessed | tf_op | source)
XLA Modules:
  0.0 1436.6 jit_solution(6494628142949733948)
XLA Ops:
  7.2 49.1 %all_gather.18 = bf16[1024,500]{1,0:T(8,128)(2,1)S(1)} all-gather(bf16[64,500]{1,0:T(8,128)(2,1)} %param.30), channel_id=1, replica_groups=mesh['section'=2,'dp'=16] {'dp'}, dimensions={0}, use_global_device_ids=true | all-gather | bytes 1088000 | tf_op jit(solution)/shard_map/all_gather | solution.py:478
  57.8 2.4 copy.165
  61.7 64.9 %all-gather = bf16[32,64,8]{1,2,0:T(8,128)(2,1)S(1)} all-gather(bf16[1,64,8]{1,2,0:T(8,128)(2,1)S(1)} %convert_bitcast_fusion.6), channel_id=1, replica_groups=mesh['section'=2,'dp'=16] {'section','dp'}, dimensions={0}, use_global_device_ids=true | all-gather | bytes 33792 | tf_op jit(solution)/shard_map/all_gather | solution.py:482
  132.0 2.0 reshape.200
  135.4 183.3 %all-gather.6.cloned.1.call-done = bf16[1,2048,4096]{1,2,0:T(8,128)(2,1)} async-done(((bf16[1,128,4096]{1,2,0:T(8,128)(2,1)}), bf16[1,2048,4096]{1,2,0:T(8,128)(2,1)}) %all-gather.6.cloned.1.call-update) | async-done | bytes 16777232 | tf_op jit(solution)/shard_map/all_gather | solution.py:477
  318.7 21.4 %copy.166.w_ref = bf16[2048,4096]{1,0:T(8,128)(2,1)} copy(bf16[2048,4096]{0,1:T(8,128)(2,1)} %bitcast.154) | data formatting | bytes 33554432 | tf_op jit(solution)/shard_map/squeeze | solution.py:486
  340.2 41.8 %shard_map.305 = (f32[384,4096]{1,0:T(8,128)}, f32[400,1024]{1,0:T(8,128)}, bf16[384,1024]{1,0:T(8,128)(2,1)}) custom-call(bf16[384,1024]{1,0:T(8,128)(2,1)} %bitcast.165, bf16[2048,4096]{1,0:T(8,128)(2,1)} %copy.166.w_ref, f32[1,4096]{1,0:T(1,128)} %bitcast.184), custom_call_target="tpu_custom_call" | custom-call | tf_op jit(solution)/shard_map/pallas_call | solution.py:65
  384.4 31.7 %all-gather.8.cloned.1.call-done = bf16[3,1024,2048]{1,2,0:T(8,128)(2,1)} async-done(((bf16[3,1024,64]{1,2,0:T(8,128)(2,1)}), bf16[3,1024,2048]{1,2,0:T(8,128)(2,1)}) %all-gather.8.cloned.1.call-update) | async-done | bytes 12582928 | tf_op jit(solution)/shard_map/all_gather | solution.py:481
  416.1 9.0 fusion.49
  425.1 6.5 copy.191
  431.6 6.5 copy.192
  438.1 6.5 copy.193
  447.6 57.0 %shard_map.306 = (bf16[144,1024]{1,0:T(8,128)(2,1)}, bf16[144,1024]{1,0:T(8,128)(2,1)}, bf16[144,1024]{1,0:T(8,128)(2,1)}, bf16[144,2048]{1,0:T(8,128)(2,1)}, bf...) custom-call(s32[6]{0:T(128)} %copy-done.30, s32[6]{0:T(128)} %copy-done.27, ...), custom_call_target="tpu_custom_call" | custom-call | tf_op jit(solution)/shard_map/pallas_call | solution.py:377
  504.6 3.2 convert_bitcast_fusion.4
  510.2 7.9 slice_bitcast_fusion.2.wt_ref
  521.6 37.4 %shard_map.307 = bf16[384,4096]{1,0:T(8,128)(2,1)} custom-call(f32[384,4096]{1,0:T(8,128)} %get-tuple-element.30.act_ref, f32[400,1024]{1,0:T(8,128)} %get-tuple-element.31.cell_ref, f32[384,1024]{1,0:T(8,128)} %bitcast.159, bf16[4096,1024]{1,0:T(8,128)(2,1)} %slice_bitcast_fusion.2.wt_ref), custom_call_target="tpu_custom_call" | custom-call | tf_op jit(solution)/shard_map/pallas_call | solution.py:117
  559.0 9.9 fusion.18
  570.5 2.5 convert_reduce_fusion
  574.5 2.3 copy.187
  576.9 2.4 convert_bitcast_fusion.2
  582.8 5.4 pad_maximum_fusion.1
  588.2 27.5 %copy.178 = bf16[3,1024,2048]{1,0,2:T(4,128)(2,1)} copy(bf16[3,1024,2048]{2,1,0:T(8,128)(2,1)} %pad_maximum_fusion.1) | data formatting | bytes 25165824 | tf_op jit(solution)/shard_map/stack | solution.py:544
  617.2 6.9 convert_bitcast_fusion
  624.1 4.8 convert_bitcast_fusion.1
  628.9 7.6 pad_maximum_fusion
  642.5 1.7 copy.182
  644.2 71.5 %reduce-scatter.15.cloned.1.call-done = f32[64,8]{1,0:T(8,128)} async-done(((f32[2048,8]{1,0:T(8,128)}), f32[64,8]{1,0:T(8,128)}) %reduce-scatter.15.cloned.1.call-update) | async-done | bytes 2064
  717.2 76.0 %reduce-scatter.13.cloned.1.call-done = bf16[64,500]{1,0:T(8,128)(2,1)} async-done(((bf16[1024,500]{1,0:T(8,128)(2,1)}), bf16[64,500]{1,0:T(8,128)(2,1)}) %reduce-scatter.13.cloned.1.call-update) | async-done | bytes 64016 | tf_op jit(solution)/shard_map/reduce_scatter | solution.py:583
  794.8 278.8 %all-reduce.8.cloned.1.call-done = bf16[3,1024,2048]{1,0,2:T(4,128)(2,1)} async-done(((bf16[3,1024,2048]{1,0,2:T(4,128)(2,1)}), bf16[3,1024,2048]{1,0,2:T(4,128)(2,1)}) %all-reduce.8.cloned.1.call-update) | async-done | bytes 12582928
  1074.8 3.2 fusion.43
  1078.0 344.2 %reduce-scatter.9.cloned.1.call-done = bf16[1,128,4096]{2,1,0:T(8,128)(2,1)} async-done(((bf16[1,2048,4096]{2,1,0:T(8,128)(2,1)}), bf16[1,128,4096]{2,1,0:T(8,128)(2,1)}) %reduce-scatter.9.cloned.1.call-update) | async-done | bytes 1048592 | tf_op jit(solution)/shard_map/reduce_scatter | solution.py:577
  1422.2 7.3 fusion.46
  (152 shorter events, 39.0 us)
Async XLA Ops:
  7.2 124.8 %all-gather.10.cloned.1.call-start = ((), (), s32[]{:S(2)}) async-start(), calls=%async_computation.8 | async-start | bytes 3096576 | tf_op jit(solution)/shard_map/all_gather | solution.py:484
  57.7 3.4 copy-start.10
  57.7 4.0 copy-start.22
  57.7 69.6 %copy-start = (bf16[1,12,24,1024]{3,2,1,0:T(8,128)(2,1)S(1)}, bf16[1,12,24,1024]{3,2,1,0:T(8,128)(2,1)}, u32[]{:S(2)}) copy-start(bf16[1,12,24,1024]{3,2,1,0:T(8,128)(2,1)} %param.18) | copy-start | bytes 1769476
  57.7 261.0 %all-gather.6.cloned.1.call-start = ((), (), s32[]{:S(2)}) async-start(), calls=%async_computation.4 | async-start | bytes 17825792 | tf_op jit(solution)/shard_map/all_gather | solution.py:477
  60.2 355.9 %all-gather.8.cloned.1.call-start = ((), (), s32[]{:S(2)}) async-start(), calls=%async_computation.5 | async-start | bytes 12976128 | tf_op jit(solution)/shard_map/all_gather | solution.py:481
  60.9 513.6 %reduce-scatter.11.cloned.1.call-start = ((), (), s32[]{:S(2)}) async-start(), calls=%async_computation.7 | async-start | bytes 3096576 | tf_op jit(solution)/shard_map/reduce_scatter | solution.py:580
  61.0 68.8 %collective-permute-start = (s32[6]{0:T(128)S(1)}, s32[6]{0:T(128)S(1)}, u32[]{:S(2)}, u32[]{:S(2)}) collective-permute-start(s32[6]{0:T(128)S(1)} %fusion.35), channel_id=1, source_target_pairs={{0,16},{16,0},{1,17},{17,1},{2,18},{18,2},{3,19},{19,3},{4,20},{20... | collective-permute-start | bytes 80 | tf_op jit(solution)/shard_map/ppermute | solution.py:428
  61.1 69.7 %collective-permute-start.2 = (bf16[6,24,500]{2,1,0:T(8,128)(2,1)S(1)}, bf16[6,24,500]{2,1,0:T(8,128)(2,1)S(1)}, u32[]{:S(2)}, u32[]{:S(2)}) collective-permute-start(bf16[6,24,500]{2,1,0:T(8,128)(2,1)S(1)} %broadcast_select_fusion.10), channel_id=1, source_target_pairs={{0,16},{16,0},{1,17},{17,1},{2,18},{18,2},{3,19},{19,3},{4,20},{20... | collective-permute-start | bytes 432008 | tf_op jit(solution)/shard_map/ppermute | solution.py:428
  130.0 4.0 copy-start.27
  130.0 4.1 copy-start.30
  130.1 3.9 copy-start.26
  384.4 60.3 %collective-permute-start.1 = (bf16[6,24,1024]{2,0,1:T(8,128)(2,1)}, bf16[6,24,1024]{2,0,1:T(8,128)(2,1)}, u32[]{:S(2)}, u32[]{:S(2)}) collective-permute-start(bf16[6,24,1024]{2,0,1:T(8,128)(2,1)} %broadcast_select_fusion.3), channel_id=1, source_target_pairs={{0,16},{16,0},{1,17},{17,1},{2,18},{18,2},{3,19},{19,3},{4,20},{20... | collective-permute-start | bytes 884744 | tf_op jit(solution)/shard_map/ppermute | solution.py:428
  447.6 57.0 %copy-start.11 = (bf16[2,500,144]{1,0,2:T(2,128)(2,1)S(1)}, bf16[2,500,144]{1,0,2:T(2,128)(2,1)}, u32[]{:S(2)}) copy-start(bf16[2,500,144]{1,0,2:T(2,128)(2,1)} %dot_general.47) | copy-start | bytes 864004
  504.6 3.7 copy-start.6
  504.6 3.7 copy-start.8
  504.6 4.5 copy-start.16
  507.8 207.9 %reduce-scatter.15.cloned.1.call-start = ((), (), s32[]{:S(2)}) async-start(), calls=%async_computation.10 | async-start | bytes 1081344
  510.1 9.7 collective-permute-start.4
  574.4 218.7 %reduce-scatter.13.cloned.1.call-start = ((), (), s32[]{:S(2)}) async-start(), calls=%async_computation.9 | async-start | bytes 1114112 | tf_op jit(solution)/shard_map/reduce_scatter | solution.py:583
  576.8 496.8 %all-reduce.8.cloned.1.call-start = ((), (), s32[]{:S(2)}) async-start(), calls=%async_computation.11 | async-start | bytes 33554432
  615.8 806.4 %reduce-scatter.9.cloned.1.call-start = ((), (), s32[]{:S(2)}) async-start(), calls=%async_computation.6 | async-start | bytes 17825792 | tf_op jit(solution)/shard_map/reduce_scatter | solution.py:577
  617.2 6.9 copy-start.1
  617.2 6.9 copy-start.3
  638.4 1.6 collective-permute-start.3
  642.4 74.1 %copy-start.28 = (f32[8,64]{1,0:T(8,128)S(1)}, f32[8,64]{1,0:T(8,128)}, u32[]{:S(2)}) copy-start(f32[8,64]{1,0:T(8,128)} %param.34) | copy-start | bytes 6148
  642.4 74.1 %copy-start.29 = (f32[8,64]{1,0:T(8,128)S(1)}, f32[8,64]{1,0:T(8,128)}, u32[]{:S(2)}) copy-start(f32[8,64]{1,0:T(8,128)} %param.35) | copy-start | bytes 6148
  642.4 150.7 %copy-start.19 = (f32[64,500]{1,0:T(8,128)S(1)}, f32[64,500]{1,0:T(8,128)}, u32[]{:S(2)}) copy-start(f32[64,500]{1,0:T(8,128)} %param.29) | copy-start | bytes 384004
  642.4 150.7 %copy-start.20 = (f32[64,500]{1,0:T(8,128)S(1)}, f32[64,500]{1,0:T(8,128)}, u32[]{:S(2)}) copy-start(f32[64,500]{1,0:T(8,128)} %param.31) | copy-start | bytes 384004
  642.4 150.7 %copy-start.21 = (f32[64,500]{1,0:T(8,128)S(1)}, f32[64,500]{1,0:T(8,128)}, u32[]{:S(2)}) copy-start(f32[64,500]{1,0:T(8,128)} %param.32) | copy-start | bytes 384004
  642.5 432.3 %copy-start.14 = (f32[3,1024,64]{1,2,0:T(8,128)S(1)}, f32[3,1024,64]{1,2,0:T(8,128)}, u32[]{:S(2)}) copy-start(f32[3,1024,64]{1,2,0:T(8,128)} %param.25) | copy-start | bytes 2359300
  642.5 432.3 %copy-start.15 = (f32[3,1024,64]{1,2,0:T(8,128)S(1)}, f32[3,1024,64]{1,2,0:T(8,128)}, u32[]{:S(2)}) copy-start(f32[3,1024,64]{1,2,0:T(8,128)} %param.27) | copy-start | bytes 2359300
  (13 other events, 31.7 us)
Sparse Core Ops, SparseCore 0:
  57.8 6.3 all-gather.9
  67.5 251.1 all-gather.5
  321.7 94.3 all-gather.7
  507.9 12.2 reduce-scatter.10
  574.5 141.1 reduce-scatter.14
  718.5 74.5 reduce-scatter.12
  799.2 274.3 all-reduce.7
  1075.9 346.2 reduce-scatter.8

commit v2 on v1

v2 whole, which is shorter than its diff:
```python
import functools
import jax
import jax.numpy as jnp
from jax import lax
from jax.experimental import pallas as pl
from jax.experimental.pallas import tpu as pltpu
from jax.sharding import PartitionSpec as P

ROWS = 16
LANES = 128
ENERGY_OFFSET = -4.0
VMEM_SPEC = pl.BlockSpec(memory_space=pltpu.VMEM)
SMEM_SPEC = pl.BlockSpec(memory_space=pltpu.SMEM)
VMEM_LIMIT = 60 * 1024 * 1024


def contract(left, right, left_dim, right_dim):
    return lax.dot_general(
        left, right, (((left_dim,), (right_dim,)), ((), ())), preferred_element_type=jnp.float32
    )


def attention_kernel(
    frames_ref,
    mask_ref,
    dec_ref,
    mem_ref,
    mats_ref,
    vec_ref,
    out_ref,
    bias_ref,
    gl_ref,
    squash_ref,
    context_ref,
    dz_ref,
    dq_ref,
    dk_ref,
    ddec_ref,
    dmem_ref,
    dvec_ref,
    logits_ref,
    gsum_ref,
    q_s,
    k_s,
    mem_s,
    ctx_s,
    dqa_s,
    dka_s,
    e_s,
    sel_s,
    prob_s,
    pow_s,
    w_s,
    a_s,
    own_s,
    nxt_s,
    g_s,
    d_s,
    bc_s,
):
    rows, width = dec_ref.shape
    utts = frames_ref.shape[0]
    length = rows // utts
    low = jnp.bfloat16
    f32 = jnp.float32
    lane = lax.broadcasted_iota(jnp.int32, (length, LANES), 1)
    lane_block = lax.broadcasted_iota(jnp.int32, (length, 8, LANES), 2)

    q_s[...] = contract(dec_ref[...], mats_ref[0], 1, 1) + vec_ref[5:6]
    k_s[...] = contract(mem_ref[...], mats_ref[1], 1, 1)
    mem_s[...] = mem_ref[...].astype(f32)
    e_s[...] = jnp.zeros_like(e_s)
    d_s[...] = jnp.zeros_like(d_s)

    tile = 256
    group = 4

    for u in range(utts):
        at = u * length

        def energy_step(block, sums, at=at):
            base = block * group
            for offset in range(group):
                j = base + offset
                row = k_s[pl.ds(at + j, 1), :]
                for head in range(2):
                    total = jnp.zeros((length, LANES), f32)
                    for c in range(width // LANES):
                        columns = slice(head * width + c * LANES, head * width + (c + 1) * LANES)
                        total = total + jnp.tanh(
                            q_s[at : at + length, columns] + row[:, columns]
                        ) * vec_ref[6:7, columns]
                    value = jnp.sum(total, -1, keepdims=True)
                    sums = tuple(
                        jnp.where(lane == j, value, s) if h == head else s
                        for h, s in enumerate(sums)
                    )
            return sums

        blocks = (frames_ref[u] + (group - 1)) // group
        zero = jnp.zeros((length, LANES), f32)
        mono, window = lax.fori_loop(0, blocks, energy_step, (zero, zero))
        e_s[0, :, u, :] = mono
        e_s[1, :, u, :] = window

    mask = mask_ref[...][None]
    mono = e_s[0] + ENERGY_OFFSET
    window = e_s[1]
    chosen = jax.nn.sigmoid(mono)
    inside = (lane_block < length).astype(f32)
    sel_s[...] = chosen * mask
    leave = (jnp.maximum(mono, 0.0) + jnp.log1p(jnp.exp(-jnp.abs(mono)))) * mask
    prob = jnp.exp(-leave) * inside
    prob_s[...] = prob

    def right(value, distance):
        return pltpu.roll(value, distance, value.ndim - 1)

    def left(value, distance):
        return pltpu.roll(value, LANES - distance, value.ndim - 1)

    power = jnp.where(lane_block >= 1, right(prob, 1), 0.0) * inside
    for n in range(5):
        pow_s[n] = power
        if n < 4:
            power = jnp.where(lane_block >= 2 ** (n + 1), power * right(power, 2**n), 0.0)

    lane_row = lax.broadcasted_iota(jnp.int32, (8, LANES), 1)

    def align_step(i, before):
        total = before
        for n in range(5):
            total = total + pow_s[n, i] * right(total, 2**n)
        w_s[i] = total
        now = sel_s[i] * total
        a_s[i] = now
        return now

    lax.fori_loop(0, length, align_step, jnp.where(lane_row == 0, 1.0, 0.0).astype(f32))

    aligned = a_s[...]
    own = jnp.where(lane_block == 0, 1.0, jax.nn.sigmoid(window - right(window, 1)))
    nxt = jax.nn.sigmoid(window - left(window, 1))
    own_s[...] = own
    nxt_s[...] = nxt
    beta = aligned * own + jnp.where(lane_block < length - 1, left(aligned, 1), 0.0) * nxt
    g_s[...] = beta

    for u in range(utts):
        at = u * length
        weights = g_s[:, u, :].astype(low)[:, :length]
        ctx_s[at : at + length] = jnp.dot(
            weights, mem_s[at : at + length].astype(low), preferred_element_type=f32
        )
    context_ref[...] = ctx_s[...].astype(low)

    squash = jnp.tanh(
        jnp.dot(dec_ref[...], mats_ref[2, :width], preferred_element_type=f32)
        + jnp.dot(context_ref[...], mats_ref[2, width:], preferred_element_type=f32)
        + vec_ref[7:8, :width]
    )
    squash_ref[...] = squash.astype(low)
    pull = contract(gl_ref[0], out_ref[0], 1, 1) + contract(gl_ref[1], out_ref[1], 1, 1)
    dz = (pull * (1.0 - squash * squash)).astype(low)
    dz_ref[...] = dz
    dvec_ref[...] = jnp.zeros_like(dvec_ref)
    dvec_ref[7:8, :width] = jnp.sum(dz.astype(f32), 0, keepdims=True)
    for h in range(2):
        logits_ref[h] = (
            jnp.dot(squash_ref[...], out_ref[h], preferred_element_type=f32) + bias_ref[h : h + 1]
        ).astype(low)
        gsum_ref[h : h + 1] = jnp.sum(gl_ref[h].astype(f32), 0, keepdims=True)
    ddec_ref[...] = contract(dz, mats_ref[2, :width], 1, 1)
    ctx_s[...] = contract(dz, mats_ref[2, width:], 1, 1).astype(low).astype(f32)

    pad = jnp.zeros((length, LANES - length), f32)
    for u in range(utts):
        at = u * length
        weights = g_s[:, u, :].astype(low)[:, :length]
        pulled = ctx_s[at : at + length].astype(low)
        beta_grad = contract(pulled, mem_s[at : at + length].astype(low), 1, 1)
        e_s[0, :, u, :] = jnp.concatenate([beta_grad, pad], -1)
        mem_s[at : at + length] = contract(weights, pulled, 0, 0)

    beta_grad = e_s[0]
    own = own_s[...]
    nxt = nxt_s[...]
    g_s[...] = beta_grad * own + jnp.where(lane_block >= 1, right(beta_grad * nxt, 1), 0.0)
    aligned = a_s[...]
    from_own = jnp.where(lane_block >= 1, beta_grad * aligned * own * (1.0 - own), 0.0)
    from_next = (
        beta_grad
        * jnp.where(lane_block < length - 1, left(aligned, 1), 0.0)
        * nxt
        * (1.0 - nxt)
    )
    d_s[1] = (from_own - left(from_own, 1) + from_next - right(from_next, 1)) * inside

    prob = prob_s[...]
    power = jnp.where(lane_block < length - 1, prob, 0.0)
    for n in range(5):
        pow_s[n] = power
        if n < 4:
            power = power * left(power, 2**n)

    def retreat_step(k, after):
        i = length - 1 - k
        grad_align = g_s[i] + after
        e_s[0, i] = grad_align
        total = sel_s[i] * grad_align
        for n in range(5):
            total = total + pow_s[n, i] * left(total, 2**n)
        e_s[1, i] = total
        return total

    lax.fori_loop(0, length, retreat_step, jnp.zeros((8, LANES), f32))
    reached = w_s[...]
    grad_select = reached * e_s[0]
    grad_prob = reached * jnp.where(lane_block < length - 1, left(e_s[1], 1), 0.0)
    chosen = sel_s[...]
    d_s[0] = grad_select * chosen * (1.0 - chosen) - grad_prob * prob * chosen

    dka_s[...] = jnp.zeros_like(dka_s)

    def energy_back(u, dvec):
        at = pl.multiple_of(u * length, 8)
        for head in range(2):
            grads = d_s[head, :, pl.ds(u, 1), :].reshape(length, LANES)
            for j in range(length):
                bc_s[head, j] = jnp.broadcast_to(grads[:, j : j + 1], (length, LANES))
        count = (frames_ref[u] + 1) // 2
        for c in range(2 * width // tile):
            columns = slice(c * tile, (c + 1) * tile)
            head = c * tile // width
            q_now = q_s[pl.ds(at, length), columns]

            def back_step(block, sums, head=head, columns=columns, q_now=q_now):
                dq, dw = sums
                for offset in range(2):
                    j = block * 2 + offset
                    squash_all = jnp.tanh(q_now + k_s[pl.ds(at + j, 1), columns])
                    grad = bc_s[head, j]
                    grad = jnp.concatenate([grad] * (tile // LANES), -1)
                    scaled = grad * squash_all
                    dw = dw + scaled
                    moved = grad - scaled * squash_all
                    dq = dq + moved
                    dka_s[pl.ds(at + j, 1), columns] = jnp.sum(moved, 0, keepdims=True)
                return (dq, dw)

            zero = jnp.zeros((length, tile), f32)
            dq, dw = lax.fori_loop(0, count, back_step, (zero, zero))
            dq = dq * vec_ref[6:7, columns]
            dqa_s[pl.ds(at, length), columns] = dq
            dvec_ref[5:6, columns] += jnp.sum(dq, 0, keepdims=True)
            dvec_ref[6:7, columns] += jnp.sum(dw, 0, keepdims=True)
        return dvec

    lax.fori_loop(0, utts, energy_back, 0)
    for h in range(2):
        columns = slice(h * width, (h + 1) * width)
        dq_ref[h] = dqa_s[:, columns].astype(low)
        dk_ref[h] = (dka_s[:, columns] * vec_ref[6:7, columns]).astype(low)
        ddec_ref[...] += jnp.dot(dq_ref[h], mats_ref[0, columns], preferred_element_type=f32)
        mem_s[...] += jnp.dot(dk_ref[h], mats_ref[1, columns], preferred_element_type=f32)
    dmem_ref[...] = mem_s[...].astype(low)


def attention(frames, decoded, memory, mats, vectors, outs, bias, gl):
    rows, width = decoded.shape
    utts = frames.shape[0]
    length = rows // utts
    lane = lax.broadcasted_iota(jnp.int32, (8, LANES), 1)
    padded = jnp.concatenate([frames, jnp.zeros((8 - utts,), frames.dtype)])
    mask = (lane < padded[:, None]).astype(jnp.float32)
    low, f32 = jnp.bfloat16, jnp.float32
    small = (length, 8, LANES)
    half_vocab = gl.shape[-1]
    return pl.pallas_call(
        attention_kernel,
        out_shape=(
            jax.ShapeDtypeStruct((rows, width), low),
            jax.ShapeDtypeStruct((rows, width), low),
            jax.ShapeDtypeStruct((rows, width), low),
            jax.ShapeDtypeStruct((2, rows, width), low),
            jax.ShapeDtypeStruct((2, rows, width), low),
            jax.ShapeDtypeStruct((rows, width), f32),
            jax.ShapeDtypeStruct((rows, width), low),
            jax.ShapeDtypeStruct((8, 2 * width), f32),
            jax.ShapeDtypeStruct((2, rows, half_vocab), low),
            jax.ShapeDtypeStruct((2, half_vocab), f32),
        ),
        in_specs=[SMEM_SPEC] + [VMEM_SPEC] * 8,
        out_specs=(VMEM_SPEC,) * 10,
        scratch_shapes=[
            pltpu.VMEM((rows, 2 * width), f32),
            pltpu.VMEM((rows, 2 * width), f32),
            pltpu.VMEM((rows, width), f32),
            pltpu.VMEM((rows, width), f32),
            pltpu.VMEM((rows, 2 * width), f32),
            pltpu.VMEM((rows, 2 * width), f32),
            pltpu.VMEM((2,) + small, f32),
            pltpu.VMEM(small, f32),
            pltpu.VMEM(small, f32),
            pltpu.VMEM((5,) + small, f32),
            pltpu.VMEM(small, f32),
            pltpu.VMEM(small, f32),
            pltpu.VMEM(small, f32),
            pltpu.VMEM(small, f32),
            pltpu.VMEM(small, f32),
            pltpu.VMEM((2,) + small, f32),
            pltpu.VMEM((2, length, length, LANES), f32),
        ],
        compiler_params=pltpu.CompilerParams(vmem_limit_bytes=VMEM_LIMIT),
    )(frames, mask, decoded, memory, mats, vectors, outs, bias, gl)


MESH_ID = pl.DeviceIdType.MESH
ANY_SPEC = pl.BlockSpec(memory_space=pl.ANY)
DP_LAYOUTS = {16: (4, 2, 1, 2), 128: (8, 4, 1, 32)}
LINE_STRIDE = 4


def flipped(value, k):
    result = value
    bit = 1
    while bit <= k:
        if k & bit:
            result = result + bit - 2 * bit * lax.rem(value // bit, 2)
        bit *= 2
    return result


class Place:
    def __init__(self, n_dp):
        self.line, self.side, stride_a, stride_b = DP_LAYOUTS[n_dp]
        self.core = lax.axis_index("section")
        self.chip = lax.axis_index("dp")
        self.z = lax.rem(self.chip // LINE_STRIDE, self.line)
        at_a = lax.rem(self.chip // stride_a, self.side)
        at_b = lax.rem(self.chip // stride_b, self.side)
        self.role = lax.rem(self.z, 2)
        moves_a = [(flipped(at_a, k) - at_a) * stride_a for k in range(self.side)]
        moves_b = [(flipped(at_b, k) - at_b) * stride_b for k in range(self.side)]
        core = self.core
        self.first = [a + (b - a) * core for a, b in zip(moves_a, moves_b)]
        self.second = [b + (a - b) * core for a, b in zip(moves_a, moves_b)]
        self.along = [(flipped(self.z, k) - self.z) * LINE_STRIDE for k in range(self.line)]

    def block(self, kz, kf=0, kg=0):
        return self.chip + self.along[kz] + self.first[kf] + self.second[kg]

    def other_block(self, kz, kf=0, kg=0):
        return self.chip + self.along[kz] + self.second[kf] + self.first[kg]

    def greet(self):
        barrier = pltpu.get_barrier_semaphore()
        peers = [(1 - self.core, self.chip)]
        for k in range(1, self.line):
            peers += [(0, self.chip + self.along[k]), (1, self.chip + self.along[k])]
        for k in range(1, self.side):
            peers += [(self.core, self.chip + self.first[k]), (self.core, self.chip + self.second[k])]
        for peer in peers:
            pl.semaphore_signal(barrier, inc=1, device_id=peer, device_id_type=MESH_ID)
        pl.semaphore_wait(barrier, len(peers))


def remote(source, target, send, receive, device):
    return pltpu.make_async_remote_copy(
        src_ref=source,
        dst_ref=target,
        send_sem=send,
        recv_sem=receive,
        device_id=device,
        device_id_type=MESH_ID,
    )


class Spread:
    def __init__(self, place, here, there, sems):
        self.place, self.here, self.there, self.sems = place, here, there, sems
        self.sent = []

    def send(self, target, device, send, receive):
        copy = remote(target, target, send, receive, device)
        copy.start()
        self.sent.append(copy)

    def arrived(self, target, semaphore):
        place = self.place
        remote(target, target, semaphore, semaphore, (1 - place.core, place.chip)).wait_recv()

    def to_second(self, kz, kf):
        place = self.place
        target = self.here(place.block(kz, kf))
        for kg in range(1, place.side):
            self.send(
                target,
                (place.core, place.chip + place.second[kg]),
                self.sems["gs"].at[kg, kf, kz],
                self.sems["gr"].at[kg, kf, kz],
            )

    def to_core(self, kz, kf, kg):
        place = self.place
        self.send(
            self.here(place.block(kz, kf, kg)),
            (1 - place.core, place.chip),
            self.sems["cs"].at[kg, kf, kz],
            self.sems["cr"].at[kg, kf, kz],
        )

    def stage_one(self, wait_line):
        place = self.place
        for kz in range(place.line):
            wait_line(kz)
            target = self.here(place.block(kz))
            for kf in range(1, place.side):
                self.send(
                    target,
                    (place.core, place.chip + place.first[kf]),
                    self.sems["fs"].at[kf, kz],
                    self.sems["fr"].at[kf, kz],
                )
            self.to_second(kz, 0)
            self.to_core(kz, 0, 0)

    def stage_two(self):
        place = self.place
        for kf in range(1, place.side):
            for kz in range(place.line):
                self.arrived(self.here(place.block(kz, kf)), self.sems["fr"].at[kf, kz])
                self.to_second(kz, kf)
                self.to_core(kz, kf, 0)

    def stage_three(self):
        place = self.place
        for kg in range(1, place.side):
            for kf in range(place.side):
                for kz in range(place.line):
                    self.arrived(self.here(place.block(kz, kf, kg)), self.sems["gr"].at[kg, kf, kz])
                    self.to_core(kz, kf, kg)

    def finish(self):
        place = self.place
        for kg in range(place.side):
            for kf in range(place.side):
                for kz in range(place.line):
                    self.arrived(self.there(place.other_block(kz, kf, kg)), self.sems["cr"].at[kg, kf, kz])

    def sent_all(self):
        for copy in self.sent:
            copy.wait_send()


def spread_sems(line, side):
    dma = pltpu.SemaphoreType.DMA
    return {
        "zs": dma((line, 2)),
        "zr": dma((line,)),
        "fs": dma((side, line)),
        "fr": dma((side, line)),
        "gs": dma((side, side, line)),
        "gr": dma((side, side, line)),
        "cs": dma((side, side, line)),
        "cr": dma((side, side, line)),
    }


def spread_even(place, source, at, sems):
    own = at(place.core, place.chip)
    spread = Spread(place, lambda block: at(place.core, block), lambda block: at(1 - place.core, block), sems)
    kept = pltpu.make_async_copy(source, own, sems["zr"].at[0])
    copies = [
        remote(source, own, sems["zs"].at[k, 0], sems["zr"].at[k], (place.core, place.chip + place.along[k]))
        for k in range(1, place.line)
    ]

    def begin():
        kept.start()
        for copy in copies:
            copy.start()
        spread.sent += copies

    def wait_line(kz):
        if kz == 0:
            kept.wait()
        else:
            spread.arrived(spread.here(place.block(kz)), sems["zr"].at[kz])

    spread.begin = begin
    spread.first_stage = lambda: spread.stage_one(wait_line)
    return spread


def spread_role(place, source, target, sems, rows, half):
    def columns(core):
        return pl.ds(pl.multiple_of(core * half, half), half)

    def at(block, core):
        return target.at[pl.ds(pl.multiple_of(block * rows, rows), rows), columns(core)]

    spread = Spread(
        place, lambda block: at(block, place.core), lambda block: at(block, 1 - place.core), sems
    )
    mine = place.role == place.core
    kept = pltpu.make_async_copy(source.at[:, columns(place.core)], at(place.chip, place.core), sems["zr"].at[0])
    cross = remote(
        source.at[:, columns(1 - place.core)],
        at(place.chip, 1 - place.core),
        sems["zs"].at[0, 0],
        sems["zr"].at[0],
        (1 - place.core, place.chip),
    )
    copies = [
        [
            remote(
                source.at[:, columns(core)],
                at(place.chip, core),
                sems["zs"].at[k, core],
                sems["zr"].at[k],
                (core, place.chip + place.along[k]),
            )
            for core in range(2)
        ]
        for k in range(1, place.line)
    ]

    def each(action):
        @pl.when(mine)
        def _():
            action(cross)
            for k in range(2, place.line, 2):
                for copy in copies[k - 1]:
                    action(copy)

        @pl.when(jnp.logical_not(mine))
        def _():
            for k in range(1, place.line, 2):
                for copy in copies[k - 1]:
                    action(copy)

    def begin():
        @pl.when(mine)
        def _():
            kept.start()

        each(lambda copy: copy.start())

    def wait_line(kz):
        if kz == 0:

            @pl.when(mine)
            def _():
                kept.wait()

            @pl.when(jnp.logical_not(mine))
            def _():
                spread.arrived(spread.here(place.chip), sems["zr"].at[0])

        else:
            spread.arrived(spread.here(place.block(kz)), sems["zr"].at[kz])

    def sent_line():
        each(lambda copy: copy.wait_send())

    spread.begin = begin
    spread.first_stage = lambda: spread.stage_one(wait_line)
    spread.sent_line = sent_line
    return spread


def forward_kernel(
    n_dp,
    base_ref,
    shard_ref,
    mats_ref,
    out_ref,
    vec_ref,
    act_ref,
    cell_ref,
    h_ref,
    x_ref,
    vectors_ref,
    w_out,
    mats_out,
    out_out,
    w_s,
    vec_s,
    state,
    keep_sem,
    sems_w,
    sems_m,
    sems_o,
    sems_v,
):
    width = base_ref.shape[1]
    steps = base_ref.shape[0] // ROWS
    place = Place(n_dp)
    place.greet()
    matrix = spread_role(place, shard_ref, w_s, sems_w, shard_ref.shape[0], 2 * width)
    mats = spread_even(place, mats_ref, lambda core, chip: mats_out.at[:, core, chip], sems_m)
    outs = spread_even(place, out_ref, lambda core, chip: out_out.at[core, chip], sems_o)
    vecs = spread_even(place, vec_ref, lambda core, chip: vec_s.at[core, chip], sems_v)
    state[...] = jnp.zeros_like(state)
    cell_ref[:ROWS] = jnp.zeros((ROWS, width), jnp.float32)
    vecs.begin()
    matrix.begin()
    matrix.first_stage()
    vecs.first_stage()
    matrix.stage_two()
    vecs.stage_two()
    matrix.stage_three()
    outs.begin()
    mats.begin()
    vecs.stage_three()
    vecs.finish()
    piece = 2 * width // (2 * n_dp)
    per_tile = LANES // piece
    for m in range(2 * width // LANES):
        tile = jnp.zeros((8, LANES), jnp.float32)
        for k in range(per_tile):
            index = m * per_tile + k
            block = vec_s[index // n_dp, index % n_dp]
            tile = tile + (pltpu.roll(block, k * piece, 1) if k else block)
        vectors_ref[:, m * LANES : (m + 1) * LANES] = tile
    encoder = place.role == 0
    gain = jnp.where(encoder, vectors_ref[4:5, :width], 1.0)
    shift = jnp.where(encoder, vectors_ref[4:5, width:], 0.0)
    x_ref[...] = (base_ref[...] * gain + shift).astype(jnp.bfloat16)
    matrix.finish()
    keep = pltpu.make_async_copy(w_s, w_out, keep_sem)
    keep.start()
    for q in range(4):
        columns = slice(q * width, (q + 1) * width)
        row = q // 2
        bias_columns = slice((q % 2) * width, (q % 2 + 1) * width)
        bias = jnp.where(
            encoder, vectors_ref[row : row + 1, bias_columns], vectors_ref[row + 2 : row + 3, bias_columns]
        )
        act_ref[:, columns] = (
            jnp.dot(x_ref[...], w_s[:width, columns], preferred_element_type=jnp.float32) + bias
        )

    def step(t, carry):
        rows = pl.ds(pl.multiple_of(t * ROWS, ROWS), ROWS)
        after = pl.ds(pl.multiple_of((t + 1) * ROWS, ROWS), ROWS)
        hidden = state[...]

        def gate(q):
            columns = slice(q * width, (q + 1) * width)
            return act_ref[rows, columns] + jnp.dot(
                hidden, w_s[width:, columns], preferred_element_type=jnp.float32
            )

        in_gate = jax.nn.sigmoid(gate(0))
        forget = jax.nn.sigmoid(gate(1))
        candidate = jnp.tanh(gate(2))
        cell = forget * cell_ref[rows] + in_gate * candidate
        out_gate = jax.nn.sigmoid(gate(3))
        hidden_new = (out_gate * jnp.tanh(cell)).astype(jnp.bfloat16)
        act_ref[rows, :width] = in_gate
        act_ref[rows, width : 2 * width] = forget
        act_ref[rows, 2 * width : 3 * width] = candidate
        act_ref[rows, 3 * width :] = out_gate
        cell_ref[after] = cell
        h_ref[rows] = hidden_new
        state[...] = hidden_new
        return carry

    first, second = steps * 3 // 8, steps * 3 // 4
    outs.first_stage()
    mats.first_stage()
    lax.fori_loop(0, first, step, 0)
    outs.stage_two()
    mats.stage_two()
    lax.fori_loop(first, second, step, 0)
    outs.stage_three()
    lax.fori_loop(second, steps, step, 0)
    mats.stage_three()
    outs.finish()
    mats.finish()
    keep.wait()
    matrix.sent_line()
    for spread in (matrix, vecs, outs, mats):
        spread.sent_all()


def forward(n_dp, base, shard, mats_block, out_block, vec_block):
    rows, width = base.shape
    low, f32 = jnp.bfloat16, jnp.float32
    line, side = DP_LAYOUTS[n_dp][:2]
    return pl.pallas_call(
        functools.partial(forward_kernel, n_dp),
        out_shape=(
            jax.ShapeDtypeStruct((rows, 4 * width), f32),
            jax.ShapeDtypeStruct((rows + ROWS, width), f32),
            jax.ShapeDtypeStruct((rows, width), low),
            jax.ShapeDtypeStruct((rows, width), low),
            jax.ShapeDtypeStruct((8, 2 * width), f32),
            jax.ShapeDtypeStruct((2 * width, 4 * width), low),
            jax.ShapeDtypeStruct((3, 2, n_dp) + mats_block.shape[1:], low),
            jax.ShapeDtypeStruct((2, n_dp) + out_block.shape, low),
        ),
        in_specs=[VMEM_SPEC, ANY_SPEC, ANY_SPEC, ANY_SPEC, VMEM_SPEC],
        out_specs=(VMEM_SPEC,) * 5 + (ANY_SPEC,) * 3,
        scratch_shapes=[
            pltpu.VMEM((2 * width, 4 * width), low),
            pltpu.VMEM((2, n_dp, 8, LANES), f32),
            pltpu.VMEM((ROWS, width), low),
            pltpu.SemaphoreType.DMA,
        ]
        + [spread_sems(line, side)] * 4,
        compiler_params=pltpu.CompilerParams(
            collective_id=1, has_side_effects=True, vmem_limit_bytes=VMEM_LIMIT
        ),
    )(base, shard, mats_block, out_block, vec_block)


class Fold:
    def __init__(self, place, part, stage, near, far, sems):
        self.place, self.part, self.stage, self.near, self.far, self.sems = place, part, stage, near, far, sems
        self.sent = []

    def send(self, source, target, device, send, receive):
        copy = remote(source, target, send, receive, device)
        copy.start()
        self.sent.append(copy)

    def arrived(self, target, semaphore):
        place = self.place
        remote(target, target, semaphore, semaphore, (1 - place.core, place.chip)).wait_recv()

    def stage_a(self):
        place = self.place
        for kg in range(1, place.side):
            for kf in reversed(range(place.side)):
                for kz in range(place.line):
                    source = self.stage.at[kg - 1, kf, kz]
                    source[...] = self.part(kz, kf, kg).astype(source.dtype)
                    self.send(
                        source,
                        self.near.at[kg - 1, kf, kz],
                        (place.core, place.chip + place.second[kg]),
                        self.sems["gs"].at[kg, kf, kz],
                        self.sems["gr"].at[kg, kf, kz],
                    )

    def stage_b(self):
        place = self.place
        for kf in reversed(range(place.side)):
            for kz in range(place.line):
                total = self.part(kz, kf, 0)
                for kg in range(1, place.side):
                    self.arrived(self.near.at[kg - 1, kf, kz], self.sems["gr"].at[kg, kf, kz])
                    total = total + self.near[kg - 1, kf, kz].astype(jnp.float32)
                source = self.near.at[0, kf, kz]
                source[...] = total.astype(source.dtype)
                if kf:
                    self.send(
                        source,
                        self.far.at[kf - 1, kz],
                        (place.core, place.chip + place.first[kf]),
                        self.sems["fs"].at[kf, kz],
                        self.sems["fr"].at[kf, kz],
                    )

    def summed(self, kz):
        place = self.place
        total = self.near[0, 0, kz].astype(jnp.float32)
        for kf in range(1, place.side):
            self.arrived(self.far.at[kf - 1, kz], self.sems["fr"].at[kf, kz])
            total = total + self.far[kf - 1, kz].astype(jnp.float32)
        source = self.far.at[0, kz]
        source[...] = total.astype(source.dtype)
        return source

    def sent_all(self):
        for copy in self.sent:
            copy.wait_send()


class FoldEven(Fold):
    def __init__(self, place, part, stage, near, far, end, sems):
        super().__init__(place, part, stage, near, far, sems)
        self.end = end

    def stage_c(self):
        place = self.place
        for kz in reversed(range(place.line)):
            source = self.summed(kz)
            if kz:
                self.send(
                    source,
                    self.end.at[kz - 1],
                    (place.core, place.chip + place.along[kz]),
                    self.sems["zs"].at[kz, 0],
                    self.sems["zr"].at[kz],
                )

    def result(self):
        place = self.place
        total = self.far[0, 0].astype(jnp.float32)
        for kz in range(1, place.line):
            self.arrived(self.end.at[kz - 1], self.sems["zr"].at[kz])
            total = total + self.end[kz - 1].astype(jnp.float32)
        return total


class FoldRole(Fold):
    def __init__(self, place, part, stage, near, far, end, sems):
        super().__init__(place, part, stage, near, far, sems)
        self.end = end

    def stage_c(self):
        place = self.place
        self.line_copies = []
        for kz in reversed(range(place.line)):
            source = self.summed(kz)
            if kz:
                copy = remote(
                    source,
                    self.end.at[place.core, kz],
                    self.sems["zs"].at[kz, 0],
                    self.sems["er"].at[place.core, kz],
                    (place.role, place.chip + place.along[kz]),
                )
                copy.start()
                self.sent.append(copy)
            else:
                self.last = source
                self.cross = remote(
                    source,
                    self.end.at[place.core, 0],
                    self.sems["zs"].at[0, 0],
                    self.sems["er"].at[place.core, 0],
                    (1 - place.core, place.chip),
                )

                @pl.when(place.core != place.role)
                def _():
                    self.cross.start()

    def result(self, sum_ref):
        place = self.place
        rows, half = self.end.shape[2:]
        mine = place.core == place.role

        def columns(core):
            return pl.ds(pl.multiple_of(core * half, half), half)

        def add(parity):
            sources = [kz for kz in range(place.line) if kz % 2 == parity]
            for core in range(2):
                total = jnp.zeros((rows, half), jnp.float32)
                for kz in sources:
                    if kz:
                        self.arrived(self.end.at[core, kz], self.sems["er"].at[core, kz])
                        total = total + self.end[core, kz].astype(jnp.float32)
                sum_ref[:, core * half : (core + 1) * half] = total

        @pl.when(mine)
        def _():
            add(0)
            own, other = columns(place.core), columns(1 - place.core)
            sum_ref[:, own] += self.last[...].astype(jnp.float32)
            self.arrived(self.end.at[1 - place.core, 0], self.sems["er"].at[1 - place.core, 0])
            sum_ref[:, other] += self.end[1 - place.core, 0].astype(jnp.float32)

        @pl.when(jnp.logical_not(mine))
        def _():
            add(1)
            self.cross.wait_send()


def fold_sems(line, side):
    dma = pltpu.SemaphoreType.DMA
    return {
        "gs": dma((side, side, line)),
        "gr": dma((side, side, line)),
        "fs": dma((side, line)),
        "fr": dma((side, line)),
        "zs": dma((line, 1)),
        "zr": dma((line,)),
        "er": dma((2, line)),
    }


def fold_buffers(line, side, shape, dtype):
    return [
        pltpu.VMEM((side - 1, side, line) + shape, dtype),
        pltpu.VMEM((side - 1, side, line) + shape, dtype),
        pltpu.VMEM((side - 1, line) + shape, dtype),
    ]


def backward_kernel(
    n_dp,
    act_ref,
    cell_ref,
    outer_ref,
    wt_ref,
    ht_ref,
    dq_ref,
    dk_ref,
    dec_ref,
    mem_ref,
    ctx_ref,
    dz_ref,
    sq_ref,
    gl_ref,
    dpre_ref,
    dpre_other,
    ht_other,
    mats_sum,
    out_sum,
    state,
    held,
    facts,
    facts_gl,
    g_mats,
    g_out,
    m_stage,
    m_near,
    m_far,
    m_end,
    o_stage,
    o_near,
    o_far,
    o_end,
    fact_sems,
    pre_sems,
    ht_sems,
    sems_m,
    sems_o,
):
    width = outer_ref.shape[1]
    steps = outer_ref.shape[0] // ROWS
    low, f32 = jnp.bfloat16, jnp.float32
    place = Place(n_dp)
    place.greet()
    core = place.core
    other = (1 - core, place.chip)
    sources = [dq_ref.at[1 - core], dk_ref.at[1 - core], dec_ref, mem_ref, ctx_ref, dz_ref, sq_ref]
    handed = [
        remote(source, facts.at[n], fact_sems.at[0, n], fact_sems.at[1, n], other)
        for n, source in enumerate(sources)
    ]
    handed.append(remote(gl_ref.at[1 - core], facts_gl, fact_sems.at[0, 7], fact_sems.at[1, 7], other))
    handed.append(remote(ht_ref, ht_other, ht_sems.at[0], ht_sems.at[1], other))
    for copy in handed:
        copy.start()
    state[...] = jnp.zeros_like(state)
    held[...] = jnp.zeros_like(held)

    def step(k, carry):
        t = steps - 1 - k
        rows = pl.ds(pl.multiple_of(t * ROWS, ROWS), ROWS)
        after = pl.ds(pl.multiple_of((t + 1) * ROWS, ROWS), ROWS)
        hidden_total = outer_ref[rows] + jnp.dot(
            state[...], wt_ref[...], preferred_element_type=f32
        )
        in_gate = act_ref[rows, :width]
        forget = act_ref[rows, width : 2 * width]
        candidate = act_ref[rows, 2 * width : 3 * width]
        out_gate = act_ref[rows, 3 * width :]
        squash = jnp.tanh(cell_ref[after])
        cell_total = held[...] + hidden_total * out_gate * (1.0 - squash * squash)
        held[...] = cell_total * forget
        grads = jnp.concatenate(
            [
                cell_total * candidate * in_gate * (1.0 - in_gate),
                cell_total * cell_ref[rows] * forget * (1.0 - forget),
                cell_total * in_gate * (1.0 - candidate * candidate),
                hidden_total * squash * out_gate * (1.0 - out_gate),
            ],
            -1,
        ).astype(low)
        state[...] = grads
        dpre_ref[rows] = grads
        return carry

    shares = 4
    share = steps // shares

    def hand_over(n):
        top = (steps - (n + 1) * share) * ROWS
        rows = slice(top, top + share * ROWS)
        columns = pl.ds(pl.multiple_of((1 - core) * 2 * width, 2 * width), 2 * width)
        copy = remote(
            dpre_ref.at[rows, columns], dpre_other.at[rows, :], pre_sems.at[0, n], pre_sems.at[1, n], other
        )
        copy.start()
        handed.append(copy)

    part_rows = g_mats.shape[1] // 3
    out_rows = g_out.shape[1]

    def matrices():
        for copy in handed[:8]:
            copy.wait_recv()
        joined = jnp.where(core == 0, dec_ref[...], ctx_ref[...])
        joined_other = jnp.where(core == 0, facts[2], facts[4])
        pairs = [
            (dq_ref[core], dec_ref[...], facts[0], facts[2]),
            (dk_ref[core], mem_ref[...], facts[1], facts[3]),
            (joined, dz_ref[...], joined_other, facts[5]),
        ]
        for m, (a, b, c, d) in enumerate(pairs):
            total = (contract(a, b, 0, 0) + contract(c, d, 0, 0)).astype(low)
            for block in range(n_dp):
                g_mats[block, m * part_rows : (m + 1) * part_rows] = total[
                    block * part_rows : (block + 1) * part_rows
                ]
        total = (contract(sq_ref[...], gl_ref[core], 0, 0) + contract(facts[6], facts_gl[...], 0, 0)).astype(low)
        for block in range(n_dp):
            g_out[block] = total[block * out_rows : (block + 1) * out_rows]

    mats = FoldEven(
        place, lambda kz, kf, kg: g_mats[place.block(kz, kf, kg)].astype(f32), m_stage, m_near, m_far, m_end, sems_m
    )
    outs = FoldEven(
        place, lambda kz, kf, kg: g_out[place.block(kz, kf, kg)].astype(f32), o_stage, o_near, o_far, o_end, sems_o
    )
    lax.fori_loop(0, share, step, 0)
    hand_over(0)
    matrices()
    mats.stage_a()
    outs.stage_a()
    lax.fori_loop(share, 2 * share, step, 0)
    hand_over(1)
    lax.fori_loop(2 * share, 3 * share, step, 0)
    hand_over(2)
    mats.stage_b()
    outs.stage_b()
    lax.fori_loop(3 * share, steps, step, 0)
    hand_over(3)
    mats.stage_c()
    outs.stage_c()
    mats_sum[...] = mats.result()
    out_sum[...] = outs.result()
    for copy in handed[8:]:
        copy.wait_recv()
    for copy in handed:
        copy.wait_send()
    mats.sent_all()
    outs.sent_all()


def backward(n_dp, act, cell, outer, weight_t, ht, facts):
    rows, width = outer.shape
    low, f32 = jnp.bfloat16, jnp.float32
    line, side = DP_LAYOUTS[n_dp][:2]
    utt_rows = facts[2].shape[0]
    half_vocab = facts[-1].shape[-1]
    mats_block = (3 * width // n_dp, width)
    out_block = (width // n_dp, half_vocab)
    dma = pltpu.SemaphoreType.DMA
    return pl.pallas_call(
        functools.partial(backward_kernel, n_dp),
        out_shape=(
            jax.ShapeDtypeStruct((rows, 4 * width), low),
            jax.ShapeDtypeStruct((rows, 2 * width), low),
            jax.ShapeDtypeStruct(ht.shape, low),
            jax.ShapeDtypeStruct(mats_block, f32),
            jax.ShapeDtypeStruct(out_block, f32),
        ),
        in_specs=[VMEM_SPEC] * 4 + [ANY_SPEC] + [VMEM_SPEC] * 8,
        out_specs=(VMEM_SPEC, VMEM_SPEC, ANY_SPEC, VMEM_SPEC, VMEM_SPEC),
        scratch_shapes=[
            pltpu.VMEM((ROWS, 4 * width), low),
            pltpu.VMEM((ROWS, width), f32),
            pltpu.VMEM((7, utt_rows, width), low),
            pltpu.VMEM((utt_rows, half_vocab), low),
            pltpu.VMEM((n_dp,) + mats_block, low),
            pltpu.VMEM((n_dp,) + out_block, low),
        ]
        + fold_buffers(line, side, mats_block, low)
        + [pltpu.VMEM((line - 1,) + mats_block, low)]
        + fold_buffers(line, side, out_block, low)
        + [pltpu.VMEM((line - 1,) + out_block, low)]
        + [dma((2, 8)), dma((2, 4)), dma((2,))]
        + [fold_sems(line, side)] * 2,
        compiler_params=pltpu.CompilerParams(
            collective_id=2, has_side_effects=True, vmem_limit_bytes=VMEM_LIMIT
        ),
    )(act, cell, outer, weight_t, ht, *facts)


def update_kernel(
    n_dp,
    batch,
    ht_ref,
    ht_other,
    dpre_ref,
    dpre_other,
    w_ref,
    base_ref,
    spread_ref,
    outer_ref,
    vectors_ref,
    dvec_ref,
    sum_ref,
    gin_ref,
    vec_sum,
    w_s,
    gin_s,
    gin_u,
    vec_s,
    vec_other,
    vec_parts,
    l_stage,
    l_near,
    l_far,
    l_end,
    v_stage,
    v_near,
    v_far,
    v_end,
    w_sem,
    gin_sems,
    vec_sems,
    sems_l,
    sems_v,
):
    width = base_ref.shape[1]
    steps = base_ref.shape[0] // ROWS
    low, f32 = jnp.bfloat16, jnp.float32
    place = Place(n_dp)
    load = pltpu.make_async_copy(w_ref.at[:width], w_s, w_sem)
    load.start()
    place.greet()
    core = place.core
    encoder = place.role == 0
    mine = core == place.role
    block_rows = sum_ref.shape[0]
    half = pl.ds(pl.multiple_of(core * 2 * width, 2 * width), 2 * width)

    def part(kz, kf, kg):
        rows = pl.ds(pl.multiple_of(place.block(kz, kf, kg) * block_rows, block_rows), block_rows)
        return jnp.dot(ht_ref[rows], dpre_ref[:, half], preferred_element_type=f32) + jnp.dot(
            ht_other[rows], dpre_other[...], preferred_element_type=f32
        )

    matrix = FoldRole(place, part, l_stage, l_near, l_far, l_end, sems_l)
    matrix.stage_a()

    load.wait()
    gin_s[...] = contract(dpre_ref[...], w_s[...], 1, 1)
    input_grad = gin_s[...]
    scaled = base_ref[...]
    vec_s[...] = dvec_ref[...]
    vec_s[4:5, :width] = jnp.where(encoder, jnp.sum(input_grad * scaled, 0, keepdims=True), 0.0)
    vec_s[4:5, width:] = jnp.where(encoder, jnp.sum(input_grad, 0, keepdims=True), 0.0)
    for q in range(4):
        columns = slice((q % 2) * width, (q % 2 + 1) * width)
        bias = jnp.sum(dpre_ref[:, q * width : (q + 1) * width].astype(f32), 0, keepdims=True)
        for role in range(2):
            row = 2 * role + q // 2
            vec_s[row : row + 1, columns] = jnp.where(place.role == role, bias, 0.0)

    @pl.when(encoder)
    def _():
        grads = gin_s[...] * vectors_ref[4:5, :width]
        values = base_ref[...]
        gin_s[...] = (
            spread_ref[...]
            * (
                grads
                - jnp.mean(grads, -1, keepdims=True)
                - values * jnp.mean(grads * values, -1, keepdims=True)
            )
            + outer_ref[...]
        )

    turned = gin_s[...].reshape(steps, ROWS, width)
    for u in range(batch):
        gin_u[u] = turned[:, u, :]
    kept = pltpu.make_async_copy(gin_u, gin_ref, gin_sems.at[0])
    handed = remote(gin_u, gin_ref, gin_sems.at[1], gin_sems.at[2], (1 - core, place.chip + place.along[1]))

    @pl.when(mine)
    def _():
        kept.start()

    @pl.when(jnp.logical_not(mine))
    def _():
        handed.start()

    own_half = pl.ds(pl.multiple_of(core * width, width), width)
    other_half = pl.ds(pl.multiple_of((1 - core) * width, width), width)
    trade = remote(
        vec_s.at[:, other_half], vec_other, vec_sems.at[0], vec_sems.at[1], (1 - core, place.chip)
    )
    trade.start()
    trade.wait_recv()
    total = vec_s[:, own_half] + vec_other[...]
    piece = width // n_dp
    per_tile = LANES // piece
    for block in range(n_dp):
        tile = total[:, (block // per_tile) * LANES : (block // per_tile + 1) * LANES]
        turn = (block % per_tile) * piece
        vec_parts[block] = pltpu.roll(tile, LANES - turn, 1) if turn else tile
    vecs = FoldEven(
        place, lambda kz, kf, kg: vec_parts[place.block(kz, kf, kg)], v_stage, v_near, v_far, v_end, sems_v
    )
    vecs.stage_a()
    matrix.stage_b()
    vecs.stage_b()
    matrix.stage_c()
    vecs.stage_c()
    matrix.result(sum_ref)
    vec_sum[...] = vecs.result()

    @pl.when(mine)
    def _():
        kept.wait()

    @pl.when(jnp.logical_not(mine))
    def _():
        handed.wait()

    trade.wait_send()
    matrix.sent_all()
    vecs.sent_all()


def update(n_dp, batch, ht, ht_other, dpre, dpre_other, weight, base, spread, outer, vectors, dvec):
    rows, width = base.shape
    steps = rows // ROWS
    low, f32 = jnp.bfloat16, jnp.float32
    line, side = DP_LAYOUTS[n_dp][:2]
    block_rows = 2 * width // n_dp
    block = (block_rows, 2 * width)
    dma = pltpu.SemaphoreType.DMA
    return pl.pallas_call(
        functools.partial(update_kernel, n_dp, batch),
        out_shape=(
            jax.ShapeDtypeStruct((block_rows, 4 * width), f32),
            jax.ShapeDtypeStruct((batch, steps, width), f32),
            jax.ShapeDtypeStruct((8, LANES), f32),
        ),
        in_specs=[VMEM_SPEC] * 4 + [ANY_SPEC] + [VMEM_SPEC] * 5,
        out_specs=(VMEM_SPEC, ANY_SPEC, VMEM_SPEC),
        scratch_shapes=[
            pltpu.VMEM((width, 4 * width), low),
            pltpu.VMEM((rows, width), f32),
            pltpu.VMEM((batch, steps, width), f32),
            pltpu.VMEM((8, 2 * width), f32),
            pltpu.VMEM((8, width), f32),
            pltpu.VMEM((n_dp, 8, LANES), f32),
        ]
        + fold_buffers(line, side, block, low)
        + [pltpu.VMEM((2, line) + block, low)]
        + fold_buffers(line, side, (8, LANES), f32)
        + [pltpu.VMEM((line - 1, 8, LANES), f32)]
        + [dma, dma((3,)), dma((2,))]
        + [fold_sems(line, side)] * 2,
        compiler_params=pltpu.CompilerParams(
            collective_id=3, has_side_effects=True, vmem_limit_bytes=VMEM_LIMIT
        ),
    )(ht, ht_other, dpre, dpre_other, weight, base, spread, outer, vectors, dvec)


STEP = 5
NORM_EPS = 1e-05
BETA_ONE = 0.9
BETA_TWO = 0.999
ADAM_EPS = 1e-08
WEIGHT_DECAY = 0.01
RATE_LSTM = 0.05
RATE_MATRIX = 0.02
RATE_VECTOR = 0.3
AXES = ("section", "dp")


def swapped(block):
    return lax.ppermute(block, "section", [(0, 1), (1, 0)])


def adamw(master, first, second, grad, rate):
    first_new = BETA_ONE * first + (1.0 - BETA_ONE) * grad
    second_new = BETA_TWO * second + (1.0 - BETA_TWO) * grad * grad
    first_hat = first_new / (1.0 - BETA_ONE**STEP)
    second_hat = second_new / (1.0 - BETA_TWO**STEP)
    master_new = master - rate * (
        first_hat / (jnp.sqrt(second_hat) + ADAM_EPS) + WEIGHT_DECAY * master
    )
    return (master_new, first_new, second_new)


def slot_major(block):
    batch_size, length, width = block.shape
    padded = jnp.pad(jnp.swapaxes(block, 0, 1), ((0, 0), (0, ROWS - batch_size), (0, 0)))
    return padded.reshape(length * ROWS, width)


def utt_major(block, batch_size):
    width = block.shape[-1]
    return jnp.swapaxes(block.reshape(-1, ROWS, width)[:, :batch_size], 0, 1)


def runner(chip, section, n_dp):
    if chip // LINE_STRIDE % 2 == section:
        return section * n_dp + chip
    return (1 - section) * n_dp + (chip ^ LINE_STRIDE)


def local(
    inputs,
    counts,
    cotangent,
    lstm_master,
    lstm_copy,
    lstm_first,
    lstm_second,
    mats_master,
    mats_copy,
    mats_first,
    mats_second,
    out_master,
    out_copy,
    out_first,
    out_second,
    vec_master,
    vec_first,
    vec_second,
):
    low, f32 = jnp.bfloat16, jnp.float32
    n_dp = lax.axis_size("dp")
    section_index = lax.axis_index("section")
    role = lax.rem(lax.axis_index("dp") // LINE_STRIDE, 2)
    on_first = section_index == 0
    as_encoder = role == 0
    at_home = section_index == role
    chips = range(n_dp)
    batch_size, length, model_width = inputs.shape[1:]
    half = batch_size // 2
    vocab_half = out_copy.shape[1]
    vocab_pad = -(-vocab_half // LANES) * LANES

    homes = [(s * n_dp + c, runner(c, s, n_dp)) for s in range(2) for c in chips]
    away = [pair for pair in homes if pair[0] != pair[1]]
    straight = [(runner(c, s, n_dp), s * n_dp + c) for s in range(2) for c in chips]
    crossed = [(runner(c, s, n_dp), (1 - s) * n_dp + c) for s in range(2) for c in chips]

    def traded(block):
        kept = jnp.where(on_first, block[:half], block[half:])
        other = swapped(jnp.where(on_first, block[half:], block[:half]))
        return jnp.where(on_first, kept, other), jnp.where(on_first, other, kept)

    def to_halves(block):
        low_half, high_half = block[:half], block[half:]
        one = lax.ppermute(jnp.where(as_encoder, low_half, high_half), AXES, straight)
        two = lax.ppermute(jnp.where(as_encoder, high_half, low_half), AXES, crossed)
        return jnp.where(on_first, one, two), jnp.where(on_first, two, one)

    def from_halves(from_encoder, from_decoder):
        one = lax.ppermute(
            jnp.where(on_first, from_encoder, from_decoder), AXES, [(b, a) for a, b in straight]
        )
        two = lax.ppermute(
            jnp.where(on_first, from_decoder, from_encoder), AXES, [(b, a) for a, b in crossed]
        )
        return jnp.where(
            as_encoder, jnp.concatenate([one, two], 0), jnp.concatenate([two, one], 0)
        )

    sequence = jnp.where(at_home, inputs[0], lax.ppermute(inputs[0], AXES, away))
    frames, labels = traded(counts[0])
    label_mask = lax.broadcasted_iota(jnp.int32, (half, length), 1) < labels[:, None]
    grad_low, grad_high = traded(cotangent)
    grad_logits = jnp.stack([grad_low, grad_high]) * label_mask[None, :, :, None].astype(low)
    grad_logits = jnp.pad(grad_logits, ((0, 0),) * 3 + ((0, vocab_pad - vocab_half),))
    grad_logits = grad_logits.reshape(2, half * length, vocab_pad)

    raw_values = sequence.astype(f32)
    center = raw_values - jnp.mean(raw_values, -1, keepdims=True)
    spread = lax.rsqrt(jnp.mean(center * center, -1, keepdims=True) + NORM_EPS)
    base = slot_major(jnp.where(as_encoder, center * spread, raw_values))
    spread = slot_major(spread)

    mats_block = jnp.swapaxes(mats_copy, 1, 2)
    out_block = jnp.pad(out_copy, ((0, 0), (0, vocab_pad - vocab_half)))
    piece = vec_master.shape[1]
    vec_block = jnp.pad(vec_master.astype(low).astype(f32), ((0, 0), (0, LANES - piece)))
    act, cell, h_rows, x_rows, vectors, weight, mats_full, out_full = forward(
        n_dp, base, lstm_copy[0], mats_block, out_block, vec_block
    )
    mats_full = mats_full.reshape(3, 2 * model_width, model_width)
    out_full = out_full.reshape(2, model_width, vocab_pad)

    states = utt_major(h_rows, batch_size).astype(f32)
    result = jnp.where(as_encoder, raw_values + states, states).astype(low)
    memory, decoded = to_halves(result)
    decoded = decoded.reshape(-1, model_width)
    memory = memory.reshape(-1, model_width)
    row = jnp.pad(vectors[7], (0, vocab_pad))
    bias = jnp.stack(
        [row[model_width + s * vocab_half : model_width + s * vocab_half + vocab_pad] for s in range(2)]
    )
    squashed, context, dz, dq, dk, ddec, dmem, vec_rows, logits, logit_sums = attention(
        frames, decoded, memory, mats_full, vectors, out_full, bias, grad_logits
    )
    logits = logits.reshape(2, half, length, vocab_pad)[..., :vocab_half]
    kept = jnp.where(on_first, logits[0], logits[1])
    other = swapped(jnp.where(on_first, logits[1], logits[0]))
    logits = jnp.concatenate([jnp.where(on_first, kept, other), jnp.where(on_first, other, kept)], 0)

    outer = from_halves(dmem, ddec.astype(low)).reshape(batch_size, length, model_width)
    outer = slot_major(outer).astype(f32)
    weight_t = jnp.swapaxes(weight[model_width:], 0, 1)
    h_before = jnp.concatenate([jnp.zeros_like(h_rows[:ROWS]), h_rows[:-ROWS]], 0)
    ht = jnp.concatenate([x_rows.T, h_before.T], 0)
    dpre, dpre_other, ht_other, mats_sum, out_sum = backward(
        n_dp, act, cell, outer, weight_t, ht, (dq, dk, decoded, memory, context, dz, squashed, grad_logits)
    )
    logit_row = jnp.concatenate(
        [
            jnp.zeros((model_width,), f32),
            logit_sums[0, :vocab_half],
            logit_sums[1, :vocab_half],
            jnp.zeros((model_width - 2 * vocab_half,), f32),
        ]
    )
    vec_rows = vec_rows + jnp.pad(logit_row[None], ((7, 0), (0, 0)))
    lstm_sum, inputs_grad, vec_sum = update(
        n_dp, batch_size, ht, ht_other, dpre, dpre_other, weight, base, spread, outer, vectors, vec_rows
    )
    mats_sum = jnp.swapaxes(mats_sum.reshape(3, -1, model_width), 1, 2)
    lstm_new, lstm_first_new, lstm_second_new = adamw(
        lstm_master, lstm_first, lstm_second, lstm_sum[None], RATE_LSTM
    )
    mats_new, mats_first_new, mats_second_new = adamw(
        mats_master, mats_first, mats_second, mats_sum, RATE_MATRIX
    )
    out_new, out_first_new, out_second_new = adamw(
        out_master, out_first, out_second, out_sum[:, :vocab_half], RATE_MATRIX
    )
    vec_new, vec_first_new, vec_second_new = adamw(
        vec_master, vec_first, vec_second, vec_sum[:, :piece], RATE_VECTOR
    )
    return (
        logits,
        inputs_grad[None],
        lstm_new,
        lstm_first_new,
        lstm_second_new,
        lstm_new.astype(low),
        mats_new,
        mats_first_new,
        mats_second_new,
        mats_new.astype(low),
        out_new,
        out_first_new,
        out_second_new,
        out_new.astype(low),
        vec_new,
        vec_first_new,
        vec_second_new,
    )


def solution(mesh):
    lstm = P("section", "dp", None)
    mats = P(None, None, ("section", "dp"))
    out = P("dp", "section")
    vec = P(None, ("section", "dp"))
    logits = P("dp", None, "section")
    rows = P("section", "dp", None, None)
    groups = (lstm,) * 4 + (mats,) * 4 + (out,) * 4 + (vec,) * 3
    return jax.shard_map(
        local,
        mesh=mesh,
        in_specs=(rows, P("section", "dp"), logits) + groups,
        out_specs=(logits, rows) + groups,
        check_vma=False,
    )
```

time: 1450 us -> 587 us (0.40)
  waiting for transfers between devices: 987 us -> 1.4 us
  Pallas kernels: 136 us -> 492 us
  blocking collectives: 114 us -> 0 us
  local copies, waits for them, and re-layouts: 109 us -> 41 us
  matrix products: 32.2 us -> 0 us
    reduce_scatter x3 -> x0, waiting for transfers between devices: 420 us -> none  [the longest x1 344 us: local(): lax.psum_scatter(weight_grad.astype(low)[None], 'dp', scatter_dimension=1...]
    pallas_call x2 -> x3, Pallas kernels: 79.2 us -> 432 us  [the longest x1 172 us: forward(): pl.pallas_call(functools.partial(forward_kernel, n_dp), out_shape=(jax.Sh...]
    unnamed x10 -> x0, waiting for transfers between devices: 351 us -> none
    all_gather x3 -> x0, waiting for transfers between devices: 215 us -> none  [the longest x1 183 us: local(): lax.all_gather(lstm_copy, 'dp', axis=1, tiled=True)]
    all_gather x2 -> x0, blocking collectives: 114 us -> none  [the longest x1 64.9 us: local(): lax.all_gather(vec_master.astype(low), ('section', 'dp'), axis=1, tiled=T...]
    dot_general x10 -> x0, matrix products: 32.2 us -> none  [the longest x9 31.4 us: contract(): lax.dot_general(left, right, (((left_dim,), (right_dim,)), ((), ())), pre...]
    unnamed x77 -> x39, local copies, waits for them, and re-layouts: 33.7 us -> 2.05 us
    another operation x1, local copies, waits for them, and re-layouts: 27.5 us -> 0.01 us  [local(): jnp.stack([contract(decoded, dq, 0, 0), contract(memory, dk, 0, 0), jnp.c...]
  transfers between devices with their start and end apart: 13 -> 8, of which waited for: 7 -> 1; matrix products, arithmetic and copies ran while one was open for 12% -> 8% of each run, Pallas kernels for 6% -> 0%
where the time goes in v2:
time: 587 us; the launch traced here: 579 us
  Pallas kernels  492 us (84%)
  local copies, waits for them, and re-layouts  41 us (7%)
  other arithmetic  28.9 us (5%)
  starting transfers between devices  14.6 us (2%)
    pallas_call x1, Pallas kernels, forward(): pl.pallas_call(functools.partial(forward_kernel, n_dp), out_shape=(jax.Sh...  172 us
    pallas_call x1, Pallas kernels, backward(): pl.pallas_call(functools.partial(backward_kernel, n_dp), out_shape=(jax.S...  134 us
    pallas_call x1, Pallas kernels, update(): pl.pallas_call(functools.partial(update_kernel, n_dp, batch), out_shape=(...  126 us
    pallas_call x1, Pallas kernels, attention(): pl.pallas_call(attention_kernel, out_shape=(jax.ShapeDtypeStruct((rows, w...  59.9 us
    pallas_call x3, local copies, waits for them, and re-layouts, forward(): pl.pallas_call(functools.partial(forward_kernel, n_dp), out_shape=(jax.Sh...  24.4 us
  transfers between devices with their start and end apart: 8, of which 1 were waited for; matrix products, arithmetic and copies ran while one was open for 8% of the time, Pallas kernels for 0%

profile of v2, /device:TPU:0, one launch (start us, length us, event | category | flops | bytes accessed | tf_op | source)
XLA Modules:
  0.0 579.2 jit_solution(6579482617131499169)
XLA Ops:
  0.7 0.8 collective-permute-start.1
  1.5 1.0 broadcast_select_fusion.8
  2.5 4.4 collective-permute-start.4
  6.9 0.8 fusion.14
  9.0 1.5 pad.35.out_ref
  10.5 0.8 broadcast_select_fusion.12
  12.1 1.0 select_bitcast_fusion.2
  15.6 1.3 pad.34.clone
  16.8 172.2 %shard_map.305 = (f32[384,4096]{1,0:T(8,128)}, f32[400,1024]{1,0:T(8,128)}, bf16[384,1024]{1,0:T(8,128)(2,1)}, bf16[384,1024]{1,0:T(8,128)(2,1)}, f32[8,2048]{1,...) custom-call(f32[384,1024]{1,0:T(8,128)} %bitcast.69, ...), custom_call_target="tpu_custom_call" | custom-call | tf_op jit(solution)/shard_map/pallas_call | solution.py:693
  189.0 0.9 fusion.23
  189.9 1.5 copy.55
  193.1 1.8 collective-permute-start.3
  195.0 22.6 %copy.57 = bf16[2048,4096]{0,1:T(8,128)(2,1)} copy(bf16[2048,4096]{1,0:T(8,128)(2,1)} %get-tuple-element.53.w_ref) | data formatting | bytes 33554432 | tf_op jit(solution)/shard_map/pallas_call | solution.py:693
  217.5 7.7 %slice_bitcast_fusion.wt_ref = bf16[4096,1024]{1,0:T(8,128)(2,1)} fusion(bf16[2048,4096]{0,1:T(8,128)(2,1)} %copy.57), kind=kLoop, calls=%fused_computation | loop fusion | bytes 16777216 | tf_op jit(solution)/shard_map/transpose | solution.py:1412
  226.8 0.8 reshape.146.spread_ref
  227.6 1.3 pad_maximum_fusion.ht_ref
  228.9 1.8 broadcast_select_fusion.5
  230.7 59.9 %shard_map.306 = (bf16[144,1024]{1,0:T(8,128)(2,1)}, bf16[144,1024]{1,0:T(8,128)(2,1)}, bf16[144,1024]{1,0:T(8,128)(2,1)}, bf16[2,144,1024]{2,1,0:T(8,128)(2,1)}...) custom-call(s32[6]{0:T(128)} %copy-done.17, ...), custom_call_target="tpu_custom_call" | custom-call | tf_op jit(solution)/shard_map/pallas_call | solution.py:279
  290.6 0.8 fusion.24
  291.4 1.2 broadcast_select_fusion.2
  293.3 6.2 %collective-permute-start.7 = (bf16[144,1024]{1,0:T(8,128)(2,1)S(1)}, bf16[144,1024]{1,0:T(8,128)(2,1)S(1)}, u32[]{:S(2)}, u32[]{:S(2)}) collective-permute-start(bf16[144,1024]{1,0:T(8,128)(2,1)S(1)} %get-tuple-element.87), channel_id=1, source_target_pairs={{16,0},{17,1},{18,2},{19,3},{20,16},{21,17},{22,18},{23,19},{24,8}... | collective-permute-start | bytes 884744 | tf_op jit(solution)/shard_map/ppermute | solution.py:1362
  299.5 1.0 select_bitcast_fusion
  300.7 1.5 pad_add_fusion.dvec_ref
  302.9 1.4 collective-permute-done.7
  305.0 1.4 bitcast_convert_fusion.outer_ref
  306.3 133.6 %shard_map.307 = (bf16[384,4096]{1,0:T(8,128)(2,1)}, bf16[384,2048]{1,0:T(8,128)(2,1)}, bf16[2048,384]{1,0:T(8,128)(2,1)}, f32[192,1024]{1,0:T(8,128)}, f32[64,512]{1,0:T(8,128)}) custom-call(f32[384,4096]{1,0:T(8,128)} %get-tuple-element.49.act_ref, f32[400,1024]{1,0:T(8,128)} %get-tuple-element.50.cell_ref, f32[384,1024]{1,0:T(8,128)} %bitcast_convert_fusion.outer_ref, ...), custom_call_target="tpu_custom_call" | custom-call | tf_op jit(solution)/shard_map/pallas_call | solution.py:1059
  440.0 126.2 %shard_map.308 = (f32[128,4096]{1,0:T(8,128)}, f32[12,24,1024]{2,1,0:T(8,128)}, f32[8,128]{1,0:T(8,128)}) custom-call(bf16[2048,384]{1,0:T(8,128)(2,1)} %pad_maximum_fusion.ht_ref, bf16[2048,384]{1,0:T(8,128)(2,1)} %get-tuple-element.59.ht_other, bf16[384,4096]{1,0:T(8,128)(2,1)} %get-tuple-element.60.dpre_ref, ...), custom_call_target="tpu_custom_call" | custom-call | tf_op jit(solution)/shard_map/pallas_call | solution.py:1236
  566.3 1.3 multiply_subtract_fusion.3
  567.6 7.3 %fusion.21 = (bf16[1,128,4096]{2,1,0:T(8,128)(2,1)}, f32[1,128,4096]{2,1,0:T(8,128)}, f32[1,128,4096]{2,1,0:T(8,128)}, f32[1,128,4096]{2,1,0:T(8,128)}) fusion(f32[1,128,4096]{2,1,0:T(8,128)S(1)} %copy-done.1, f32[128,4096]{1,0:T(8,128)} %get-tuple-element.65, f32[1,128,4096]{2,1,0:T(8,128)} %param.23, f32[1,128,4096]{2,1,0:T(8,128)} %param.24), kind=kLoop, calls=%fused_computation.68 | loop fusion | flops 8388608 | bytes 15728640 | tf_op jit(solution)/shard_map/convert_element_type | solution.py:1449
  574.9 2.0 fusion.19
  576.9 0.8 fusion.17
  577.7 1.0 copy.67
  (75 shorter events, 10.1 us)
Async XLA Ops:
  0.7 13.3 %copy-start.9 = (bf16[1,12,24,1024]{3,2,1,0:T(8,128)(2,1)S(1)}, bf16[1,12,24,1024]{3,2,1,0:T(8,128)(2,1)}, u32[]{:S(2)}) copy-start(bf16[1,12,24,1024]{3,2,1,0:T(8,128)(2,1)} %param.18) | copy-start | bytes 1769476
  0.7 13.3 %collective-permute-start.1 = (bf16[12,24,1024]{2,1,0:T(8,128)(2,1)}, bf16[12,24,1024]{2,1,0:T(8,128)(2,1)S(1)}, u32[]{:S(2)}, u32[]{:S(2)}) collective-permute-start(bf16[12,24,1024]{2,1,0:T(8,128)(2,1)} %bitcast.89), channel_id=1, source_target_pairs={{4,16},{5,17},{6,18},{7,19},{12,24},{13,25},{14,26},{15,27},{16,4}... | collective-permute-start | bytes 1769480 | tf_op jit(solution)/shard_map/ppermute | solution.py:1369
  2.5 9.6 %collective-permute-start.4 = (bf16[6,24,500]{2,1,0:T(8,128)(2,1)S(1)}, bf16[6,24,500]{2,1,0:T(8,128)(2,1)S(1)}, u32[]{:S(2)}, u32[]{:S(2)}) collective-permute-start(bf16[6,24,500]{2,1,0:T(8,128)(2,1)S(1)} %broadcast_select_fusion.8), channel_id=1, source_target_pairs={{0,16},{16,0},{1,17},{17,1},{2,18},{18,2},{3,19},{19,3},{4,20},{20... | collective-permute-start | bytes 432008 | tf_op jit(solution)/shard_map/ppermute | solution.py:1278
  7.7 2.8 collective-permute-start
  11.3 0.7 copy-start.17
  189.0 2.4 copy-start
  192.6 36.3 %collective-permute-start.2 = (bf16[6,24,1024]{2,1,0:T(8,128)(2,1)}, bf16[6,24,1024]{2,1,0:T(8,128)(2,1)S(1)}, u32[]{:S(2)}, u32[]{:S(2)}) collective-permute-start(bf16[6,24,1024]{2,1,0:T(8,128)(2,1)} %get-tuple-element.91), channel_id=1, source_target_pairs={{0,16},{1,17},{2,18},{3,19},{16,20},{17,21},{18,22},{19,23},{8,24}... | collective-permute-start | bytes 884744 | tf_op jit(solution)/shard_map/ppermute | solution.py:1355
  193.1 35.8 %collective-permute-start.3 = (bf16[6,24,1024]{2,1,0:T(8,128)(2,1)S(1)}, bf16[6,24,1024]{2,1,0:T(8,128)(2,1)}, u32[]{:S(2)}, u32[]{:S(2)}) collective-permute-start(bf16[6,24,1024]{2,1,0:T(8,128)(2,1)S(1)} %get-tuple-element.90), channel_id=1, source_target_pairs={{0,0},{1,1},{2,2},{3,3},{16,4},{17,5},{18,6},{19,7},{8,8},{9,9},{1... | collective-permute-start | bytes 884744 | tf_op jit(solution)/shard_map/ppermute | solution.py:1354
  225.2 1.1 copy-start.4
  290.6 11.5 %copy-start.3 = (bf16[2,144,512]{2,1,0:T(8,128)(2,1)S(1)}, bf16[2,144,512]{2,1,0:T(8,128)(2,1)}, u32[]{:S(2)}) copy-start(bf16[2,144,512]{2,1,0:T(8,128)(2,1)} %get-tuple-element.47) | copy-start | bytes 884740
  292.6 10.3 %collective-permute-start.6 = (bf16[144,1024]{1,0:T(8,128)(2,1)S(1)}, bf16[144,1024]{1,0:T(8,128)(2,1)S(1)}, u32[]{:S(2)}, u32[]{:S(2)}) collective-permute-start(bf16[144,1024]{1,0:T(8,128)(2,1)S(1)} %get-tuple-element.86), channel_id=1, source_target_pairs={{0,0},{1,1},{2,2},{3,3},{4,16},{5,17},{6,18},{7,19},{8,8},{9,9},{1... | collective-permute-start | bytes 884744 | tf_op jit(solution)/shard_map/ppermute | solution.py:1359
  293.3 11.0 %collective-permute-start.7 = (bf16[144,1024]{1,0:T(8,128)(2,1)S(1)}, bf16[144,1024]{1,0:T(8,128)(2,1)S(1)}, u32[]{:S(2)}, u32[]{:S(2)}) collective-permute-start(bf16[144,1024]{1,0:T(8,128)(2,1)S(1)} %get-tuple-element.87), channel_id=1, source_target_pairs={{16,0},{17,1},{18,2},{19,3},{20,16},{21,17},{22,18},{23,19},{24,8}... | collective-permute-start | bytes 884744 | tf_op jit(solution)/shard_map/ppermute | solution.py:1362
  300.5 1.7 collective-permute-start.5
  440.0 126.3 %copy-start.14 = (f32[8,64]{1,0:T(8,128)S(1)}, f32[8,64]{1,0:T(8,128)}, u32[]{:S(2)}) copy-start(f32[8,64]{1,0:T(8,128)} %param.33) | copy-start | bytes 6148
  440.0 126.3 %copy-start.15 = (f32[8,64]{1,0:T(8,128)S(1)}, f32[8,64]{1,0:T(8,128)}, u32[]{:S(2)}) copy-start(f32[8,64]{1,0:T(8,128)} %param.34) | copy-start | bytes 6148
  440.0 126.3 %copy-start.16 = (f32[8,64]{1,0:T(8,128)S(1)}, f32[8,64]{1,0:T(8,128)}, u32[]{:S(2)}) copy-start(f32[8,64]{1,0:T(8,128)} %param.35) | copy-start | bytes 6148
  440.0 127.6 %copy-start.1 = (f32[1,128,4096]{2,1,0:T(8,128)S(1)}, f32[1,128,4096]{2,1,0:T(8,128)}, u32[]{:S(2)}) copy-start(f32[1,128,4096]{2,1,0:T(8,128)} %param.21) | copy-start | bytes 6291460
  567.6 7.3 %copy-start.5 = (f32[3,1024,64]{1,2,0:T(8,128)S(1)}, f32[3,1024,64]{1,2,0:T(8,128)}, u32[]{:S(2)}) copy-start(f32[3,1024,64]{1,2,0:T(8,128)} %param.25) | copy-start | bytes 2359300
  567.6 7.3 %copy-start.6 = (f32[3,1024,64]{1,2,0:T(8,128)S(1)}, f32[3,1024,64]{1,2,0:T(8,128)}, u32[]{:S(2)}) copy-start(f32[3,1024,64]{1,2,0:T(8,128)} %param.27) | copy-start | bytes 2359300
  567.6 7.3 %copy-start.7 = (f32[3,1024,64]{1,2,0:T(8,128)S(1)}, f32[3,1024,64]{1,2,0:T(8,128)}, u32[]{:S(2)}) copy-start(f32[3,1024,64]{1,2,0:T(8,128)} %param.28) | copy-start | bytes 2359300
  567.6 7.3 %copy-start.8 = (f32[192,1024]{1,0:T(8,128)S(1)}, f32[192,1024]{1,0:T(8,128)}, u32[]{:S(2)}) copy-start(f32[192,1024]{1,0:T(8,128)} %get-tuple-element.66) | copy-start | bytes 2359300
  574.9 2.0 copy-start.10
  574.9 2.0 copy-start.11
  574.9 2.0 copy-start.12
  574.9 2.0 copy-start.13
  574.9 2.8 copy-start.2

commit v3 on v2

--- a/solution.py
+++ b/solution.py
@@ -319,6 +319,7 @@
 ANY_SPEC = pl.BlockSpec(memory_space=pl.ANY)
 DP_LAYOUTS = {16: (4, 2, 1, 2), 128: (8, 4, 1, 32)}
 LINE_STRIDE = 4
+TURN = 256
 
 
 def flipped(value, k):
@@ -410,10 +411,10 @@
             self.sems["cr"].at[kg, kf, kz],
         )
 
-    def stage_one(self, wait_line):
+    def stage_one(self, *steps):
         place = self.place
-        for kz in range(place.line):
-            wait_line(kz)
+        for kz in steps or range(place.line):
+            self.wait_line(kz)
             target = self.here(place.block(kz))
             for kf in range(1, place.side):
                 self.send(
@@ -489,7 +490,7 @@
             spread.arrived(spread.here(place.block(kz)), sems["zr"].at[kz])
 
     spread.begin = begin
-    spread.first_stage = lambda: spread.stage_one(wait_line)
+    spread.wait_line = wait_line
     return spread
 
 
@@ -526,26 +527,25 @@
         for k in range(1, place.line)
     ]
 
-    def each(action):
-        @pl.when(mine)
+    guest = jnp.logical_not(mine)
+
+    def each(condition, steps, action):
+        @pl.when(condition)
         def _():
-            action(cross)
-            for k in range(2, place.line, 2):
-                for copy in copies[k - 1]:
+            for k in steps:
+                for copy in copies[k - 1] if k else [cross]:
                     action(copy)
 
-        @pl.when(jnp.logical_not(mine))
-        def _():
-            for k in range(1, place.line, 2):
-                for copy in copies[k - 1]:
-                    action(copy)
+    def start(copy):
+        copy.start()
 
     def begin():
         @pl.when(mine)
         def _():
             kept.start()
 
-        each(lambda copy: copy.start())
+        each(mine, range(0, place.line, 2), start)
+        each(guest, range(1, place.line, 2), start)
 
     def wait_line(kz):
         if kz == 0:
@@ -561,11 +561,15 @@
         else:
             spread.arrived(spread.here(place.block(kz)), sems["zr"].at[kz])
 
+    def finished(copy):
+        copy.wait_send()
+
     def sent_line():
-        each(lambda copy: copy.wait_send())
+        each(mine, range(0, place.line, 2), finished)
+        each(guest, range(1, place.line, 2), finished)
 
     spread.begin = begin
-    spread.first_stage = lambda: spread.stage_one(wait_line)
+    spread.wait_line = wait_line
     spread.sent_line = sent_line
     return spread
 
@@ -583,9 +587,11 @@
     x_ref,
     vectors_ref,
     w_out,
+    wt_out,
     mats_out,
     out_out,
     w_s,
+    wt_s,
     vec_s,
     state,
     keep_sem,
@@ -606,13 +612,15 @@
     cell_ref[:ROWS] = jnp.zeros((ROWS, width), jnp.float32)
     vecs.begin()
     matrix.begin()
-    matrix.first_stage()
-    vecs.first_stage()
+    matrix.stage_one()
+    vecs.stage_one()
+    outs.begin()
+    mats.begin()
     matrix.stage_two()
     vecs.stage_two()
+    outs.stage_one(0)
+    mats.stage_one(0)
     matrix.stage_three()
-    outs.begin()
-    mats.begin()
     vecs.stage_three()
     vecs.finish()
     piece = 2 * width // (2 * n_dp)
@@ -629,7 +637,7 @@
     shift = jnp.where(encoder, vectors_ref[4:5, width:], 0.0)
     x_ref[...] = (base_ref[...] * gain + shift).astype(jnp.bfloat16)
     matrix.finish()
-    keep = pltpu.make_async_copy(w_s, w_out, keep_sem)
+    keep = pltpu.make_async_copy(w_s.at[:width], w_out, keep_sem.at[0])
     keep.start()
     for q in range(4):
         columns = slice(q * width, (q + 1) * width)
@@ -668,18 +676,27 @@
         state[...] = hidden_new
         return carry
 
-    first, second = steps * 3 // 8, steps * 3 // 4
-    outs.first_stage()
-    mats.first_stage()
-    lax.fori_loop(0, first, step, 0)
+    line_rest = range(1, place.line)
+    marks = [steps * n // 24 for n in (0, 4, 10, 18, 24)]
+    lax.fori_loop(marks[0], marks[1], step, 0)
+    outs.stage_one(*line_rest)
+    mats.stage_one(*line_rest)
+    lax.fori_loop(marks[1], marks[2], step, 0)
     outs.stage_two()
     mats.stage_two()
-    lax.fori_loop(first, second, step, 0)
+    lax.fori_loop(marks[2], marks[3], step, 0)
     outs.stage_three()
-    lax.fori_loop(second, steps, step, 0)
+    lax.fori_loop(marks[3], marks[4], step, 0)
+    for q in range(4):
+        for n in range(width // TURN):
+            rows = slice(width + n * TURN, width + (n + 1) * TURN)
+            wt_s[q, :, n * TURN : (n + 1) * TURN] = w_s[rows, q * width : (q + 1) * width].T
+    keep_turned = pltpu.make_async_copy(wt_s, wt_out, keep_sem.at[1])
+    keep_turned.start()
     mats.stage_three()
     outs.finish()
     mats.finish()
+    keep_turned.wait()
     keep.wait()
     matrix.sent_line()
     for spread in (matrix, vecs, outs, mats):
@@ -698,17 +715,19 @@
             jax.ShapeDtypeStruct((rows, width), low),
             jax.ShapeDtypeStruct((rows, width), low),
             jax.ShapeDtypeStruct((8, 2 * width), f32),
-            jax.ShapeDtypeStruct((2 * width, 4 * width), low),
+            jax.ShapeDtypeStruct((width, 4 * width), low),
+            jax.ShapeDtypeStruct((4, width, width), low),
             jax.ShapeDtypeStruct((3, 2, n_dp) + mats_block.shape[1:], low),
             jax.ShapeDtypeStruct((2, n_dp) + out_block.shape, low),
         ),
         in_specs=[VMEM_SPEC, ANY_SPEC, ANY_SPEC, ANY_SPEC, VMEM_SPEC],
-        out_specs=(VMEM_SPEC,) * 5 + (ANY_SPEC,) * 3,
+        out_specs=(VMEM_SPEC,) * 5 + (ANY_SPEC,) * 4,
         scratch_shapes=[
             pltpu.VMEM((2 * width, 4 * width), low),
+            pltpu.VMEM((4, width, width), low),
             pltpu.VMEM((2, n_dp, 8, LANES), f32),
             pltpu.VMEM((ROWS, width), low),
-            pltpu.SemaphoreType.DMA,
+            pltpu.SemaphoreType.DMA((2,)),
         ]
         + [spread_sems(line, side)] * 4,
         compiler_params=pltpu.CompilerParams(
@@ -731,11 +750,11 @@
         place = self.place
         remote(target, target, semaphore, semaphore, (1 - place.core, place.chip)).wait_recv()
 
-    def stage_a(self):
+    def stage_a(self, *steps):
         place = self.place
-        for kg in range(1, place.side):
-            for kf in reversed(range(place.side)):
-                for kz in range(place.line):
+        for kz in steps or reversed(range(place.line)):
+            for kg in range(1, place.side):
+                for kf in reversed(range(place.side)):
                     source = self.stage.at[kg - 1, kf, kz]
                     source[...] = self.part(kz, kf, kg).astype(source.dtype)
                     self.send(
@@ -746,10 +765,10 @@
                         self.sems["gr"].at[kg, kf, kz],
                     )
 
-    def stage_b(self):
+    def stage_b(self, *steps):
         place = self.place
-        for kf in reversed(range(place.side)):
-            for kz in range(place.line):
+        for kz in steps or reversed(range(place.line)):
+            for kf in reversed(range(place.side)):
                 total = self.part(kz, kf, 0)
                 for kg in range(1, place.side):
                     self.arrived(self.near.at[kg - 1, kf, kz], self.sems["gr"].at[kg, kf, kz])
@@ -771,40 +790,42 @@
         for kf in range(1, place.side):
             self.arrived(self.far.at[kf - 1, kz], self.sems["fr"].at[kf, kz])
             total = total + self.far[kf - 1, kz].astype(jnp.float32)
-        source = self.far.at[0, kz]
-        source[...] = total.astype(source.dtype)
-        return source
+        return total.astype(self.far.dtype)
 
     def sent_all(self):
         for copy in self.sent:
             copy.wait_send()
 
 
-class FoldEven(Fold):
-    def __init__(self, place, part, stage, near, far, end, sems):
-        super().__init__(place, part, stage, near, far, sems)
-        self.end = end
-
-    def stage_c(self):
+class FoldLine:
+    def __init__(self, place, parts, end, sems):
+        self.place, self.parts, self.end, self.sems = place, parts, end, sems
+
+    def begin(self, *steps):
         place = self.place
-        for kz in reversed(range(place.line)):
-            source = self.summed(kz)
-            if kz:
-                self.send(
-                    source,
-                    self.end.at[kz - 1],
-                    (place.core, place.chip + place.along[kz]),
-                    self.sems["zs"].at[kz, 0],
-                    self.sems["zr"].at[kz],
-                )
+        for kz in steps or reversed(range(1, place.line)):
+            self.copy(kz).start()
+
+    def copy(self, kz):
+        place = self.place
+        return remote(
+            self.parts.at[kz],
+            self.end.at[kz - 1],
+            self.sems["zs"].at[kz, 0],
+            self.sems["zr"].at[kz],
+            (place.core, place.chip + place.along[kz]),
+        )
 
     def result(self):
-        place = self.place
-        total = self.far[0, 0].astype(jnp.float32)
-        for kz in range(1, place.line):
-            self.arrived(self.end.at[kz - 1], self.sems["zr"].at[kz])
+        total = self.parts[0].astype(jnp.float32)
+        for kz in range(1, self.place.line):
+            self.copy(kz).wait_recv()
             total = total + self.end[kz - 1].astype(jnp.float32)
         return total
+
+    def sent_all(self):
+        for kz in range(1, self.place.line):
+            self.copy(kz).wait_send()
 
 
 class FoldRole(Fold):
@@ -812,34 +833,31 @@
         super().__init__(place, part, stage, near, far, sems)
         self.end = end
 
-    def stage_c(self):
+    def stage_c(self, kz):
         place = self.place
-        self.line_copies = []
-        for kz in reversed(range(place.line)):
-            source = self.summed(kz)
-            if kz:
-                copy = remote(
-                    source,
-                    self.end.at[place.core, kz],
-                    self.sems["zs"].at[kz, 0],
-                    self.sems["er"].at[place.core, kz],
-                    (place.role, place.chip + place.along[kz]),
-                )
-                copy.start()
-                self.sent.append(copy)
-            else:
-                self.last = source
-                self.cross = remote(
-                    source,
-                    self.end.at[place.core, 0],
-                    self.sems["zs"].at[0, 0],
-                    self.sems["er"].at[place.core, 0],
-                    (1 - place.core, place.chip),
-                )
-
-                @pl.when(place.core != place.role)
-                def _():
-                    self.cross.start()
+        source = self.far.at[0, kz]
+        source[...] = self.summed(kz)
+        if kz:
+            self.send(
+                source,
+                self.end.at[place.core, kz // 2],
+                (place.role, place.chip + place.along[kz]),
+                self.sems["zs"].at[kz, 0],
+                self.sems["er"].at[place.core, kz // 2],
+            )
+        else:
+            self.last = source
+            self.cross = remote(
+                source,
+                self.end.at[place.core, 0],
+                self.sems["zs"].at[0, 0],
+                self.sems["er"].at[place.core, 0],
+                (1 - place.core, place.chip),
+            )
+
+            @pl.when(place.core != place.role)
+            def _():
+                self.cross.start()
 
     def result(self, sum_ref):
         place = self.place
@@ -855,8 +873,8 @@
                 total = jnp.zeros((rows, half), jnp.float32)
                 for kz in sources:
                     if kz:
-                        self.arrived(self.end.at[core, kz], self.sems["er"].at[core, kz])
-                        total = total + self.end[core, kz].astype(jnp.float32)
+                        self.arrived(self.end.at[core, kz // 2], self.sems["er"].at[core, kz // 2])
+                        total = total + self.end[core, kz // 2].astype(jnp.float32)
                 sum_ref[:, core * half : (core + 1) * half] = total
 
         @pl.when(mine)
@@ -882,7 +900,7 @@
         "fr": dma((side, line)),
         "zs": dma((line, 1)),
         "zr": dma((line,)),
-        "er": dma((2, line)),
+        "er": dma((2, line // 2)),
     }
 
 
@@ -890,7 +908,6 @@
     return [
         pltpu.VMEM((side - 1, side, line) + shape, dtype),
         pltpu.VMEM((side - 1, side, line) + shape, dtype),
-        pltpu.VMEM((side - 1, line) + shape, dtype),
     ]
 
 
@@ -912,8 +929,8 @@
     dpre_ref,
     dpre_other,
     ht_other,
-    mats_sum,
-    out_sum,
+    mats_part,
+    out_part,
     state,
     held,
     facts,
@@ -922,12 +939,10 @@
     g_out,
     m_stage,
     m_near,
-    m_far,
-    m_end,
     o_stage,
     o_near,
+    m_far,
     o_far,
-    o_end,
     fact_sems,
     pre_sems,
     ht_sems,
@@ -958,8 +973,12 @@
         rows = pl.ds(pl.multiple_of(t * ROWS, ROWS), ROWS)
         after = pl.ds(pl.multiple_of((t + 1) * ROWS, ROWS), ROWS)
         hidden_total = outer_ref[rows] + jnp.dot(
-            state[...], wt_ref[...], preferred_element_type=f32
+            state[:, :width], wt_ref[0], preferred_element_type=f32
         )
+        for q in range(1, 4):
+            hidden_total = hidden_total + jnp.dot(
+                state[:, q * width : (q + 1) * width], wt_ref[q], preferred_element_type=f32
+            )
         in_gate = act_ref[rows, :width]
         forget = act_ref[rows, width : 2 * width]
         candidate = act_ref[rows, 2 * width : 3 * width]
@@ -1016,29 +1035,29 @@
         for block in range(n_dp):
             g_out[block] = total[block * out_rows : (block + 1) * out_rows]
 
-    mats = FoldEven(
-        place, lambda kz, kf, kg: g_mats[place.block(kz, kf, kg)].astype(f32), m_stage, m_near, m_far, m_end, sems_m
-    )
-    outs = FoldEven(
-        place, lambda kz, kf, kg: g_out[place.block(kz, kf, kg)].astype(f32), o_stage, o_near, o_far, o_end, sems_o
-    )
-    lax.fori_loop(0, share, step, 0)
-    hand_over(0)
+    mats = Fold(
+        place, lambda kz, kf, kg: g_mats[place.block(kz, kf, kg)].astype(f32), m_stage, m_near, m_far, sems_m
+    )
+    outs = Fold(
+        place, lambda kz, kf, kg: g_out[place.block(kz, kf, kg)].astype(f32), o_stage, o_near, o_far, sems_o
+    )
     matrices()
     mats.stage_a()
     outs.stage_a()
-    lax.fori_loop(share, 2 * share, step, 0)
-    hand_over(1)
-    lax.fori_loop(2 * share, 3 * share, step, 0)
-    hand_over(2)
-    mats.stage_b()
+    lax.fori_loop(0, share, step, 0)
+    hand_over(0)
+    lines = list(reversed(range(place.line)))
+    for n in range(1, shares):
+        for kz in lines[(n - 1) * place.line // shares : n * place.line // shares]:
+            mats.stage_b(kz)
+        lax.fori_loop(n * share, (n + 1) * share, step, 0)
+        hand_over(n)
+    for kz in lines[(shares - 1) * place.line // shares :]:
+        mats.stage_b(kz)
     outs.stage_b()
-    lax.fori_loop(3 * share, steps, step, 0)
-    hand_over(3)
-    mats.stage_c()
-    outs.stage_c()
-    mats_sum[...] = mats.result()
-    out_sum[...] = outs.result()
+    for kz in lines:
+        mats_part[kz] = mats.summed(kz)
+        out_part[kz] = outs.summed(kz)
     for copy in handed[8:]:
         copy.wait_recv()
     for copy in handed:
@@ -1062,8 +1081,8 @@
             jax.ShapeDtypeStruct((rows, 4 * width), low),
             jax.ShapeDtypeStruct((rows, 2 * width), low),
             jax.ShapeDtypeStruct(ht.shape, low),
-            jax.ShapeDtypeStruct(mats_block, f32),
-            jax.ShapeDtypeStruct(out_block, f32),
+            jax.ShapeDtypeStruct((line,) + mats_block, low),
+            jax.ShapeDtypeStruct((line,) + out_block, low),
         ),
         in_specs=[VMEM_SPEC] * 4 + [ANY_SPEC] + [VMEM_SPEC] * 8,
         out_specs=(VMEM_SPEC, VMEM_SPEC, ANY_SPEC, VMEM_SPEC, VMEM_SPEC),
@@ -1076,9 +1095,8 @@
             pltpu.VMEM((n_dp,) + out_block, low),
         ]
         + fold_buffers(line, side, mats_block, low)
-        + [pltpu.VMEM((line - 1,) + mats_block, low)]
         + fold_buffers(line, side, out_block, low)
-        + [pltpu.VMEM((line - 1,) + out_block, low)]
+        + [pltpu.VMEM((side - 1, line) + block, low) for block in (mats_block, out_block)]
         + [dma((2, 8)), dma((2, 4)), dma((2,))]
         + [fold_sems(line, side)] * 2,
         compiler_params=pltpu.CompilerParams(
@@ -1100,9 +1118,13 @@
     outer_ref,
     vectors_ref,
     dvec_ref,
+    mats_part,
+    out_part,
     sum_ref,
     gin_ref,
     vec_sum,
+    mats_sum,
+    out_sum,
     w_s,
     gin_s,
     gin_u,
@@ -1111,23 +1133,28 @@
     vec_parts,
     l_stage,
     l_near,
+    v_stage,
+    v_near,
     l_far,
     l_end,
-    v_stage,
-    v_near,
     v_far,
+    v_parts,
     v_end,
+    m_end,
+    o_end,
     w_sem,
     gin_sems,
     vec_sems,
     sems_l,
     sems_v,
+    sems_m,
+    sems_o,
 ):
     width = base_ref.shape[1]
     steps = base_ref.shape[0] // ROWS
     low, f32 = jnp.bfloat16, jnp.float32
     place = Place(n_dp)
-    load = pltpu.make_async_copy(w_ref.at[:width], w_s, w_sem)
+    load = pltpu.make_async_copy(w_ref, w_s, w_sem)
     load.start()
     place.greet()
     core = place.core
@@ -1143,7 +1170,11 @@
         )
 
     matrix = FoldRole(place, part, l_stage, l_near, l_far, l_end, sems_l)
+    mats = FoldLine(place, mats_part, m_end, sems_m)
+    outs = FoldLine(place, out_part, o_end, sems_o)
     matrix.stage_a()
+    mats.begin()
+    outs.begin()
 
     load.wait()
     gin_s[...] = contract(dpre_ref[...], w_s[...], 1, 1)
@@ -1201,16 +1232,24 @@
         tile = total[:, (block // per_tile) * LANES : (block // per_tile + 1) * LANES]
         turn = (block % per_tile) * piece
         vec_parts[block] = pltpu.roll(tile, LANES - turn, 1) if turn else tile
-    vecs = FoldEven(
-        place, lambda kz, kf, kg: vec_parts[place.block(kz, kf, kg)], v_stage, v_near, v_far, v_end, sems_v
-    )
+    vecs = Fold(place, lambda kz, kf, kg: vec_parts[place.block(kz, kf, kg)], v_stage, v_near, v_far, sems_v)
+    vec_line = FoldLine(place, v_parts, v_end, sems_v)
     vecs.stage_a()
-    matrix.stage_b()
-    vecs.stage_b()
-    matrix.stage_c()
-    vecs.stage_c()
+    lines = list(reversed(range(place.line)))
+    matrix.stage_b(lines[0])
+    for n, kz in enumerate(lines[1:]):
+        if n == place.line // 2 - 1:
+            vecs.stage_b()
+        matrix.stage_b(kz)
+        matrix.stage_c(lines[n])
+    for n in lines:
+        v_parts[n] = vecs.summed(n)
+    vec_line.begin()
+    matrix.stage_c(lines[-1])
+    mats_sum[...] = mats.result()
+    out_sum[...] = outs.result()
+    vec_sum[...] = vec_line.result()
     matrix.result(sum_ref)
-    vec_sum[...] = vecs.result()
 
     @pl.when(mine)
     def _():
@@ -1221,11 +1260,13 @@
         handed.wait()
 
     trade.wait_send()
-    matrix.sent_all()
-    vecs.sent_all()
-
-
-def update(n_dp, batch, ht, ht_other, dpre, dpre_other, weight, base, spread, outer, vectors, dvec):
+    for fold in (matrix, vecs, vec_line, mats, outs):
+        fold.sent_all()
+
+
+def update(
+    n_dp, batch, ht, ht_other, dpre, dpre_other, weight, base, spread, outer, vectors, dvec, mats_part, out_part
+):
     rows, width = base.shape
     steps = rows // ROWS
     low, f32 = jnp.bfloat16, jnp.float32
@@ -1239,9 +1280,11 @@
             jax.ShapeDtypeStruct((block_rows, 4 * width), f32),
             jax.ShapeDtypeStruct((batch, steps, width), f32),
             jax.ShapeDtypeStruct((8, LANES), f32),
+            jax.ShapeDtypeStruct(mats_part.shape[1:], f32),
+            jax.ShapeDtypeStruct(out_part.shape[1:], f32),
         ),
-        in_specs=[VMEM_SPEC] * 4 + [ANY_SPEC] + [VMEM_SPEC] * 5,
-        out_specs=(VMEM_SPEC, ANY_SPEC, VMEM_SPEC),
+        in_specs=[VMEM_SPEC] * 4 + [ANY_SPEC] + [VMEM_SPEC] * 7,
+        out_specs=(VMEM_SPEC, ANY_SPEC, VMEM_SPEC, VMEM_SPEC, VMEM_SPEC),
         scratch_shapes=[
             pltpu.VMEM((width, 4 * width), low),
             pltpu.VMEM((rows, width), f32),
@@ -1251,15 +1294,22 @@
             pltpu.VMEM((n_dp, 8, LANES), f32),
         ]
         + fold_buffers(line, side, block, low)
-        + [pltpu.VMEM((2, line) + block, low)]
         + fold_buffers(line, side, (8, LANES), f32)
-        + [pltpu.VMEM((line - 1, 8, LANES), f32)]
+        + [
+            pltpu.VMEM((side - 1, line) + block, low),
+            pltpu.VMEM((2, line // 2) + block, low),
+            pltpu.VMEM((side - 1, line, 8, LANES), f32),
+            pltpu.VMEM((line, 8, LANES), f32),
+            pltpu.VMEM((line - 1, 8, LANES), f32),
+            pltpu.VMEM((line - 1,) + mats_part.shape[1:], low),
+            pltpu.VMEM((line - 1,) + out_part.shape[1:], low),
+        ]
         + [dma, dma((3,)), dma((2,))]
-        + [fold_sems(line, side)] * 2,
+        + [fold_sems(line, side)] * 4,
         compiler_params=pltpu.CompilerParams(
             collective_id=3, has_side_effects=True, vmem_limit_bytes=VMEM_LIMIT
         ),
-    )(ht, ht_other, dpre, dpre_other, weight, base, spread, outer, vectors, dvec)
+    )(ht, ht_other, dpre, dpre_other, weight, base, spread, outer, vectors, dvec, mats_part, out_part)
 
 
 STEP = 5
@@ -1384,7 +1434,7 @@
     out_block = jnp.pad(out_copy, ((0, 0), (0, vocab_pad - vocab_half)))
     piece = vec_master.shape[1]
     vec_block = jnp.pad(vec_master.astype(low).astype(f32), ((0, 0), (0, LANES - piece)))
-    act, cell, h_rows, x_rows, vectors, weight, mats_full, out_full = forward(
+    act, cell, h_rows, x_rows, vectors, weight, weight_t, mats_full, out_full = forward(
         n_dp, base, lstm_copy[0], mats_block, out_block, vec_block
     )
     mats_full = mats_full.reshape(3, 2 * model_width, model_width)
@@ -1409,10 +1459,9 @@
 
     outer = from_halves(dmem, ddec.astype(low)).reshape(batch_size, length, model_width)
     outer = slot_major(outer).astype(f32)
-    weight_t = jnp.swapaxes(weight[model_width:], 0, 1)
     h_before = jnp.concatenate([jnp.zeros_like(h_rows[:ROWS]), h_rows[:-ROWS]], 0)
     ht = jnp.concatenate([x_rows.T, h_before.T], 0)
-    dpre, dpre_other, ht_other, mats_sum, out_sum = backward(
+    dpre, dpre_other, ht_other, mats_part, out_part = backward(
         n_dp, act, cell, outer, weight_t, ht, (dq, dk, decoded, memory, context, dz, squashed, grad_logits)
     )
     logit_row = jnp.concatenate(
@@ -1424,8 +1473,21 @@
         ]
     )
     vec_rows = vec_rows + jnp.pad(logit_row[None], ((7, 0), (0, 0)))
-    lstm_sum, inputs_grad, vec_sum = update(
-        n_dp, batch_size, ht, ht_other, dpre, dpre_other, weight, base, spread, outer, vectors, vec_rows
+    lstm_sum, inputs_grad, vec_sum, mats_sum, out_sum = update(
+        n_dp,
+        batch_size,
+        ht,
+        ht_other,
+        dpre,
+        dpre_other,
+        weight,
+        base,
+        spread,
+        outer,
+        vectors,
+        vec_rows,
+        mats_part,
+        out_part,
     )
     mats_sum = jnp.swapaxes(mats_sum.reshape(3, -1, model_width), 1, 2)
     lstm_new, lstm_first_new, lstm_second_new = adamw(

time: 587 us -> 486 us (0.83); the launches traced: 579 us -> 485 us
  Pallas kernels: 492 us -> 429 us
  local copies, waits for them, and re-layouts: 41 us -> 10.6 us
    pallas_call x1, Pallas kernels: 134 us -> 91.8 us  [backward(): pl.pallas_call(functools.partial(backward_kernel, n_dp), out_shape=(jax.S...]
    pallas_call x1, Pallas kernels: 126 us -> 104 us  [update(): pl.pallas_call(functools.partial(update_kernel, n_dp, batch), out_shape=(...]
    pallas_call x3 -> x2, local copies, waits for them, and re-layouts: 24.4 us -> 1.84 us  [forward(): pl.pallas_call(functools.partial(forward_kernel, n_dp), out_shape=(jax.Sh...]
    transpose x1 -> x0, local copies, waits for them, and re-layouts: 7.66 us -> none  [local(): weight_t = jnp.swapaxes(weight[model_width:], 0, 1)]
  transfers between devices with their start and end apart: 8 -> 8, of which waited for: 1 -> 2; matrix products, arithmetic and copies ran while one was open for 8% -> 3% of each run, Pallas kernels for 0% -> 0%
where the time goes in v3:
time: 486 us; the launch traced here: 485 us
  Pallas kernels  429 us (88%)
  other arithmetic  27.9 us (6%)
  starting transfers between devices  10.8 us (2%)
  local copies, waits for them, and re-layouts  10.6 us (2%)
  waiting for transfers between devices  4.97 us (1%)
    pallas_call x1, Pallas kernels, forward(): pl.pallas_call(functools.partial(forward_kernel, n_dp), out_shape=(jax.Sh...  173 us
    pallas_call x1, Pallas kernels, update(): pl.pallas_call(functools.partial(update_kernel, n_dp, batch), out_shape=(...  104 us
    pallas_call x1, Pallas kernels, backward(): pl.pallas_call(functools.partial(backward_kernel, n_dp), out_shape=(jax.S...  91.8 us
    pallas_call x1, Pallas kernels, attention(): pl.pallas_call(attention_kernel, out_shape=(jax.ShapeDtypeStruct((rows, w...  61.1 us
  transfers between devices with their start and end apart: 8, of which 2 were waited for; matrix products, arithmetic and copies ran while one was open for 3% of the time, Pallas kernels for 0%

profile of v3, /device:TPU:0, one launch (start us, length us, event | category | flops | bytes accessed | tf_op | source)
XLA Modules:
  0.0 484.5 jit_solution(925084826503500380)
XLA Ops:
  0.7 0.8 collective-permute-start.1
  1.5 1.0 broadcast_select_fusion.8
  2.5 4.4 collective-permute-start.4
  6.9 0.8 fusion.14
  9.0 1.5 pad.35.out_ref
  10.5 0.8 broadcast_select_fusion.12
  12.1 1.0 select_bitcast_fusion.2
  15.6 1.3 pad.34.clone
  16.8 172.7 %shard_map.305 = (f32[384,4096]{1,0:T(8,128)}, f32[400,1024]{1,0:T(8,128)}, bf16[384,1024]{1,0:T(8,128)(2,1)}, bf16[384,1024]{1,0:T(8,128)(2,1)}, f32[8,2048]{1,...) custom-call(f32[384,1024]{1,0:T(8,128)} %bitcast.67, ...), custom_call_target="tpu_custom_call" | custom-call | tf_op jit(solution)/shard_map/pallas_call | solution.py:710
  189.5 0.9 fusion.23
  190.4 1.5 copy.53
  192.4 0.8 broadcast_select_fusion.3
  193.7 0.8 collective-permute-start.3
  196.0 0.8 reshape.146.spread_ref
  196.8 1.3 pad_maximum_fusion.ht_ref
  198.1 2.0 collective-permute-done.2
  200.1 0.9 broadcast_select_fusion.5
  200.9 61.1 %shard_map.306 = (bf16[144,1024]{1,0:T(8,128)(2,1)}, bf16[144,1024]{1,0:T(8,128)(2,1)}, bf16[144,1024]{1,0:T(8,128)(2,1)}, bf16[2,144,1024]{2,1,0:T(8,128)(2,1)}...) custom-call(s32[6]{0:T(128)} %copy-done.17, ...), custom_call_target="tpu_custom_call" | custom-call | tf_op jit(solution)/shard_map/pallas_call | solution.py:279
  262.0 0.8 fusion.24
  262.8 1.2 broadcast_select_fusion.2
  264.7 3.2 collective-permute-start.7
  267.9 1.0 select_bitcast_fusion
  269.2 1.5 pad_add_fusion.dvec_ref
  271.5 3.0 collective-permute-done.7
  275.1 1.4 bitcast_convert_fusion.outer_ref
  276.5 91.8 %shard_map.307 = (bf16[384,4096]{1,0:T(8,128)(2,1)}, bf16[384,2048]{1,0:T(8,128)(2,1)}, bf16[2048,384]{1,0:T(8,128)(2,1)}, bf16[4,192,1024]{2,1,0:T(8,128)(2,1)}, bf16[4,64,512]{2,1,0:T(8,128)(2,1)}) custom-call(f32[384,4096]{1,0:T(8,128)} %get-tuple-element.52.act_ref, f32[400,1024]{1,0:T(8,128)} %get-tuple-element.53.cell_ref, ...), custom_call_target="tpu_custom_call" | custom-call | tf_op jit(solution)/shard_map/pallas_call | solution.py:1078
  368.3 103.6 %shard_map.308 = (f32[128,4096]{1,0:T(8,128)}, f32[12,24,1024]{2,1,0:T(8,128)}, f32[8,128]{1,0:T(8,128)}, f32[192,1024]{1,0:T(8,128)}, f32[64,512]{1,0:T(8,128)}) custom-call(bf16[2048,384]{1,0:T(8,128)(2,1)} %pad_maximum_fusion.ht_ref, bf16[2048,384]{1,0:T(8,128)(2,1)} %get-tuple-element.62.ht_other, bf16[384,4096]{1,0:T(8,128)(2,1)} %get-tuple-element.63.dpre_ref, ...), custom_call_target="tpu_custom_call" | custom-call | tf_op jit(solution)/shard_map/pallas_call | solution.py:1277
  471.9 1.3 multiply_subtract_fusion.3
  473.2 7.3 %fusion.21 = (bf16[1,128,4096]{2,1,0:T(8,128)(2,1)}, f32[1,128,4096]{2,1,0:T(8,128)}, f32[1,128,4096]{2,1,0:T(8,128)}, f32[1,128,4096]{2,1,0:T(8,128)}) fusion(f32[1,128,4096]{2,1,0:T(8,128)S(1)} %copy-done.1, f32[128,4096]{1,0:T(8,128)} %get-tuple-element.71, f32[1,128,4096]{2,1,0:T(8,128)} %param.23, f32[1,128,4096]{2,1,0:T(8,128)} %param.24), kind=kLoop, calls=%fused_computation.67 | loop fusion | flops 8388608 | bytes 15728640 | tf_op jit(solution)/shard_map/convert_element_type | solution.py:1511
  480.5 2.0 fusion.19
  482.5 0.8 fusion.17
  483.3 1.0 copy.64
  (73 shorter events, 9.3 us)
Async XLA Ops:
  0.7 13.3 %copy-start.9 = (bf16[1,12,24,1024]{3,2,1,0:T(8,128)(2,1)S(1)}, bf16[1,12,24,1024]{3,2,1,0:T(8,128)(2,1)}, u32[]{:S(2)}) copy-start(bf16[1,12,24,1024]{3,2,1,0:T(8,128)(2,1)} %param.18) | copy-start | bytes 1769476
  0.7 13.3 %collective-permute-start.1 = (bf16[12,24,1024]{2,1,0:T(8,128)(2,1)}, bf16[12,24,1024]{2,1,0:T(8,128)(2,1)S(1)}, u32[]{:S(2)}, u32[]{:S(2)}) collective-permute-start(bf16[12,24,1024]{2,1,0:T(8,128)(2,1)} %bitcast.87), channel_id=1, source_target_pairs={{4,16},{5,17},{6,18},{7,19},{12,24},{13,25},{14,26},{15,27},{16,4}... | collective-permute-start | bytes 1769480 | tf_op jit(solution)/shard_map/ppermute | solution.py:1419
  2.5 9.6 %collective-permute-start.4 = (bf16[6,24,500]{2,1,0:T(8,128)(2,1)S(1)}, bf16[6,24,500]{2,1,0:T(8,128)(2,1)S(1)}, u32[]{:S(2)}, u32[]{:S(2)}) collective-permute-start(bf16[6,24,500]{2,1,0:T(8,128)(2,1)S(1)} %broadcast_select_fusion.8), channel_id=1, source_target_pairs={{0,16},{16,0},{1,17},{17,1},{2,18},{18,2},{3,19},{19,3},{4,20},{20... | collective-permute-start | bytes 432008 | tf_op jit(solution)/shard_map/ppermute | solution.py:1328
  7.7 2.8 collective-permute-start
  11.3 3.2 copy-start.17
  189.5 2.4 copy-start
  191.9 3.6 copy-start.4
  193.1 6.9 %collective-permute-start.2 = (bf16[6,24,1024]{2,1,0:T(8,128)(2,1)}, bf16[6,24,1024]{2,1,0:T(8,128)(2,1)S(1)}, u32[]{:S(2)}, u32[]{:S(2)}) collective-permute-start(bf16[6,24,1024]{2,1,0:T(8,128)(2,1)} %get-tuple-element.97), channel_id=1, source_target_pairs={{0,16},{1,17},{2,18},{3,19},{16,20},{17,21},{18,22},{19,23},{8,24}... | collective-permute-start | bytes 884744 | tf_op jit(solution)/shard_map/ppermute | solution.py:1405
  193.7 6.4 %collective-permute-start.3 = (bf16[6,24,1024]{2,1,0:T(8,128)(2,1)S(1)}, bf16[6,24,1024]{2,1,0:T(8,128)(2,1)S(1)}, u32[]{:S(2)}, u32[]{:S(2)}) collective-permute-start(bf16[6,24,1024]{2,1,0:T(8,128)(2,1)S(1)} %get-tuple-element.96), channel_id=1, source_target_pairs={{0,0},{1,1},{2,2},{3,3},{16,4},{17,5},{18,6},{19,7},{8,8},{9,9},{1... | collective-permute-start | bytes 884744 | tf_op jit(solution)/shard_map/ppermute | solution.py:1404
  262.0 8.7 %copy-start.3 = (bf16[2,144,512]{2,1,0:T(8,128)(2,1)S(1)}, bf16[2,144,512]{2,1,0:T(8,128)(2,1)}, u32[]{:S(2)}) copy-start(bf16[2,144,512]{2,1,0:T(8,128)(2,1)} %get-tuple-element.50) | copy-start | bytes 884740
  264.0 7.5 %collective-permute-start.6 = (bf16[144,1024]{1,0:T(8,128)(2,1)S(1)}, bf16[144,1024]{1,0:T(8,128)(2,1)S(1)}, u32[]{:S(2)}, u32[]{:S(2)}) collective-permute-start(bf16[144,1024]{1,0:T(8,128)(2,1)S(1)} %get-tuple-element.92), channel_id=1, source_target_pairs={{0,0},{1,1},{2,2},{3,3},{4,16},{5,17},{6,18},{7,19},{8,8},{9,9},{1... | collective-permute-start | bytes 884744 | tf_op jit(solution)/shard_map/ppermute | solution.py:1409
  264.7 9.7 %collective-permute-start.7 = (bf16[144,1024]{1,0:T(8,128)(2,1)S(1)}, bf16[144,1024]{1,0:T(8,128)(2,1)S(1)}, u32[]{:S(2)}, u32[]{:S(2)}) collective-permute-start(bf16[144,1024]{1,0:T(8,128)(2,1)S(1)} %get-tuple-element.93), channel_id=1, source_target_pairs={{16,0},{17,1},{18,2},{19,3},{20,16},{21,17},{22,18},{23,19},{24,8}... | collective-permute-start | bytes 884744 | tf_op jit(solution)/shard_map/ppermute | solution.py:1412
  268.9 1.8 collective-permute-start.5
  368.2 103.6 %copy-start.14 = (f32[8,64]{1,0:T(8,128)S(1)}, f32[8,64]{1,0:T(8,128)}, u32[]{:S(2)}) copy-start(f32[8,64]{1,0:T(8,128)} %param.33) | copy-start | bytes 6148
  368.2 103.6 %copy-start.15 = (f32[8,64]{1,0:T(8,128)S(1)}, f32[8,64]{1,0:T(8,128)}, u32[]{:S(2)}) copy-start(f32[8,64]{1,0:T(8,128)} %param.34) | copy-start | bytes 6148
  368.3 103.6 %copy-start.16 = (f32[8,64]{1,0:T(8,128)S(1)}, f32[8,64]{1,0:T(8,128)}, u32[]{:S(2)}) copy-start(f32[8,64]{1,0:T(8,128)} %param.35) | copy-start | bytes 6148
  368.3 104.9 %copy-start.1 = (f32[1,128,4096]{2,1,0:T(8,128)S(1)}, f32[1,128,4096]{2,1,0:T(8,128)}, u32[]{:S(2)}) copy-start(f32[1,128,4096]{2,1,0:T(8,128)} %param.21) | copy-start | bytes 6291460
  473.2 7.3 %copy-start.5 = (f32[3,1024,64]{1,2,0:T(8,128)S(1)}, f32[3,1024,64]{1,2,0:T(8,128)}, u32[]{:S(2)}) copy-start(f32[3,1024,64]{1,2,0:T(8,128)} %param.25) | copy-start | bytes 2359300
  473.2 7.3 %copy-start.6 = (f32[3,1024,64]{1,2,0:T(8,128)S(1)}, f32[3,1024,64]{1,2,0:T(8,128)}, u32[]{:S(2)}) copy-start(f32[3,1024,64]{1,2,0:T(8,128)} %param.27) | copy-start | bytes 2359300
  473.2 7.3 %copy-start.7 = (f32[3,1024,64]{1,2,0:T(8,128)S(1)}, f32[3,1024,64]{1,2,0:T(8,128)}, u32[]{:S(2)}) copy-start(f32[3,1024,64]{1,2,0:T(8,128)} %param.28) | copy-start | bytes 2359300
  473.2 7.3 %copy-start.8 = (f32[192,1024]{1,0:T(8,128)S(1)}, f32[192,1024]{1,0:T(8,128)}, u32[]{:S(2)}) copy-start(f32[192,1024]{1,0:T(8,128)} %get-tuple-element.72) | copy-start | bytes 2359300
  480.5 2.0 copy-start.10
  480.5 2.0 copy-start.11
  480.5 2.0 copy-start.12
  480.5 2.0 copy-start.13
  480.5 2.8 copy-start.2

commit v4 on v3

v4 whole, which is shorter than its diff:
```python
import functools
import jax
import jax.numpy as jnp
from jax import lax
from jax.experimental import pallas as pl
from jax.experimental.pallas import tpu as pltpu
from jax.sharding import PartitionSpec as P

ROWS = 16
LANES = 128
UNROLL = 8
ENERGY_OFFSET = -4.0
NORM_EPS = 1e-05
VMEM_SPEC = pl.BlockSpec(memory_space=pltpu.VMEM)
SMEM_SPEC = pl.BlockSpec(memory_space=pltpu.SMEM)
VMEM_LIMIT = 60 * 1024 * 1024


def contract(left, right, left_dim, right_dim):
    return lax.dot_general(
        left, right, (((left_dim,), (right_dim,)), ((), ())), preferred_element_type=jnp.float32
    )


MESH_ID = pl.DeviceIdType.MESH
ANY_SPEC = pl.BlockSpec(memory_space=pl.ANY)
DP_LAYOUTS = {16: (4, 2, 1, 2), 128: (8, 4, 1, 32)}
LINE_STRIDE = 4
TURN = 256
CHUNKS = 2


def flipped(value, k):
    result = value
    bit = 1
    while bit <= k:
        if k & bit:
            result = result + bit - 2 * bit * lax.rem(value // bit, 2)
        bit *= 2
    return result


class Place:
    def __init__(self, n_dp):
        self.line, self.side, stride_a, stride_b = DP_LAYOUTS[n_dp]
        self.core = lax.axis_index("section")
        self.chip = lax.axis_index("dp")
        self.z = lax.rem(self.chip // LINE_STRIDE, self.line)
        at_a = lax.rem(self.chip // stride_a, self.side)
        at_b = lax.rem(self.chip // stride_b, self.side)
        self.role = lax.rem(self.z, 2)
        moves_a = [(flipped(at_a, k) - at_a) * stride_a for k in range(self.side)]
        moves_b = [(flipped(at_b, k) - at_b) * stride_b for k in range(self.side)]
        core = self.core
        self.first = [a + (b - a) * core for a, b in zip(moves_a, moves_b)]
        self.second = [b + (a - b) * core for a, b in zip(moves_a, moves_b)]
        self.along = [(flipped(self.z, k) - self.z) * LINE_STRIDE for k in range(self.line)]

    def block(self, kz, kf=0, kg=0):
        return self.chip + self.along[kz] + self.first[kf] + self.second[kg]

    def other_block(self, kz, kf=0, kg=0):
        return self.chip + self.along[kz] + self.second[kf] + self.first[kg]

    def greet(self):
        barrier = pltpu.get_barrier_semaphore()
        peers = [(1 - self.core, self.chip)]
        for k in range(1, self.line):
            peers += [(0, self.chip + self.along[k]), (1, self.chip + self.along[k])]
        for k in range(1, self.side):
            peers += [(self.core, self.chip + self.first[k]), (self.core, self.chip + self.second[k])]
        for peer in peers:
            pl.semaphore_signal(barrier, inc=1, device_id=peer, device_id_type=MESH_ID)
        pl.semaphore_wait(barrier, len(peers))


def remote(source, target, send, receive, device):
    return pltpu.make_async_remote_copy(
        src_ref=source,
        dst_ref=target,
        send_sem=send,
        recv_sem=receive,
        device_id=device,
        device_id_type=MESH_ID,
    )


class Spread:
    def __init__(self, place, here, there, sems):
        self.place, self.here, self.there, self.sems = place, here, there, sems
        self.sent = []

    def send(self, target, device, send, receive):
        copy = remote(target, target, send, receive, device)
        copy.start()
        self.sent.append(copy)

    def arrived(self, target, semaphore):
        place = self.place
        remote(target, target, semaphore, semaphore, (1 - place.core, place.chip)).wait_recv()

    def to_second(self, kz, kf):
        place = self.place
        target = self.here(place.block(kz, kf))
        for kg in range(1, place.side):
            self.send(
                target,
                (place.core, place.chip + place.second[kg]),
                self.sems["gs"].at[kg, kf, kz],
                self.sems["gr"].at[kg, kf, kz],
            )

    def to_core(self, kz, kf, kg):
        place = self.place
        self.send(
            self.here(place.block(kz, kf, kg)),
            (1 - place.core, place.chip),
            self.sems["cs"].at[kg, kf, kz],
            self.sems["cr"].at[kg, kf, kz],
        )

    def stage_one(self, *steps):
        place = self.place
        for kz in steps or range(place.line):
            self.wait_line(kz)
            target = self.here(place.block(kz))
            for kf in range(1, place.side):
                self.send(
                    target,
                    (place.core, place.chip + place.first[kf]),
                    self.sems["fs"].at[kf, kz],
                    self.sems["fr"].at[kf, kz],
                )
            self.to_second(kz, 0)
            self.to_core(kz, 0, 0)

    def stage_two(self):
        place = self.place
        for kf in range(1, place.side):
            for kz in range(place.line):
                self.arrived(self.here(place.block(kz, kf)), self.sems["fr"].at[kf, kz])
                self.to_second(kz, kf)
                self.to_core(kz, kf, 0)

    def stage_three(self):
        place = self.place
        for kg in range(1, place.side):
            for kf in range(place.side):
                for kz in range(place.line):
                    self.arrived(self.here(place.block(kz, kf, kg)), self.sems["gr"].at[kg, kf, kz])
                    self.to_core(kz, kf, kg)

    def finish(self):
        place = self.place
        for kg in range(place.side):
            for kf in range(place.side):
                for kz in range(place.line):
                    self.arrived(self.there(place.other_block(kz, kf, kg)), self.sems["cr"].at[kg, kf, kz])

    def sent_all(self):
        for copy in self.sent:
            copy.wait_send()


def spread_sems(line, side):
    dma = pltpu.SemaphoreType.DMA
    return {
        "zs": dma((line, 2)),
        "zr": dma((line,)),
        "fs": dma((side, line)),
        "fr": dma((side, line)),
        "gs": dma((side, side, line)),
        "gr": dma((side, side, line)),
        "cs": dma((side, side, line)),
        "cr": dma((side, side, line)),
    }


def spread_even(place, source, at, sems):
    own = at(place.core, place.chip)
    spread = Spread(place, lambda block: at(place.core, block), lambda block: at(1 - place.core, block), sems)
    kept = pltpu.make_async_copy(source, own, sems["zr"].at[0])
    copies = [
        remote(source, own, sems["zs"].at[k, 0], sems["zr"].at[k], (place.core, place.chip + place.along[k]))
        for k in range(1, place.line)
    ]

    def begin():
        kept.start()
        for copy in copies:
            copy.start()
        spread.sent += copies

    def wait_line(kz):
        if kz == 0:
            kept.wait()
        else:
            spread.arrived(spread.here(place.block(kz)), sems["zr"].at[kz])

    spread.begin = begin
    spread.wait_line = wait_line
    return spread


class LineGather:
    def __init__(self, place, source, target, sems):
        self.kept = pltpu.make_async_copy(source, target.at[0], sems["zr"].at[0])
        self.copies = [
            remote(source, target.at[k], sems["zs"].at[k, 0], sems["zr"].at[k], (place.core, place.chip + place.along[k]))
            for k in range(1, place.line)
        ]

    def begin(self):
        for copy in [self.kept] + self.copies:
            copy.start()

    def finish(self):
        for copy in [self.kept] + self.copies:
            copy.wait()


def spread_line(place, source, target, sems):
    spread = Spread(
        place,
        lambda block: target.at[place.core, block],
        lambda block: target.at[1 - place.core, block],
        sems,
    )
    kept = [
        pltpu.make_async_copy(source.at[kz], spread.here(place.block(kz)), sems["zr"].at[kz])
        for kz in range(place.line)
    ]

    def begin():
        for copy in kept:
            copy.start()

    spread.begin = begin
    spread.wait_line = lambda kz: kept[kz].wait()
    return spread


def spread_role(place, source, target, sems, rows, half, first, count):
    source = source.at[first : first + count]

    def columns(core):
        return pl.ds(pl.multiple_of(core * half, half), half)

    def at(block, core):
        return target.at[pl.ds(pl.multiple_of(block * rows + first, count), count), columns(core)]

    spread = Spread(
        place, lambda block: at(block, place.core), lambda block: at(block, 1 - place.core), sems
    )
    mine = place.role == place.core
    kept = pltpu.make_async_copy(source.at[:, columns(place.core)], at(place.chip, place.core), sems["zr"].at[0])
    cross = remote(
        source.at[:, columns(1 - place.core)],
        at(place.chip, 1 - place.core),
        sems["zs"].at[0, 0],
        sems["zr"].at[0],
        (1 - place.core, place.chip),
    )
    copies = [
        [
            remote(
                source.at[:, columns(core)],
                at(place.chip, core),
                sems["zs"].at[k, core],
                sems["zr"].at[k],
                (core, place.chip + place.along[k]),
            )
            for core in range(2)
        ]
        for k in range(1, place.line)
    ]

    guest = jnp.logical_not(mine)

    def each(condition, steps, action):
        @pl.when(condition)
        def _():
            for k in steps:
                for copy in copies[k - 1] if k else [cross]:
                    action(copy)

    def start(copy):
        copy.start()

    def begin():
        @pl.when(mine)
        def _():
            kept.start()

        each(mine, range(0, place.line, 2), start)
        each(guest, range(1, place.line, 2), start)

    def wait_line(kz):
        if kz == 0:

            @pl.when(mine)
            def _():
                kept.wait()

            @pl.when(jnp.logical_not(mine))
            def _():
                spread.arrived(spread.here(place.chip), sems["zr"].at[0])

        else:
            spread.arrived(spread.here(place.block(kz)), sems["zr"].at[kz])

    def finished(copy):
        copy.wait_send()

    def sent_line():
        each(mine, range(0, place.line, 2), finished)
        each(guest, range(1, place.line, 2), finished)

    spread.begin = begin
    spread.wait_line = wait_line
    spread.sent_line = sent_line
    return spread


def forward_kernel(
    n_dp,
    seq_ref,
    shard_ref,
    mats_ref,
    out_ref,
    vec_ref,
    act_ref,
    cell_ref,
    ht_ref,
    base_ref,
    spread_ref,
    vectors_ref,
    pair_ref,
    w_out,
    wt_out,
    mats_out,
    mats_line,
    out_line,
    seq_s,
    result_s,
    x_s,
    h_s,
    w_s,
    wt_s,
    vec_s,
    state,
    keep_sem,
    seq_sem,
    pair_sem,
    sems_m,
    sems_v,
    sems_n,
    sems_o,
    *sems_w,
):
    batch, steps, width = seq_ref.shape
    low, f32 = jnp.bfloat16, jnp.float32
    place = Place(n_dp)
    core, chip = place.core, place.chip
    mine = core == place.role
    guest = jnp.logical_not(mine)
    encoder = place.role == 0
    place.greet()
    rows = shard_ref.shape[0]
    count = max(ROWS, rows // CHUNKS)
    matrix = [
        spread_role(place, shard_ref, w_s, sems, rows, 2 * width, n * count, count)
        for n, sems in zip(range(rows // count), sems_w)
    ]
    mats = spread_even(place, mats_ref.at[:2], lambda core, chip: mats_out.at[:, core, chip], sems_m)
    vecs = spread_even(place, vec_ref, lambda core, chip: vec_s.at[core, chip], sems_v)
    thirds = LineGather(place, mats_ref.at[2], mats_line, sems_n)
    outs = LineGather(place, out_ref, out_line, sems_o)
    vecs.begin()
    for part in matrix:
        part.begin()
    seq_kept = pltpu.make_async_copy(seq_ref, seq_s, seq_sem.at[0])
    seq_away = remote(seq_ref, seq_s, seq_sem.at[1], seq_sem.at[2], (1 - core, chip + place.along[1]))
    pl.when(mine)(seq_kept.start)
    pl.when(guest)(seq_away.start)
    for part in matrix:
        part.stage_one(0)
    state[...] = jnp.zeros_like(state)
    cell_ref[:ROWS] = jnp.zeros((ROWS, width), f32)
    base_ref[:, batch:] = jnp.zeros((steps, ROWS - batch, width), f32)
    spread_ref[...] = jnp.zeros_like(spread_ref)
    pl.when(mine)(seq_kept.wait)
    pl.when(guest)(seq_away.wait)
    for u in range(batch):
        raw = seq_s[u].astype(f32)
        center = raw - jnp.mean(raw, -1, keepdims=True)
        spread = lax.rsqrt(jnp.mean(center * center, -1, keepdims=True) + NORM_EPS)
        base_ref[:, u, :] = jnp.where(encoder, center * spread, raw)
        spread_ref[:, u, :] = jnp.broadcast_to(spread, (steps, LANES))
    line_rest = range(1, place.line)
    for n in range(len(matrix) + 2):
        if n < len(matrix):
            matrix[n].stage_one(*line_rest)
        if n == 0:
            vecs.stage_one()
        if n == len(matrix) - 1:
            mats.begin()
            thirds.begin()
            outs.begin()
        if 1 <= n <= len(matrix):
            matrix[n - 1].stage_two()
        if n == 1:
            vecs.stage_two()
        if n >= 2:
            matrix[n - 2].stage_three()
    mats.stage_one(0)
    vecs.stage_three()
    vecs.finish()
    piece = 2 * width // (2 * n_dp)
    per_tile = LANES // piece
    for m in range(2 * width // LANES):
        tile = jnp.zeros((8, LANES), f32)
        for k in range(per_tile):
            index = m * per_tile + k
            block = vec_s[index // n_dp, index % n_dp]
            tile = tile + (pltpu.roll(block, k * piece, 1) if k else block)
        vectors_ref[:, m * LANES : (m + 1) * LANES] = tile
    gain = jnp.where(encoder, vectors_ref[4:5, :width], 1.0)
    shift = jnp.where(encoder, vectors_ref[4:5, width:], 0.0)
    x_s[...] = (base_ref[...].reshape(steps * ROWS, width) * gain + shift).astype(low)
    ht_ref[:width] = x_s[...].T
    for part in matrix:
        part.finish()
    keep = pltpu.make_async_copy(w_s.at[:width], w_out, keep_sem.at[0])
    keep.start()
    for q in range(4):
        columns = slice(q * width, (q + 1) * width)
        row = q // 2
        bias_columns = slice((q % 2) * width, (q % 2 + 1) * width)
        bias = jnp.where(
            encoder, vectors_ref[row : row + 1, bias_columns], vectors_ref[row + 2 : row + 3, bias_columns]
        )
        act_ref[:, columns] = jnp.dot(x_s[...], w_s[:width, columns], preferred_element_type=f32) + bias

    def step(t, carry):
        rows = pl.ds(pl.multiple_of(t * ROWS, ROWS), ROWS)
        after = pl.ds(pl.multiple_of((t + 1) * ROWS, ROWS), ROWS)
        hidden = state[...]

        def gate(q):
            columns = slice(q * width, (q + 1) * width)
            return act_ref[rows, columns] + jnp.dot(hidden, w_s[width:, columns], preferred_element_type=f32)

        in_gate = jax.nn.sigmoid(gate(0))
        forget = jax.nn.sigmoid(gate(1))
        candidate = jnp.tanh(gate(2))
        cell = forget * cell_ref[rows] + in_gate * candidate
        out_gate = jax.nn.sigmoid(gate(3))
        hidden_new = (out_gate * jnp.tanh(cell)).astype(low)
        act_ref[rows, :width] = in_gate
        act_ref[rows, width : 2 * width] = forget
        act_ref[rows, 2 * width : 3 * width] = candidate
        act_ref[rows, 3 * width :] = out_gate
        cell_ref[after] = cell
        h_s[after] = hidden_new
        state[...] = hidden_new
        return carry

    h_s[:ROWS] = jnp.zeros((ROWS, width), low)
    marks = [steps * n // 24 for n in (0, 4, 14, 24)]
    lax.fori_loop(marks[0], marks[1], step, 0)
    mats.stage_one(*line_rest)
    lax.fori_loop(marks[1], marks[2], step, 0)
    mats.stage_two()
    lax.fori_loop(marks[2], marks[3], step, 0)
    turned = h_s[ROWS:].astype(f32).reshape(steps, ROWS, width)
    for u in range(batch):
        value = turned[:, u, :]
        result_s[u] = jnp.where(encoder, seq_s[u].astype(f32) + value, value).astype(low)
    half = batch // 2
    for h in range(2):
        home = jnp.logical_and(mine, core == h)
        source, target = result_s.at[h * half : (h + 1) * half], pair_ref.at[place.role]
        stay = pltpu.make_async_copy(source, target, pair_sem.at[0, h])
        leave = remote(
            source,
            target,
            pair_sem.at[0, h],
            pair_sem.at[1, place.role],
            (h, jnp.where(mine, chip, chip + place.along[1])),
        )
        pl.when(home)(stay.start)
        pl.when(jnp.logical_not(home))(leave.start)
    for q in range(4):
        for n in range(width // TURN):
            rows = slice(width + n * TURN, width + (n + 1) * TURN)
            wt_s[q, :, n * TURN : (n + 1) * TURN] = w_s[rows, q * width : (q + 1) * width].T
    keep_turned = pltpu.make_async_copy(wt_s, wt_out, keep_sem.at[1])
    keep_turned.start()
    ht_ref[width:] = h_s[:-ROWS].T
    mats.stage_three()
    mats.finish()
    thirds.finish()
    outs.finish()
    for h in range(2):
        home = jnp.logical_and(mine, core == h)
        source, target = result_s.at[h * half : (h + 1) * half], pair_ref.at[place.role]
        stay = pltpu.make_async_copy(source, target, pair_sem.at[0, h])
        leave = remote(
            source,
            target,
            pair_sem.at[0, h],
            pair_sem.at[1, place.role],
            (h, jnp.where(mine, chip, chip + place.along[1])),
        )
        pl.when(home)(stay.wait)
        pl.when(jnp.logical_not(home))(leave.wait_send)

    def arrived(section):
        target = pair_ref.at[section]
        remote(target, target, pair_sem.at[0, 0], pair_sem.at[1, section], (1 - core, chip)).wait_recv()

    pl.when(guest)(lambda: arrived(place.role))
    arrived(1 - place.role)
    keep.wait()
    keep_turned.wait()
    for part in matrix:
        part.sent_line()
    for spread in (*matrix, vecs, mats):
        spread.sent_all()


def forward(n_dp, seq, shard, mats_block, out_block, vec_block):
    batch, steps, width = seq.shape
    rows = steps * ROWS
    low, f32 = jnp.bfloat16, jnp.float32
    line, side = DP_LAYOUTS[n_dp][:2]
    columns = mats_block.shape[1]
    dma = pltpu.SemaphoreType.DMA
    return pl.pallas_call(
        functools.partial(forward_kernel, n_dp),
        out_shape=(
            jax.ShapeDtypeStruct((rows, 4 * width), f32),
            jax.ShapeDtypeStruct((rows + ROWS, width), f32),
            jax.ShapeDtypeStruct((2 * width, rows), low),
            jax.ShapeDtypeStruct((steps, ROWS, width), f32),
            jax.ShapeDtypeStruct((steps, ROWS, LANES), f32),
            jax.ShapeDtypeStruct((8, 2 * width), f32),
            jax.ShapeDtypeStruct((2, batch // 2, steps, width), low),
            jax.ShapeDtypeStruct((width, 4 * width), low),
            jax.ShapeDtypeStruct((4, width, width), low),
            jax.ShapeDtypeStruct((2, 2, n_dp, columns, width), low),
            jax.ShapeDtypeStruct((line, columns, width), low),
            jax.ShapeDtypeStruct((line,) + out_block.shape, low),
        ),
        in_specs=[VMEM_SPEC, ANY_SPEC, ANY_SPEC, ANY_SPEC, VMEM_SPEC],
        out_specs=(VMEM_SPEC,) * 7 + (ANY_SPEC,) * 5,
        scratch_shapes=[
            pltpu.VMEM((batch, steps, width), low),
            pltpu.VMEM((batch, steps, width), low),
            pltpu.VMEM((rows, width), low),
            pltpu.VMEM((rows + ROWS, width), low),
            pltpu.VMEM((2 * width, 4 * width), low),
            pltpu.VMEM((4, width, width), low),
            pltpu.VMEM((2, n_dp, 8, LANES), f32),
            pltpu.VMEM((ROWS, width), low),
            dma((2,)),
            dma((3,)),
            dma((2, 2)),
        ]
        + [spread_sems(line, side)] * (4 + CHUNKS),
        compiler_params=pltpu.CompilerParams(
            collective_id=1, has_side_effects=True, vmem_limit_bytes=VMEM_LIMIT
        ),
    )(seq, shard, mats_block, out_block, vec_block)


class Fold:
    def __init__(self, place, part, stage, near, far, sems):
        self.place, self.part, self.stage, self.near, self.far, self.sems = place, part, stage, near, far, sems
        self.sent = []

    def send(self, source, target, device, send, receive):
        copy = remote(source, target, send, receive, device)
        copy.start()
        self.sent.append(copy)

    def arrived(self, target, semaphore):
        place = self.place
        remote(target, target, semaphore, semaphore, (1 - place.core, place.chip)).wait_recv()

    def stage_a(self, *steps):
        place = self.place
        for kz in steps or reversed(range(place.line)):
            for kg in range(1, place.side):
                for kf in reversed(range(place.side)):
                    source = self.stage.at[kg - 1, kf, kz]
                    source[...] = self.part(kz, kf, kg).astype(source.dtype)
                    self.send(
                        source,
                        self.near.at[kg - 1, kf, kz],
                        (place.core, place.chip + place.second[kg]),
                        self.sems["gs"].at[kg, kf, kz],
                        self.sems["gr"].at[kg, kf, kz],
                    )

    def stage_b(self, *steps):
        place = self.place
        for kz in steps or reversed(range(place.line)):
            for kf in reversed(range(place.side)):
                total = self.part(kz, kf, 0)
                for kg in range(1, place.side):
                    self.arrived(self.near.at[kg - 1, kf, kz], self.sems["gr"].at[kg, kf, kz])
                    total = total + self.near[kg - 1, kf, kz].astype(jnp.float32)
                source = self.near.at[0, kf, kz]
                source[...] = total.astype(source.dtype)
                if kf:
                    self.send(
                        source,
                        self.far.at[kf - 1, kz],
                        (place.core, place.chip + place.first[kf]),
                        self.sems["fs"].at[kf, kz],
                        self.sems["fr"].at[kf, kz],
                    )

    def summed(self, kz):
        place = self.place
        total = self.near[0, 0, kz].astype(jnp.float32)
        for kf in range(1, place.side):
            self.arrived(self.far.at[kf - 1, kz], self.sems["fr"].at[kf, kz])
            total = total + self.far[kf - 1, kz].astype(jnp.float32)
        return total.astype(self.far.dtype)

    def sent_all(self):
        for copy in self.sent:
            copy.wait_send()


class FoldLine:
    def __init__(self, place, parts, end, sems):
        self.place, self.parts, self.end, self.sems = place, parts, end, sems

    def begin(self, *steps):
        place = self.place
        for kz in steps or reversed(range(1, place.line)):
            self.copy(kz).start()

    def copy(self, kz):
        place = self.place
        return remote(
            self.parts.at[kz],
            self.end.at[kz - 1],
            self.sems["zs"].at[kz, 0],
            self.sems["zr"].at[kz],
            (place.core, place.chip + place.along[kz]),
        )

    def result(self):
        total = self.parts[0].astype(jnp.float32)
        for kz in range(1, self.place.line):
            self.copy(kz).wait_recv()
            total = total + self.end[kz - 1].astype(jnp.float32)
        return total

    def sent_all(self):
        for kz in range(1, self.place.line):
            self.copy(kz).wait_send()


class FoldRole(Fold):
    def __init__(self, place, part, stage, near, far, end, sems):
        super().__init__(place, part, stage, near, far, sems)
        self.end = end

    def stage_c(self, kz):
        place = self.place
        source = self.far.at[0, kz]
        source[...] = self.summed(kz)
        if kz:
            self.send(
                source,
                self.end.at[place.core, kz // 2],
                (place.role, place.chip + place.along[kz]),
                self.sems["zs"].at[kz, 0],
                self.sems["er"].at[place.core, kz // 2],
            )
        else:
            self.last = source
            self.cross = remote(
                source,
                self.end.at[place.core, 0],
                self.sems["zs"].at[0, 0],
                self.sems["er"].at[place.core, 0],
                (1 - place.core, place.chip),
            )

            @pl.when(place.core != place.role)
            def _():
                self.cross.start()

    def result(self, sum_ref):
        place = self.place
        rows, half = self.end.shape[2:]
        mine = place.core == place.role

        def columns(core):
            return pl.ds(pl.multiple_of(core * half, half), half)

        def add(parity):
            sources = [kz for kz in range(place.line) if kz % 2 == parity]
            for core in range(2):
                total = jnp.zeros((rows, half), jnp.float32)
                for kz in sources:
                    if kz:
                        self.arrived(self.end.at[core, kz // 2], self.sems["er"].at[core, kz // 2])
                        total = total + self.end[core, kz // 2].astype(jnp.float32)
                sum_ref[:, core * half : (core + 1) * half] = total

        @pl.when(mine)
        def _():
            add(0)
            own, other = columns(place.core), columns(1 - place.core)
            sum_ref[:, own] += self.last[...].astype(jnp.float32)
            self.arrived(self.end.at[1 - place.core, 0], self.sems["er"].at[1 - place.core, 0])
            sum_ref[:, other] += self.end[1 - place.core, 0].astype(jnp.float32)

        @pl.when(jnp.logical_not(mine))
        def _():
            add(1)
            self.cross.wait_send()


def fold_sems(line, side):
    dma = pltpu.SemaphoreType.DMA
    return {
        "gs": dma((side, side, line)),
        "gr": dma((side, side, line)),
        "fs": dma((side, line)),
        "fr": dma((side, line)),
        "zs": dma((line, 1)),
        "zr": dma((line,)),
        "er": dma((2, line // 2)),
    }


def fold_buffers(line, side, shape, dtype):
    return [
        pltpu.VMEM((side - 1, side, line) + shape, dtype),
        pltpu.VMEM((side - 1, side, line) + shape, dtype),
    ]


def attention_kernel(
    n_dp,
    frames_ref,
    labels_ref,
    mem_ref,
    dec_ref,
    cot_ref,
    vec_ref,
    pairs_any,
    third_line,
    out_line,
    dz_ref,
    dq_ref,
    dk_ref,
    dvec_ref,
    logits_ref,
    outer_ref,
    third_part,
    out_part,
    squash_ref,
    context_ref,
    ddec_ref,
    cot_s,
    gl_f,
    gl_ref,
    own_logits,
    mats_ref,
    third_s,
    out_s,
    back_s,
    facts,
    facts_gl,
    g_third,
    g_out,
    t_stage,
    t_near,
    o_stage,
    o_near,
    t_far,
    o_far,
    q_s,
    k_s,
    mem_s,
    ctx_s,
    dqa_s,
    dka_s,
    e_s,
    sel_s,
    prob_s,
    sel_d,
    prob_d,
    reach_d,
    back_d,
    w_s,
    a_s,
    own_s,
    nxt_s,
    g_s,
    d_s,
    d_rows,
    bc_s,
    load_sem,
    cot_sems,
    fact_sems,
    logit_sems,
    back_sems,
    sems_t,
    sems_o,
    sems_ft,
    sems_fo,
):
    rows, width = dec_ref.shape
    utts = frames_ref.shape[0]
    length = rows // utts
    vocab_half = cot_ref.shape[2]
    vocab_pad = gl_f.shape[2]
    low = jnp.bfloat16
    f32 = jnp.float32
    lane = lax.broadcasted_iota(jnp.int32, (length, LANES), 1)
    lane_block = lax.broadcasted_iota(jnp.int32, (length, 8, LANES), 2)

    place = Place(n_dp)
    core, chip = place.core, place.chip
    other = (1 - core, chip)
    load = pltpu.make_async_copy(pairs_any, mats_ref, load_sem)
    load.start()
    place.greet()
    third = spread_line(place, third_line, third_s, sems_t)
    outs = spread_line(place, out_line, out_s, sems_o)
    third.begin()
    outs.begin()
    cot_away = remote(
        cot_ref.at[pl.ds((1 - core) * utts, utts)], cot_s, cot_sems.at[0], cot_sems.at[1], other
    )
    cot_away.start()
    third.stage_one()
    outs.stage_one()
    load.wait()
    q_s[...] = contract(dec_ref[...], mats_ref[0], 1, 1) + vec_ref[5:6]
    k_s[...] = contract(mem_ref[...], mats_ref[1], 1, 1)
    mem_s[...] = mem_ref[...].astype(f32)
    e_s[...] = jnp.zeros_like(e_s)
    d_s[...] = jnp.zeros_like(d_s)

    tile = 256
    group = 4

    gl_f[...] = jnp.zeros_like(gl_f)
    cot_away.wait()
    slot = lax.broadcasted_iota(jnp.int32, (length, 1), 0)
    for u in range(utts):
        keep = (slot < labels_ref[u]).astype(f32)
        at = slice(u * length, (u + 1) * length)
        gl_f[core, at, :vocab_half] = cot_ref[core * utts + u].astype(f32) * keep
        gl_f[1 - core, at, :vocab_half] = cot_s[u].astype(f32) * keep
    gl_ref[...] = gl_f[...].astype(low)

    for u in range(utts):
        at = u * length
        if u == utts // 2:
            third.stage_two()
            outs.stage_two()

        def energy_step(block, sums, at=at):
            base = block * group
            for offset in range(group):
                j = base + offset
                row = k_s[pl.ds(at + j, 1), :]
                for head in range(2):
                    total = jnp.zeros((length, LANES), f32)
                    for c in range(width // LANES):
                        columns = slice(head * width + c * LANES, head * width + (c + 1) * LANES)
                        total = total + jnp.tanh(
                            q_s[at : at + length, columns] + row[:, columns]
                        ) * vec_ref[6:7, columns]
                    value = jnp.sum(total, -1, keepdims=True)
                    sums = tuple(
                        jnp.where(lane == j, value, s) if h == head else s
                        for h, s in enumerate(sums)
                    )
            return sums

        blocks = length // group
        zero = jnp.zeros((length, LANES), f32)
        mono, window = lax.fori_loop(0, blocks, energy_step, (zero, zero))
        e_s[0, :, u, :] = mono
        e_s[1, :, u, :] = window

    mask = jnp.zeros((8, LANES), f32)
    row_u = lax.broadcasted_iota(jnp.int32, (8, LANES), 0)
    lane_u = lax.broadcasted_iota(jnp.int32, (8, LANES), 1)
    for u in range(utts):
        inside_u = jnp.logical_and(row_u == u, lane_u < frames_ref[u])
        mask = jnp.where(inside_u, 1.0, mask)
    mask = mask[None]
    third.stage_three()
    outs.stage_three()
    mono = e_s[0] + ENERGY_OFFSET
    window = e_s[1]
    chosen = jax.nn.sigmoid(mono)
    inside = (lane_block < length).astype(f32)
    sel_s[...] = chosen * mask
    leave = (jnp.maximum(mono, 0.0) + jnp.log1p(jnp.exp(-jnp.abs(mono)))) * mask
    prob = jnp.exp(-leave) * inside
    prob_s[...] = prob

    def right(value, distance):
        return pltpu.roll(value, distance, value.ndim - 1)

    def left(value, distance):
        return pltpu.roll(value, LANES - distance, value.ndim - 1)

    diagonals = 2 * length - 1
    bits = [2**n for n in range(5)]

    def skewed(value):
        value = jnp.concatenate([value, jnp.zeros((diagonals - length, 8, LANES), f32)], 0)
        for bit in bits:
            moved = jnp.concatenate([jnp.zeros((bit, 8, LANES), f32), value[:-bit]], 0)
            value = jnp.where(lane_row & bit != 0, moved, value)
        return value

    def straight(value):
        for bit in bits:
            moved = jnp.concatenate([value[bit:], jnp.zeros((bit, 8, LANES), f32)], 0)
            value = jnp.where(lane_row & bit != 0, moved, value)
        return value[:length]

    lane_row = lax.broadcasted_iota(jnp.int32, (8, LANES), 1)
    sel_d[...] = skewed(sel_s[...])
    prob_d[...] = skewed(jnp.where(lane_block < length - 1, prob, 0.0))

    def align_step(d, total):
        reach_d[d] = total
        return sel_d[d] * total + right(prob_d[d] * total, 1)

    lax.fori_loop(0, diagonals, align_step, jnp.where(lane_row == 0, 1.0, 0.0).astype(f32))
    w_s[...] = straight(reach_d[...])
    a_s[...] = sel_s[...] * w_s[...]

    aligned = a_s[...]
    own = jnp.where(lane_block == 0, 1.0, jax.nn.sigmoid(window - right(window, 1)))
    nxt = jax.nn.sigmoid(window - left(window, 1))
    own_s[...] = own
    nxt_s[...] = nxt
    beta = aligned * own + jnp.where(lane_block < length - 1, left(aligned, 1), 0.0) * nxt
    g_s[...] = beta

    for u in range(utts):
        at = u * length
        weights = g_s[:, u, :].astype(low)[:, :length]
        ctx_s[at : at + length] = jnp.dot(
            weights, mem_s[at : at + length].astype(low), preferred_element_type=f32
        )
    context_ref[...] = ctx_s[...].astype(low)

    third.finish()
    outs.finish()
    third_low, third_high = (third_s[s].reshape(width, width) for s in range(2))
    squash = jnp.tanh(
        jnp.dot(dec_ref[...], third_low, preferred_element_type=f32)
        + jnp.dot(context_ref[...], third_high, preferred_element_type=f32)
        + vec_ref[7:8, :width]
    )
    squash_ref[...] = squash.astype(low)
    pull = contract(gl_ref[0], out_s[0].reshape(width, vocab_pad), 1, 1) + contract(
        gl_ref[1], out_s[1].reshape(width, vocab_pad), 1, 1
    )
    dz = (pull * (1.0 - squash * squash)).astype(low)
    dz_ref[...] = dz
    sources = [dec_ref, context_ref, dz_ref, squash_ref]
    handed = [
        remote(source, facts.at[n], fact_sems.at[0, n], fact_sems.at[1, n], other)
        for n, source in enumerate(sources)
    ]
    handed.append(remote(gl_ref.at[1 - core], facts_gl, fact_sems.at[0, 4], fact_sems.at[1, 4], other))
    for copy in handed:
        copy.start()
    dvec_ref[...] = jnp.zeros_like(dvec_ref)
    dvec_ref[7:8, :width] = jnp.sum(dz.astype(f32), 0, keepdims=True)
    for h in range(2):
        begin = width + h * vocab_half
        row = jnp.concatenate(
            [
                jnp.sum(gl_f[h], 0, keepdims=True),
                jnp.zeros((1, 2 * width - vocab_pad), f32),
            ],
            -1,
        )
        dvec_ref[7:8] += pltpu.roll(row, begin, 1)
        bias = pltpu.roll(vec_ref[7:8], 2 * width - begin, 1)[:, :vocab_pad]
        own_logits[h] = (
            jnp.dot(squash_ref[...], out_s[h].reshape(width, vocab_pad), preferred_element_type=f32) + bias
        ).astype(low)
    logits_kept = pltpu.make_async_copy(own_logits.at[core], logits_ref.at[core], logit_sems.at[0])
    logits_away = remote(
        own_logits.at[1 - core], logits_ref.at[core], logit_sems.at[1], logit_sems.at[2], other
    )
    logits_kept.start()
    logits_away.start()
    ddec_ref[...] = contract(dz, third_low, 1, 1)
    ctx_s[...] = contract(dz, third_high, 1, 1).astype(low).astype(f32)

    pad = jnp.zeros((length, LANES - length), f32)
    for u in range(utts):
        at = u * length
        weights = g_s[:, u, :].astype(low)[:, :length]
        pulled = ctx_s[at : at + length].astype(low)
        beta_grad = contract(pulled, mem_s[at : at + length].astype(low), 1, 1)
        e_s[0, :, u, :] = jnp.concatenate([beta_grad, pad], -1)
        mem_s[at : at + length] = contract(weights, pulled, 0, 0)

    for copy in handed:
        copy.wait_recv()
    joined = jnp.where(core == 0, dec_ref[...], context_ref[...])
    joined_other = jnp.where(core == 0, facts[0], facts[1])
    part_rows, out_rows = g_third.shape[1], g_out.shape[1]
    total = (contract(joined, dz_ref[...], 0, 0) + contract(joined_other, facts[2], 0, 0)).astype(low)
    for block in range(n_dp):
        g_third[block] = total[block * part_rows : (block + 1) * part_rows]
    total = (contract(squash_ref[...], gl_ref[core], 0, 0) + contract(facts[3], facts_gl[...], 0, 0)).astype(low)
    for block in range(n_dp):
        g_out[block] = total[block * out_rows : (block + 1) * out_rows]
    third_fold = Fold(
        place, lambda kz, kf, kg: g_third[place.block(kz, kf, kg)].astype(f32), t_stage, t_near, t_far, sems_ft
    )
    out_fold = Fold(
        place, lambda kz, kf, kg: g_out[place.block(kz, kf, kg)].astype(f32), o_stage, o_near, o_far, sems_fo
    )
    third_fold.stage_a()
    out_fold.stage_a()

    beta_grad = e_s[0]
    own = own_s[...]
    nxt = nxt_s[...]
    g_s[...] = beta_grad * own + jnp.where(lane_block >= 1, right(beta_grad * nxt, 1), 0.0)
    aligned = a_s[...]
    from_own = jnp.where(lane_block >= 1, beta_grad * aligned * own * (1.0 - own), 0.0)
    from_next = (
        beta_grad
        * jnp.where(lane_block < length - 1, left(aligned, 1), 0.0)
        * nxt
        * (1.0 - nxt)
    )
    d_s[1] = (from_own - left(from_own, 1) + from_next - right(from_next, 1)) * inside

    prob = prob_s[...]
    reach_d[...] = skewed(g_s[...])

    def retreat_step(k, after):
        d = diagonals - 1 - k
        grad_align = reach_d[d] + after
        total = sel_d[d] * grad_align + prob_d[d] * left(after, 1)
        reach_d[d] = grad_align
        back_d[d] = total
        return total

    lax.fori_loop(0, diagonals, retreat_step, jnp.zeros((8, LANES), f32))
    e_s[0] = straight(reach_d[...])
    e_s[1] = straight(back_d[...])
    reached = w_s[...]
    grad_select = reached * e_s[0]
    grad_prob = reached * jnp.where(lane_block < length - 1, left(e_s[1], 1), 0.0)
    chosen = sel_s[...]
    d_s[0] = grad_select * chosen * (1.0 - chosen) - grad_prob * prob * chosen

    dka_s[...] = jnp.zeros_like(dka_s)
    spots = lax.broadcasted_iota(jnp.int32, (LANES, length * LANES), 1) // LANES
    picks = (lax.broadcasted_iota(jnp.int32, (LANES, length * LANES), 0) == spots).astype(f32)
    for head in range(2):
        for u in range(utts):
            d_rows[u * length : (u + 1) * length] = d_s[head, :, u, :]
        bc_s[head] = jnp.dot(
            d_rows[...], picks, precision=lax.Precision.HIGHEST, preferred_element_type=f32
        )

    def energy_back(u, dvec):
        at = pl.multiple_of(u * length, 8)
        count = length // UNROLL
        for c in range(2 * width // tile):
            columns = slice(c * tile, (c + 1) * tile)
            head = c * tile // width
            q_now = q_s[pl.ds(at, length), columns]

            def back_step(block, sums, head=head, columns=columns, q_now=q_now):
                dq, dw = sums
                for offset in range(UNROLL):
                    j = block * UNROLL + offset
                    squash_all = jnp.tanh(q_now + k_s[pl.ds(at + j, 1), columns])
                    grad = bc_s[head, pl.ds(at, length), pl.ds(pl.multiple_of(j * LANES, LANES), LANES)]
                    grad = jnp.concatenate([grad] * (tile // LANES), -1)
                    scaled = grad * squash_all
                    dw = dw + scaled
                    moved = grad - scaled * squash_all
                    dq = dq + moved
                    dka_s[pl.ds(at + j, 1), columns] = jnp.sum(moved, 0, keepdims=True)
                return (dq, dw)

            zero = jnp.zeros((length, tile), f32)
            dq, dw = lax.fori_loop(0, count, back_step, (zero, zero))
            dq = dq * vec_ref[6:7, columns]
            dqa_s[pl.ds(at, length), columns] = dq
            dvec_ref[5:6, columns] += jnp.sum(dq, 0, keepdims=True)
            dvec_ref[6:7, columns] += jnp.sum(dw, 0, keepdims=True)
        return dvec

    lax.fori_loop(0, utts // 2, energy_back, 0)
    third_fold.stage_b()
    out_fold.stage_b()
    lax.fori_loop(utts // 2, utts, energy_back, 0)
    for h in range(2):
        columns = slice(h * width, (h + 1) * width)
        dq_ref[h] = dqa_s[:, columns].astype(low)
        dk_ref[h] = (dka_s[:, columns] * vec_ref[6:7, columns]).astype(low)
        ddec_ref[...] += jnp.dot(dq_ref[h], mats_ref[0, columns], preferred_element_type=f32)
        mem_s[...] += jnp.dot(dk_ref[h], mats_ref[1, columns], preferred_element_type=f32)
    for u in range(utts):
        at = slice(u * length, (u + 1) * length)
        back_s[0, u] = mem_s[at].astype(low)
        back_s[1, u] = ddec_ref[at].astype(low)
    role = place.role
    mine = core == role
    guest = jnp.logical_not(mine)
    stay = pltpu.make_async_copy(back_s.at[role], outer_ref.at[core], back_sems.at[0, 0])
    cross = remote(back_s.at[role], outer_ref.at[core], back_sems.at[0, 0], back_sems.at[1, core], (role, chip))
    away = remote(
        back_s.at[1 - role],
        outer_ref.at[core],
        back_sems.at[0, 1],
        back_sems.at[1, core],
        (role, chip + place.along[1]),
    )
    away.start()
    pl.when(mine)(stay.start)
    pl.when(guest)(cross.start)
    for kz in range(place.line):
        third_part[kz] = third_fold.summed(kz)
        out_part[kz] = out_fold.summed(kz)
    logits_kept.wait()
    logits_away.wait()
    for copy in handed:
        copy.wait_send()
    away.wait_send()
    pl.when(mine)(stay.wait)
    pl.when(guest)(cross.wait_send)

    def arrived(slot):
        target = outer_ref.at[slot]
        remote(target, target, back_sems.at[0, 0], back_sems.at[1, slot], other).wait_recv()

    arrived(1 - core)
    pl.when(guest)(lambda: arrived(core))
    for moved in (third, outs, third_fold, out_fold):
        moved.sent_all()


def attention(n_dp, frames, labels, memory, decoded, cotangent, vectors, pairs, third_line, out_line):
    rows, width = decoded.shape
    utts = frames.shape[0]
    length = rows // utts
    low, f32 = jnp.bfloat16, jnp.float32
    line, side = DP_LAYOUTS[n_dp][:2]
    third_block, out_block = third_line.shape[1:], out_line.shape[1:]
    vocab_half, vocab_pad = cotangent.shape[2], out_block[1]
    small = (length, 8, LANES)
    diagonal = (2 * length - 1, 8, LANES)
    dma = pltpu.SemaphoreType.DMA
    return pl.pallas_call(
        functools.partial(attention_kernel, n_dp),
        out_shape=(
            jax.ShapeDtypeStruct((rows, width), low),
            jax.ShapeDtypeStruct((2, rows, width), low),
            jax.ShapeDtypeStruct((2, rows, width), low),
            jax.ShapeDtypeStruct((8, 2 * width), f32),
            jax.ShapeDtypeStruct((2, rows, vocab_pad), low),
            jax.ShapeDtypeStruct((2, utts, length, width), low),
            jax.ShapeDtypeStruct((line,) + third_block, low),
            jax.ShapeDtypeStruct((line,) + out_block, low),
        ),
        in_specs=[SMEM_SPEC] * 2 + [VMEM_SPEC] * 4 + [ANY_SPEC] * 3,
        out_specs=(VMEM_SPEC,) * 8,
        scratch_shapes=[
            pltpu.VMEM((rows, width), low),
            pltpu.VMEM((rows, width), low),
            pltpu.VMEM((rows, width), f32),
            pltpu.VMEM((utts, length, vocab_half), low),
            pltpu.VMEM((2, rows, vocab_pad), f32),
            pltpu.VMEM((2, rows, vocab_pad), low),
            pltpu.VMEM((2, rows, vocab_pad), low),
            pltpu.VMEM((2, 2 * width, width), low),
            pltpu.VMEM((2, n_dp) + third_block, low),
            pltpu.VMEM((2, n_dp) + out_block, low),
            pltpu.VMEM((2, utts, length, width), low),
            pltpu.VMEM((4, rows, width), low),
            pltpu.VMEM((rows, vocab_pad), low),
            pltpu.VMEM((n_dp,) + third_block, low),
            pltpu.VMEM((n_dp,) + out_block, low),
        ]
        + fold_buffers(line, side, third_block, low)
        + fold_buffers(line, side, out_block, low)
        + [pltpu.VMEM((side - 1, line) + block, low) for block in (third_block, out_block)]
        + [
            pltpu.VMEM((rows, 2 * width), f32),
            pltpu.VMEM((rows, 2 * width), f32),
            pltpu.VMEM((rows, width), f32),
            pltpu.VMEM((rows, width), f32),
            pltpu.VMEM((rows, 2 * width), f32),
            pltpu.VMEM((rows, 2 * width), f32),
            pltpu.VMEM((2,) + small, f32),
            pltpu.VMEM(small, f32),
            pltpu.VMEM(small, f32),
            pltpu.VMEM(diagonal, f32),
            pltpu.VMEM(diagonal, f32),
            pltpu.VMEM(diagonal, f32),
            pltpu.VMEM(diagonal, f32),
            pltpu.VMEM(small, f32),
            pltpu.VMEM(small, f32),
            pltpu.VMEM(small, f32),
            pltpu.VMEM(small, f32),
            pltpu.VMEM(small, f32),
            pltpu.VMEM((2,) + small, f32),
            pltpu.VMEM((rows, LANES), f32),
            pltpu.VMEM((2, rows, length * LANES), f32),
            dma,
            dma((2,)),
            dma((2, 5)),
            dma((3,)),
            dma((2, 2)),
        ]
        + [spread_sems(line, side)] * 2
        + [fold_sems(line, side)] * 2,
        compiler_params=pltpu.CompilerParams(
            collective_id=2, has_side_effects=True, vmem_limit_bytes=VMEM_LIMIT
        ),
    )(frames, labels, memory, decoded, cotangent, vectors, pairs, third_line, out_line)


def backward_kernel(
    n_dp,
    act_ref,
    cell_ref,
    outer_ref,
    dq_ref,
    dk_ref,
    dec_ref,
    mem_ref,
    wt_any,
    ht_ref,
    dpre_ref,
    dpre_other,
    ht_other,
    mats_part,
    wt_ref,
    outer_s,
    state,
    held,
    facts,
    g_mats,
    m_stage,
    m_near,
    m_far,
    load_sem,
    fact_sems,
    pre_sems,
    ht_sems,
    sems_m,
):
    halves, half, steps, width = outer_ref.shape
    low, f32 = jnp.bfloat16, jnp.float32
    place = Place(n_dp)
    load = pltpu.make_async_copy(wt_any, wt_ref, load_sem)
    load.start()
    place.greet()
    core = place.core
    other = (1 - core, place.chip)
    sources = [dq_ref.at[1 - core], dk_ref.at[1 - core], dec_ref, mem_ref]
    handed = [
        remote(source, facts.at[n], fact_sems.at[0, n], fact_sems.at[1, n], other)
        for n, source in enumerate(sources)
    ]
    handed.append(remote(ht_ref, ht_other, ht_sems.at[0], ht_sems.at[1], other))
    for copy in handed:
        copy.start()
    state[...] = jnp.zeros_like(state)
    held[...] = jnp.zeros_like(held)
    outer_s[:, halves * half :] = jnp.zeros((steps, ROWS - halves * half, width), f32)
    for u in range(halves * half):
        outer_s[:, u, :] = outer_ref[u // half, u % half].astype(f32)

    def step(k, carry):
        t = steps - 1 - k
        rows = pl.ds(pl.multiple_of(t * ROWS, ROWS), ROWS)
        after = pl.ds(pl.multiple_of((t + 1) * ROWS, ROWS), ROWS)
        hidden_total = outer_s[t]
        for q in range(4):
            hidden_total = hidden_total + jnp.dot(
                state[:, q * width : (q + 1) * width], wt_ref[q], preferred_element_type=f32
            )
        in_gate = act_ref[rows, :width]
        forget = act_ref[rows, width : 2 * width]
        candidate = act_ref[rows, 2 * width : 3 * width]
        out_gate = act_ref[rows, 3 * width :]
        squash = jnp.tanh(cell_ref[after])
        cell_total = held[...] + hidden_total * out_gate * (1.0 - squash * squash)
        held[...] = cell_total * forget
        grads = jnp.concatenate(
            [
                cell_total * candidate * in_gate * (1.0 - in_gate),
                cell_total * cell_ref[rows] * forget * (1.0 - forget),
                cell_total * in_gate * (1.0 - candidate * candidate),
                hidden_total * squash * out_gate * (1.0 - out_gate),
            ],
            -1,
        ).astype(low)
        state[...] = grads
        dpre_ref[rows] = grads
        return carry

    shares = 4
    share = steps // shares

    def hand_over(n):
        top = (steps - (n + 1) * share) * ROWS
        rows = slice(top, top + share * ROWS)
        columns = pl.ds(pl.multiple_of((1 - core) * 2 * width, 2 * width), 2 * width)
        copy = remote(
            dpre_ref.at[rows, columns], dpre_other.at[rows, :], pre_sems.at[0, n], pre_sems.at[1, n], other
        )
        copy.start()
        handed.append(copy)

    part_rows = g_mats.shape[1] // 2

    def matrices():
        for copy in handed[:4]:
            copy.wait_recv()
        pairs = [
            (dq_ref[core], dec_ref[...], facts[0], facts[2]),
            (dk_ref[core], mem_ref[...], facts[1], facts[3]),
        ]
        for m, (a, b, c, d) in enumerate(pairs):
            total = (contract(a, b, 0, 0) + contract(c, d, 0, 0)).astype(low)
            for block in range(n_dp):
                g_mats[block, m * part_rows : (m + 1) * part_rows] = total[
                    block * part_rows : (block + 1) * part_rows
                ]

    mats = Fold(
        place, lambda kz, kf, kg: g_mats[place.block(kz, kf, kg)].astype(f32), m_stage, m_near, m_far, sems_m
    )
    matrices()
    mats.stage_a()
    load.wait()
    lines = list(reversed(range(place.line)))
    lax.fori_loop(0, share, step, 0)
    hand_over(0)
    lax.fori_loop(share, 2 * share, step, 0)
    hand_over(1)
    mats.stage_b(*lines[: place.line // 2])
    lax.fori_loop(2 * share, 3 * share, step, 0)
    hand_over(2)
    mats.stage_b(*lines[place.line // 2 :])
    lax.fori_loop(3 * share, steps, step, 0)
    hand_over(3)
    for kz in lines:
        mats_part[kz] = mats.summed(kz)
    for copy in handed[4:]:
        copy.wait_recv()
    for copy in handed:
        copy.wait_send()
    mats.sent_all()


def backward(n_dp, act, cell, outer, dq, dk, decoded, memory, weight_t, ht):
    rows = act.shape[0]
    steps, width = outer.shape[2:]
    low, f32 = jnp.bfloat16, jnp.float32
    line, side = DP_LAYOUTS[n_dp][:2]
    utt_rows = decoded.shape[0]
    mats_block = (2 * width // n_dp, width)
    dma = pltpu.SemaphoreType.DMA
    return pl.pallas_call(
        functools.partial(backward_kernel, n_dp),
        out_shape=(
            jax.ShapeDtypeStruct((rows, 4 * width), low),
            jax.ShapeDtypeStruct((rows, 2 * width), low),
            jax.ShapeDtypeStruct(ht.shape, low),
            jax.ShapeDtypeStruct((line,) + mats_block, low),
        ),
        in_specs=[VMEM_SPEC] * 7 + [ANY_SPEC] * 2,
        out_specs=(VMEM_SPEC, VMEM_SPEC, ANY_SPEC, VMEM_SPEC),
        scratch_shapes=[
            pltpu.VMEM((4, width, width), low),
            pltpu.VMEM((steps, ROWS, width), f32),
            pltpu.VMEM((ROWS, 4 * width), low),
            pltpu.VMEM((ROWS, width), f32),
            pltpu.VMEM((4, utt_rows, width), low),
            pltpu.VMEM((n_dp,) + mats_block, low),
        ]
        + fold_buffers(line, side, mats_block, low)
        + [pltpu.VMEM((side - 1, line) + mats_block, low)]
        + [dma, dma((2, 4)), dma((2, 4)), dma((2,))]
        + [fold_sems(line, side)],
        compiler_params=pltpu.CompilerParams(
            collective_id=3, has_side_effects=True, vmem_limit_bytes=VMEM_LIMIT
        ),
    )(act, cell, outer, dq, dk, decoded, memory, weight_t, ht)


def update_kernel(
    n_dp,
    batch,
    ht_ref,
    ht_other,
    dpre_ref,
    dpre_other,
    w_ref,
    base_ref,
    spread_ref,
    outer_ref,
    vectors_ref,
    dvec_ref,
    mats_part,
    third_part,
    out_part,
    sum_ref,
    gin_ref,
    vec_sum,
    mats_sum,
    third_sum,
    out_sum,
    w_s,
    gin_s,
    gin_u,
    vec_s,
    vec_other,
    vec_parts,
    l_stage,
    l_near,
    v_stage,
    v_near,
    l_far,
    l_end,
    v_far,
    v_parts,
    v_end,
    m_end,
    t_end,
    o_end,
    w_sem,
    gin_sems,
    vec_sems,
    sems_l,
    sems_v,
    sems_m,
    sems_t,
    sems_o,
):
    width = base_ref.shape[1]
    steps = base_ref.shape[0] // ROWS
    low, f32 = jnp.bfloat16, jnp.float32
    place = Place(n_dp)
    load = pltpu.make_async_copy(w_ref, w_s, w_sem)
    load.start()
    place.greet()
    core = place.core
    encoder = place.role == 0
    mine = core == place.role
    block_rows = sum_ref.shape[0]
    half = pl.ds(pl.multiple_of(core * 2 * width, 2 * width), 2 * width)

    def part(kz, kf, kg):
        rows = pl.ds(pl.multiple_of(place.block(kz, kf, kg) * block_rows, block_rows), block_rows)
        return jnp.dot(ht_ref[rows], dpre_ref[:, half], preferred_element_type=f32) + jnp.dot(
            ht_other[rows], dpre_other[...], preferred_element_type=f32
        )

    matrix = FoldRole(place, part, l_stage, l_near, l_far, l_end, sems_l)
    mats = FoldLine(place, mats_part, m_end, sems_m)
    third = FoldLine(place, third_part, t_end, sems_t)
    outs = FoldLine(place, out_part, o_end, sems_o)
    matrix.stage_a()
    mats.begin()
    third.begin()
    outs.begin()

    load.wait()
    gin_s[...] = contract(dpre_ref[...], w_s[...], 1, 1)
    input_grad = gin_s[...]
    scaled = base_ref[...]
    vec_s[...] = dvec_ref[...]
    vec_s[4:5, :width] = jnp.where(encoder, jnp.sum(input_grad * scaled, 0, keepdims=True), 0.0)
    vec_s[4:5, width:] = jnp.where(encoder, jnp.sum(input_grad, 0, keepdims=True), 0.0)
    for q in range(4):
        columns = slice((q % 2) * width, (q % 2 + 1) * width)
        bias = jnp.sum(dpre_ref[:, q * width : (q + 1) * width].astype(f32), 0, keepdims=True)
        for role in range(2):
            row = 2 * role + q // 2
            vec_s[row : row + 1, columns] = jnp.where(place.role == role, bias, 0.0)

    @pl.when(encoder)
    def _():
        grads = gin_s[...] * vectors_ref[4:5, :width]
        values = base_ref[...]
        gin_s[...] = (
            spread_ref[:, :1]
            * (
                grads
                - jnp.mean(grads, -1, keepdims=True)
                - values * jnp.mean(grads * values, -1, keepdims=True)
            )
        )

    turned = gin_s[...].reshape(steps, ROWS, width)
    half_batch = batch // 2
    for u in range(batch):
        straight = outer_ref[u // half_batch, u % half_batch].astype(f32)
        gin_u[u] = turned[:, u, :] + jnp.where(encoder, straight, 0.0)
    kept = pltpu.make_async_copy(gin_u, gin_ref, gin_sems.at[0])
    handed = remote(gin_u, gin_ref, gin_sems.at[1], gin_sems.at[2], (1 - core, place.chip + place.along[1]))

    @pl.when(mine)
    def _():
        kept.start()

    @pl.when(jnp.logical_not(mine))
    def _():
        handed.start()

    own_half = pl.ds(pl.multiple_of(core * width, width), width)
    other_half = pl.ds(pl.multiple_of((1 - core) * width, width), width)
    trade = remote(
        vec_s.at[:, other_half], vec_other, vec_sems.at[0], vec_sems.at[1], (1 - core, place.chip)
    )
    trade.start()
    trade.wait_recv()
    total = vec_s[:, own_half] + vec_other[...]
    piece = width // n_dp
    per_tile = LANES // piece
    for block in range(n_dp):
        tile = total[:, (block // per_tile) * LANES : (block // per_tile + 1) * LANES]
        turn = (block % per_tile) * piece
        vec_parts[block] = pltpu.roll(tile, LANES - turn, 1) if turn else tile
    vecs = Fold(place, lambda kz, kf, kg: vec_parts[place.block(kz, kf, kg)], v_stage, v_near, v_far, sems_v)
    vec_line = FoldLine(place, v_parts, v_end, sems_v)
    vecs.stage_a()
    lines = list(reversed(range(place.line)))
    matrix.stage_b(lines[0])
    for n, kz in enumerate(lines[1:]):
        if n == place.line // 2 - 1:
            vecs.stage_b()
        matrix.stage_b(kz)
        matrix.stage_c(lines[n])
    for n in lines:
        v_parts[n] = vecs.summed(n)
    vec_line.begin()
    matrix.stage_c(lines[-1])
    mats_sum[...] = mats.result()
    third_sum[...] = third.result()
    out_sum[...] = outs.result()
    vec_sum[...] = vec_line.result()
    matrix.result(sum_ref)

    @pl.when(mine)
    def _():
        kept.wait()

    @pl.when(jnp.logical_not(mine))
    def _():
        handed.wait()

    trade.wait_send()
    for fold in (matrix, vecs, vec_line, mats, third, outs):
        fold.sent_all()


def update(n_dp, batch, ht, ht_other, dpre, dpre_other, weight, base, spread, outer, vectors, dvec, *parts):
    rows, width = base.shape
    steps = rows // ROWS
    low, f32 = jnp.bfloat16, jnp.float32
    line, side = DP_LAYOUTS[n_dp][:2]
    block_rows = 2 * width // n_dp
    block = (block_rows, 2 * width)
    dma = pltpu.SemaphoreType.DMA
    return pl.pallas_call(
        functools.partial(update_kernel, n_dp, batch),
        out_shape=(
            jax.ShapeDtypeStruct((block_rows, 4 * width), f32),
            jax.ShapeDtypeStruct((batch, steps, width), f32),
            jax.ShapeDtypeStruct((8, LANES), f32),
        )
        + tuple(jax.ShapeDtypeStruct(part.shape[1:], f32) for part in parts),
        in_specs=[VMEM_SPEC] * 4 + [ANY_SPEC] + [VMEM_SPEC] * 8,
        out_specs=(VMEM_SPEC, ANY_SPEC) + (VMEM_SPEC,) * 4,
        scratch_shapes=[
            pltpu.VMEM((width, 4 * width), low),
            pltpu.VMEM((rows, width), f32),
            pltpu.VMEM((batch, steps, width), f32),
            pltpu.VMEM((8, 2 * width), f32),
            pltpu.VMEM((8, width), f32),
            pltpu.VMEM((n_dp, 8, LANES), f32),
        ]
        + fold_buffers(line, side, block, low)
        + fold_buffers(line, side, (8, LANES), f32)
        + [
            pltpu.VMEM((side - 1, line) + block, low),
            pltpu.VMEM((2, line // 2) + block, low),
            pltpu.VMEM((side - 1, line, 8, LANES), f32),
            pltpu.VMEM((line, 8, LANES), f32),
            pltpu.VMEM((line - 1, 8, LANES), f32),
        ]
        + [pltpu.VMEM((line - 1,) + part.shape[1:], low) for part in parts]
        + [dma, dma((3,)), dma((2,))]
        + [fold_sems(line, side)] * 5,
        compiler_params=pltpu.CompilerParams(
            collective_id=4, has_side_effects=True, vmem_limit_bytes=VMEM_LIMIT
        ),
    )(ht, ht_other, dpre, dpre_other, weight, base, spread, outer, vectors, dvec, *parts)


STEP = 5
BETA_ONE = 0.9
BETA_TWO = 0.999
ADAM_EPS = 1e-08
WEIGHT_DECAY = 0.01
RATE_LSTM = 0.05
RATE_MATRIX = 0.02
RATE_VECTOR = 0.3


def adamw(master, first, second, grad, rate):
    first_new = BETA_ONE * first + (1.0 - BETA_ONE) * grad
    second_new = BETA_TWO * second + (1.0 - BETA_TWO) * grad * grad
    first_hat = first_new / (1.0 - BETA_ONE**STEP)
    second_hat = second_new / (1.0 - BETA_TWO**STEP)
    master_new = master - rate * (
        first_hat / (jnp.sqrt(second_hat) + ADAM_EPS) + WEIGHT_DECAY * master
    )
    return (master_new, first_new, second_new)


def local(
    inputs,
    counts,
    cotangent,
    lstm_master,
    lstm_copy,
    lstm_first,
    lstm_second,
    mats_master,
    mats_copy,
    mats_first,
    mats_second,
    out_master,
    out_copy,
    out_first,
    out_second,
    vec_master,
    vec_first,
    vec_second,
):
    low, f32 = jnp.bfloat16, jnp.float32
    n_dp = lax.axis_size("dp")
    on_first = lax.axis_index("section") == 0
    batch_size, length, model_width = inputs.shape[1:]
    half = batch_size // 2
    vocab_half = out_copy.shape[1]
    vocab_pad = -(-vocab_half // LANES) * LANES
    piece = vec_master.shape[1]

    kept = jnp.where(on_first, counts[0, :half], counts[0, half:])
    other = jnp.where(on_first, counts[0, half:], counts[0, :half])
    other = lax.ppermute(other, "section", [(0, 1), (1, 0)])
    frames, labels = jnp.where(on_first, kept, other), jnp.where(on_first, other, kept)

    mats_block = jnp.swapaxes(mats_copy, 1, 2)
    out_block = jnp.pad(out_copy, ((0, 0), (0, vocab_pad - vocab_half)))
    vec_block = jnp.pad(vec_master.astype(low).astype(f32), ((0, 0), (0, LANES - piece)))
    act, cell, ht, base, spread, vectors, pair, weight, weight_t, pairs, third_line, out_line = forward(
        n_dp, inputs[0], lstm_copy[0], mats_block, out_block, vec_block
    )
    memory, decoded = pair.reshape(2, half * length, model_width)
    pairs = pairs.reshape(2, 2 * model_width, model_width)
    dz, dq, dk, vec_rows, logits, outer, third_part, out_part = attention(
        n_dp, frames, labels, memory, decoded, cotangent, vectors, pairs, third_line, out_line
    )
    logits = logits.reshape(batch_size, length, vocab_pad)[..., :vocab_half]
    dpre, dpre_other, ht_other, mats_part = backward(
        n_dp, act, cell, outer, dq, dk, decoded, memory, weight_t, ht
    )
    lstm_sum, inputs_grad, vec_sum, mats_sum, third_sum, out_sum = update(
        n_dp,
        batch_size,
        ht,
        ht_other,
        dpre,
        dpre_other,
        weight,
        base.reshape(-1, model_width),
        spread.reshape(-1, LANES),
        outer,
        vectors,
        vec_rows,
        mats_part,
        third_part,
        out_part,
    )
    mats_sum = jnp.concatenate([mats_sum.reshape(2, -1, model_width), third_sum[None]], 0)
    mats_sum = jnp.swapaxes(mats_sum, 1, 2)
    lstm_new, lstm_first_new, lstm_second_new = adamw(
        lstm_master, lstm_first, lstm_second, lstm_sum[None], RATE_LSTM
    )
    mats_new, mats_first_new, mats_second_new = adamw(
        mats_master, mats_first, mats_second, mats_sum, RATE_MATRIX
    )
    out_new, out_first_new, out_second_new = adamw(
        out_master, out_first, out_second, out_sum[:, :vocab_half], RATE_MATRIX
    )
    vec_new, vec_first_new, vec_second_new = adamw(
        vec_master, vec_first, vec_second, vec_sum[:, :piece], RATE_VECTOR
    )
    return (
        logits,
        inputs_grad[None],
        lstm_new,
        lstm_first_new,
        lstm_second_new,
        lstm_new.astype(low),
        mats_new,
        mats_first_new,
        mats_second_new,
        mats_new.astype(low),
        out_new,
        out_first_new,
        out_second_new,
        out_new.astype(low),
        vec_new,
        vec_first_new,
        vec_second_new,
    )


def solution(mesh):
    lstm = P("section", "dp", None)
    mats = P(None, None, ("section", "dp"))
    out = P("dp", "section")
    vec = P(None, ("section", "dp"))
    logits = P("dp", None, "section")
    rows = P("section", "dp", None, None)
    groups = (lstm,) * 4 + (mats,) * 4 + (out,) * 4 + (vec,) * 3
    return jax.shard_map(
        local,
        mesh=mesh,
        in_specs=(rows, P("section", "dp"), logits) + groups,
        out_specs=(logits, rows) + groups,
        check_vma=False,
    )
```

time: 486 us -> 431 us (0.89); the launches traced: 485 us -> 424 us
  Pallas kernels: 429 us -> 403 us
  other arithmetic: 27.9 us -> 14.9 us
  starting transfers between devices: 10.8 us -> 0.45 us
  local copies, waits for them, and re-layouts: 10.6 us -> 5.18 us
  waiting for transfers between devices: 4.97 us -> 0.01 us
    pallas_call x1, Pallas kernels: 91.8 us -> 57.8 us  [backward(): pl.pallas_call(functools.partial(backward_kernel, n_dp), out_shape=(jax.S...]
    pallas_call x1, Pallas kernels: 61.1 us -> 87.2 us  [attention(): pl.pallas_call(functools.partial(attention_kernel, n_dp), out_shape=(jax....]
    pallas_call x1, Pallas kernels: 173 us -> 154 us  [forward(): pl.pallas_call(functools.partial(forward_kernel, n_dp), out_shape=(jax.Sh...]
    ppermute x8 -> x1, starting transfers between devices: 10.8 us -> 0.45 us  [local(): other = lax.ppermute(other, 'section', [(0, 1), (1, 0)])]
    select_n x9 -> x2, other arithmetic: 6.63 us -> 1.41 us  [the longest x1 0.82 us: local(): other = jnp.where(on_first, counts[0, half:], counts[0, :half])]
    ppermute x8 -> x1, waiting for transfers between devices: 4.97 us -> 0.01 us  [local(): other = lax.ppermute(other, 'section', [(0, 1), (1, 0)])]
  transfers between devices with their start and end apart: 8 -> 1, of which waited for: 2 -> 0; matrix products, arithmetic and copies ran while one was open for 3% -> 1% of each run, Pallas kernels for 0% -> 36%
where the time goes in v4:
time: 431 us; the launch traced here: 424 us
  Pallas kernels  403 us (94%)
  other arithmetic  14.9 us (3%)
  local copies, waits for them, and re-layouts  5.18 us (1%)
    pallas_call x1, Pallas kernels, forward(): pl.pallas_call(functools.partial(forward_kernel, n_dp), out_shape=(jax.Sh...  154 us
    pallas_call x1, Pallas kernels, update(): pl.pallas_call(functools.partial(update_kernel, n_dp, batch), out_shape=(...  104 us
    pallas_call x1, Pallas kernels, attention(): pl.pallas_call(functools.partial(attention_kernel, n_dp), out_shape=(jax....  87.2 us
    pallas_call x1, Pallas kernels, backward(): pl.pallas_call(functools.partial(backward_kernel, n_dp), out_shape=(jax.S...  57.8 us
  transfers between devices with their start and end apart: 1, of which 0 were waited for; matrix products, arithmetic and copies ran while one was open for 1% of the time, Pallas kernels for 36%

profile of v4, /device:TPU:0, one launch (start us, length us, event | category | flops | bytes accessed | tf_op | source)
XLA Modules:
  0.0 424.4 jit_solution(3336934064646258169)
XLA Ops:
  0.7 0.0 copy-start.12
  0.7 0.8 fusion.6
  1.5 0.5 collective-permute-start
  1.9 0.7 convert_element_type.17
  2.6 0.6 pad_convert_fusion.vec_ref
  3.2 1.5 pad.10.out_ref
  4.7 153.8 %shard_map.305 = (f32[384,4096]{1,0:T(8,128)}, f32[400,1024]{1,0:T(8,128)}, bf16[2048,384]{1,0:T(8,128)(2,1)}, f32[24,16,1024]{2,1,0:T(8,128)}, f32[24,16,128]{2...) custom-call(bf16[12,24,1024]{2,1,0:T(8,128)(2,1)} %bitcast.45, ...), custom_call_target="tpu_custom_call" | custom-call | tf_op jit(solution)/shard_map/pallas_call | solution.py:540
  158.5 1.9 fusion.14
  160.4 0.0 collective-permute-done
  160.4 0.0 copy-done.12
  160.4 0.6 broadcast_select_fusion.2
  161.0 87.2 %shard_map.306 = (bf16[144,1024]{1,0:T(8,128)(2,1)}, bf16[2,144,1024]{2,1,0:T(8,128)(2,1)}, bf16[2,144,1024]{2,1,0:T(8,128)(2,1)}, f32[8,2048]{1,0:T(8,128)}, bf...) custom-call(s32[6]{0:T(128)} %get-tuple-element.93.frames_ref, ...), custom_call_target="tpu_custom_call" | custom-call | tf_op jit(solution)/shard_map/pallas_call | solution.py:1180
  248.2 57.8 %shard_map.307 = (bf16[384,4096]{1,0:T(8,128)(2,1)}, bf16[384,2048]{1,0:T(8,128)(2,1)}, bf16[2048,384]{1,0:T(8,128)(2,1)}, bf16[4,128,1024]{2,1,0:T(8,128)(2,1)}) custom-call(f32[384,4096]{1,0:T(8,128)} %get-tuple-element.53.act_ref, f32[400,1024]{1,0:T(8,128)} %get-tuple-element.54.cell_ref, bf16[2,6,24,1024]{3,2,1,0:T(8,128)(2,1)} %get-tuple-element.55.outer_ref, ...), custom_call_target="tpu_custom_call" | custom-call | tf_op jit(solution)/shard_map/pallas_call | solution.py:1394
  306.0 0.0 copy-start.11
  306.0 0.0 copy-start.13
  306.1 0.0 copy-start.14
  306.1 0.0 copy-start.8
  306.1 0.0 copy-start.9
  306.1 0.0 copy-start.10
  306.1 0.0 copy-start
  306.1 104.0 %shard_map.308 = (f32[128,4096]{1,0:T(8,128)}, f32[12,24,1024]{2,1,0:T(8,128)}, f32[8,128]{1,0:T(8,128)}, f32[128,1024]{1,0:T(8,128)}, f32[64,1024]{1,0:T(8,128)}, /*index=5*/f32[64,512]{1,0:T(8,128)}) custom-call(bf16[2048,384]{1,0:T(8,128)(2,1)} %get-tuple-element.52.ht_ref, bf16[2048,384]{1,0:T(8,128)(2,1)} %get-tuple-element.59.ht_other, ...), custom_call_target="tpu_custom_call" | custom-call | tf_op jit(solution)/shard_map/pallas_call | solution.py:1597
  410.1 0.0 copy-done.11
  410.1 0.0 copy-done.13
  410.1 0.0 copy-done.14
  410.1 1.3 multiply_subtract_fusion.3
  411.4 1.7 fusion.8
  413.2 0.0 copy-start.4
  413.2 7.3 %fusion.12 = (bf16[1,128,4096]{2,1,0:T(8,128)(2,1)}, f32[1,128,4096]{2,1,0:T(8,128)}, f32[1,128,4096]{2,1,0:T(8,128)}, f32[1,128,4096]{2,1,0:T(8,128)}) fusion(f32[1,128,4096]{2,1,0:T(8,128)S(1)} %copy-done, f32[128,4096]{1,0:T(8,128)} %get-tuple-element.70, f32[1,128,4096]{2,1,0:T(8,128)} %param.23, f32[1,128,4096]{2,1,0:T(8,128)} %param.24), kind=kLoop, calls=%fused_computation.27 | loop fusion | flops 8388608 | bytes 15728640 | tf_op jit(solution)/shard_map/convert_element_type | solution.py:1740
  420.5 0.0 copy-done.4
  420.5 2.0 fusion.10
  422.5 0.7 copy.37
  423.2 1.0 copy.38
  (16 shorter events, 0.0 us)
Async XLA Ops:
  0.7 159.8 %copy-start.12 = (s32[1,12]{1,0:T(1,128)S(1)}, s32[1,12]{1,0:T(1,128)}, u32[]{:S(2)}) copy-start(s32[1,12]{1,0:T(1,128)} %param.19) | copy-start | bytes 148
  1.5 158.9 %collective-permute-start = (s32[6]{0:T(128)S(1)}, s32[6]{0:T(128)S(1)}, u32[]{:S(2)}, u32[]{:S(2)}) collective-permute-start(s32[6]{0:T(128)S(1)} %fusion.6), channel_id=1, source_target_pairs={{0,16},{16,0},{1,17},{17,1},{2,18},{18,2},{3,19},{19,3},{4,20},{20... | collective-permute-start | bytes 80 | tf_op jit(solution)/shard_map/ppermute | solution.py:1685
  306.0 104.1 %copy-start.11 = (f32[8,64]{1,0:T(8,128)S(1)}, f32[8,64]{1,0:T(8,128)}, u32[]{:S(2)}) copy-start(f32[8,64]{1,0:T(8,128)} %param.33) | copy-start | bytes 6148
  306.0 104.1 %copy-start.13 = (f32[8,64]{1,0:T(8,128)S(1)}, f32[8,64]{1,0:T(8,128)}, u32[]{:S(2)}) copy-start(f32[8,64]{1,0:T(8,128)} %param.34) | copy-start | bytes 6148
  306.1 104.1 %copy-start.14 = (f32[8,64]{1,0:T(8,128)S(1)}, f32[8,64]{1,0:T(8,128)}, u32[]{:S(2)}) copy-start(f32[8,64]{1,0:T(8,128)} %param.35) | copy-start | bytes 6148
  306.1 105.4 %copy-start.8 = (f32[64,500]{1,0:T(8,128)S(1)}, f32[64,500]{1,0:T(8,128)}, u32[]{:S(2)}) copy-start(f32[64,500]{1,0:T(8,128)} %param.29) | copy-start | bytes 384004
  306.1 105.4 %copy-start.9 = (f32[64,500]{1,0:T(8,128)S(1)}, f32[64,500]{1,0:T(8,128)}, u32[]{:S(2)}) copy-start(f32[64,500]{1,0:T(8,128)} %param.31) | copy-start | bytes 384004
  306.1 105.4 %copy-start.10 = (f32[64,500]{1,0:T(8,128)S(1)}, f32[64,500]{1,0:T(8,128)}, u32[]{:S(2)}) copy-start(f32[64,500]{1,0:T(8,128)} %param.32) | copy-start | bytes 384004
  306.1 107.1 %copy-start = (f32[1,128,4096]{2,1,0:T(8,128)S(1)}, f32[1,128,4096]{2,1,0:T(8,128)}, u32[]{:S(2)}) copy-start(f32[1,128,4096]{2,1,0:T(8,128)} %param.21) | copy-start | bytes 6291460
  413.2 7.3 %copy-start.2 = (f32[3,1024,64]{1,2,0:T(8,128)S(1)}, f32[3,1024,64]{1,2,0:T(8,128)}, u32[]{:S(2)}) copy-start(f32[3,1024,64]{1,2,0:T(8,128)} %param.25) | copy-start | bytes 2359300
  413.2 7.3 %copy-start.3 = (f32[3,1024,64]{1,2,0:T(8,128)S(1)}, f32[3,1024,64]{1,2,0:T(8,128)}, u32[]{:S(2)}) copy-start(f32[3,1024,64]{1,2,0:T(8,128)} %param.27) | copy-start | bytes 2359300
  413.2 7.3 %copy-start.4 = (f32[3,1024,64]{1,2,0:T(8,128)S(1)}, f32[3,1024,64]{1,2,0:T(8,128)}, u32[]{:S(2)}) copy-start(f32[3,1024,64]{1,2,0:T(8,128)} %param.28) | copy-start | bytes 2359300
  413.2 7.3 %copy-start.5 = (f32[128,1024]{1,0:T(8,128)S(1)}, f32[128,1024]{1,0:T(8,128)}, u32[]{:S(2)}) copy-start(f32[128,1024]{1,0:T(8,128)} %get-tuple-element.71) | copy-start | bytes 1572868
  413.2 7.3 %copy-start.7 = (f32[64,1024]{1,0:T(8,128)S(1)}, f32[64,1024]{1,0:T(8,128)}, u32[]{:S(2)}) copy-start(f32[64,1024]{1,0:T(8,128)} %get-tuple-element.72) | copy-start | bytes 786436
  420.5 2.0 copy-start.6
  420.5 2.7 copy-start.1

commit v5 on v4

--- a/solution.py
+++ b/solution.py
@@ -9,6 +9,9 @@
 ROWS = 16
 LANES = 128
 UNROLL = 8
+FOLDS = 4
+LAG = 2
+LAST_LAG = 3
 ENERGY_OFFSET = -4.0
 NORM_EPS = 1e-05
 VMEM_SPEC = pl.BlockSpec(memory_space=pltpu.VMEM)
@@ -162,9 +165,10 @@
             copy.wait_send()
 
 
-def spread_sems(line, side):
+def spread_sems(line, side, last=False):
     dma = pltpu.SemaphoreType.DMA
-    return {
+    ends = {"ls": dma((side, side, line)), "lr": dma((side, side, line))}
+    return (ends if last else {}) | {
         "zs": dma((line, 2)),
         "zr": dma((line,)),
         "fs": dma((side, line)),
@@ -202,42 +206,54 @@
     return spread
 
 
-class LineGather:
-    def __init__(self, place, source, target, sems):
-        self.kept = pltpu.make_async_copy(source, target.at[0], sems["zr"].at[0])
-        self.copies = [
-            remote(source, target.at[k], sems["zs"].at[k, 0], sems["zr"].at[k], (place.core, place.chip + place.along[k]))
-            for k in range(1, place.line)
-        ]
+class SpreadLast(Spread):
+    def __init__(self, place, source, at, sems):
+        super().__init__(place, lambda block: at(place.core, block), lambda block: at(1 - place.core, block), sems)
+        self.source = source
+        self.kept = pltpu.make_async_copy(source, self.here(place.chip), sems["zr"].at[0])
 
     def begin(self):
-        for copy in [self.kept] + self.copies:
-            copy.start()
-
-    def finish(self):
-        for copy in [self.kept] + self.copies:
-            copy.wait()
-
-
-def spread_line(place, source, target, sems):
-    spread = Spread(
-        place,
-        lambda block: target.at[place.core, block],
-        lambda block: target.at[1 - place.core, block],
-        sems,
-    )
-    kept = [
-        pltpu.make_async_copy(source.at[kz], spread.here(place.block(kz)), sems["zr"].at[kz])
-        for kz in range(place.line)
-    ]
-
-    def begin():
-        for copy in kept:
-            copy.start()
-
-    spread.begin = begin
-    spread.wait_line = lambda kz: kept[kz].wait()
-    return spread
+        place = self.place
+        self.kept.start()
+        own = self.here(place.chip)
+        for k in range(1, place.side):
+            for moves, send, receive in (
+                (place.first, self.sems["fs"].at[k, 0], self.sems["fr"].at[k, 0]),
+                (place.second, self.sems["gs"].at[k, 0, 0], self.sems["gr"].at[k, 0, 0]),
+            ):
+                copy = remote(self.source, own, send, receive, (place.core, place.chip + moves[k]))
+                copy.start()
+                self.sent.append(copy)
+
+    def stage_plane(self):
+        for kf in range(1, self.place.side):
+            self.arrived(self.here(self.place.block(0, kf)), self.sems["fr"].at[kf, 0])
+            self.to_second(0, kf)
+
+    def stage_line(self):
+        place = self.place
+        self.kept.wait()
+        for kg in range(place.side):
+            for kf in range(place.side):
+                target = self.here(place.block(0, kf, kg))
+                if kg:
+                    self.arrived(target, self.sems["gr"].at[kg, kf, 0])
+                for kz in reversed(range(1, place.line)):
+                    self.send(
+                        target,
+                        (place.core, place.chip + place.along[kz]),
+                        self.sems["ls"].at[kg, kf, kz],
+                        self.sems["lr"].at[kg, kf, kz],
+                    )
+                self.to_core(0, kf, kg)
+
+    def stage_core(self):
+        place = self.place
+        for kg in range(place.side):
+            for kf in range(place.side):
+                for kz in range(1, place.line):
+                    self.arrived(self.here(place.block(kz, kf, kg)), self.sems["lr"].at[kg, kf, kz])
+                    self.to_core(kz, kf, kg)
 
 
 def spread_role(place, source, target, sems, rows, half, first, count):
@@ -329,7 +345,7 @@
     mats_ref,
     out_ref,
     vec_ref,
-    act_ref,
+    act_out,
     cell_ref,
     ht_ref,
     base_ref,
@@ -339,8 +355,9 @@
     w_out,
     wt_out,
     mats_out,
-    mats_line,
-    out_line,
+    third_out,
+    out_out,
+    act_ref,
     seq_s,
     result_s,
     x_s,
@@ -374,8 +391,8 @@
     ]
     mats = spread_even(place, mats_ref.at[:2], lambda core, chip: mats_out.at[:, core, chip], sems_m)
     vecs = spread_even(place, vec_ref, lambda core, chip: vec_s.at[core, chip], sems_v)
-    thirds = LineGather(place, mats_ref.at[2], mats_line, sems_n)
-    outs = LineGather(place, out_ref, out_line, sems_o)
+    thirds = SpreadLast(place, mats_ref.at[2], lambda core, chip: third_out.at[core, chip], sems_n)
+    outs = spread_even(place, out_ref, lambda core, chip: out_out.at[core, chip], sems_o)
     vecs.begin()
     for part in matrix:
         part.begin()
@@ -383,12 +400,31 @@
     seq_away = remote(seq_ref, seq_s, seq_sem.at[1], seq_sem.at[2], (1 - core, chip + place.along[1]))
     pl.when(mine)(seq_kept.start)
     pl.when(guest)(seq_away.start)
+    thirds.begin()
     for part in matrix:
         part.stage_one(0)
     state[...] = jnp.zeros_like(state)
     cell_ref[:ROWS] = jnp.zeros((ROWS, width), f32)
     base_ref[:, batch:] = jnp.zeros((steps, ROWS - batch, width), f32)
     spread_ref[...] = jnp.zeros_like(spread_ref)
+    line_rest = range(1, place.line)
+    thirds.stage_plane()
+    for n in range(len(matrix) + 2):
+        if n < len(matrix):
+            matrix[n].stage_one(*line_rest)
+        if n == 0:
+            vecs.stage_one()
+        if n == len(matrix) - 1:
+            mats.begin()
+            outs.begin()
+        if 1 <= n <= len(matrix):
+            matrix[n - 1].stage_two()
+        if n == 1:
+            vecs.stage_two()
+        if n >= 2:
+            matrix[n - 2].stage_three()
+    mats.stage_one(0)
+    thirds.stage_line()
     pl.when(mine)(seq_kept.wait)
     pl.when(guest)(seq_away.wait)
     for u in range(batch):
@@ -397,23 +433,6 @@
         spread = lax.rsqrt(jnp.mean(center * center, -1, keepdims=True) + NORM_EPS)
         base_ref[:, u, :] = jnp.where(encoder, center * spread, raw)
         spread_ref[:, u, :] = jnp.broadcast_to(spread, (steps, LANES))
-    line_rest = range(1, place.line)
-    for n in range(len(matrix) + 2):
-        if n < len(matrix):
-            matrix[n].stage_one(*line_rest)
-        if n == 0:
-            vecs.stage_one()
-        if n == len(matrix) - 1:
-            mats.begin()
-            thirds.begin()
-            outs.begin()
-        if 1 <= n <= len(matrix):
-            matrix[n - 1].stage_two()
-        if n == 1:
-            vecs.stage_two()
-        if n >= 2:
-            matrix[n - 2].stage_three()
-    mats.stage_one(0)
     vecs.stage_three()
     vecs.finish()
     piece = 2 * width // (2 * n_dp)
@@ -467,12 +486,24 @@
         return carry
 
     h_s[:ROWS] = jnp.zeros((ROWS, width), low)
-    marks = [steps * n // 24 for n in (0, 4, 14, 24)]
-    lax.fori_loop(marks[0], marks[1], step, 0)
+    marks = [steps * n // 24 for n in (0, 8, 12, 18, 24)]
+    gates_out = []
+
+    def run(n):
+        lax.fori_loop(marks[n], marks[n + 1], step, 0)
+        rows = slice(marks[n] * ROWS, marks[n + 1] * ROWS)
+        gates_out.append(pltpu.make_async_copy(act_ref.at[rows], act_out.at[rows], keep_sem.at[2 + n]))
+        gates_out[-1].start()
+
     mats.stage_one(*line_rest)
-    lax.fori_loop(marks[1], marks[2], step, 0)
+    run(0)
     mats.stage_two()
-    lax.fori_loop(marks[2], marks[3], step, 0)
+    outs.stage_one()
+    run(1)
+    outs.stage_two()
+    run(2)
+    mats.stage_three()
+    run(3)
     turned = h_s[ROWS:].astype(f32).reshape(steps, ROWS, width)
     for u in range(batch):
         value = turned[:, u, :]
@@ -498,10 +529,11 @@
     keep_turned = pltpu.make_async_copy(wt_s, wt_out, keep_sem.at[1])
     keep_turned.start()
     ht_ref[width:] = h_s[:-ROWS].T
-    mats.stage_three()
+    outs.stage_three()
+    thirds.stage_core()
     mats.finish()
+    outs.finish()
     thirds.finish()
-    outs.finish()
     for h in range(2):
         home = jnp.logical_and(mine, core == h)
         source, target = result_s.at[h * half : (h + 1) * half], pair_ref.at[place.role]
@@ -524,9 +556,11 @@
     arrived(1 - place.role)
     keep.wait()
     keep_turned.wait()
+    for copy in gates_out:
+        copy.wait()
     for part in matrix:
         part.sent_line()
-    for spread in (*matrix, vecs, mats):
+    for spread in (*matrix, vecs, mats, thirds, outs):
         spread.sent_all()
 
 
@@ -550,12 +584,13 @@
             jax.ShapeDtypeStruct((width, 4 * width), low),
             jax.ShapeDtypeStruct((4, width, width), low),
             jax.ShapeDtypeStruct((2, 2, n_dp, columns, width), low),
-            jax.ShapeDtypeStruct((line, columns, width), low),
-            jax.ShapeDtypeStruct((line,) + out_block.shape, low),
+            jax.ShapeDtypeStruct((2, n_dp, columns, width), low),
+            jax.ShapeDtypeStruct((2, n_dp) + out_block.shape, low),
         ),
         in_specs=[VMEM_SPEC, ANY_SPEC, ANY_SPEC, ANY_SPEC, VMEM_SPEC],
-        out_specs=(VMEM_SPEC,) * 7 + (ANY_SPEC,) * 5,
+        out_specs=(ANY_SPEC,) + (VMEM_SPEC,) * 6 + (ANY_SPEC,) * 5,
         scratch_shapes=[
+            pltpu.VMEM((rows, 4 * width), f32),
             pltpu.VMEM((batch, steps, width), low),
             pltpu.VMEM((batch, steps, width), low),
             pltpu.VMEM((rows, width), low),
@@ -564,11 +599,13 @@
             pltpu.VMEM((4, width, width), low),
             pltpu.VMEM((2, n_dp, 8, LANES), f32),
             pltpu.VMEM((ROWS, width), low),
-            dma((2,)),
+            dma((6,)),
             dma((3,)),
             dma((2, 2)),
         ]
-        + [spread_sems(line, side)] * (4 + CHUNKS),
+        + [spread_sems(line, side)] * 2
+        + [spread_sems(line, side, last=True)]
+        + [spread_sems(line, side)] * (1 + shard.shape[0] // max(ROWS, shard.shape[0] // CHUNKS)),
         compiler_params=pltpu.CompilerParams(
             collective_id=1, has_side_effects=True, vmem_limit_bytes=VMEM_LIMIT
         ),
@@ -623,6 +660,16 @@
                         self.sems["fr"].at[kf, kz],
                     )
 
+    def stage_half(self, half_ref):
+        place = self.place
+        for kz in range(place.line):
+            for kf in range(place.side):
+                total = self.part(kz, kf, 0)
+                for kg in range(1, place.side):
+                    self.arrived(self.near.at[kg - 1, kf, kz], self.sems["gr"].at[kg, kf, kz])
+                    total = total + self.near[kg - 1, kf, kz].astype(jnp.float32)
+                half_ref[kf, kz] = total.astype(half_ref.dtype)
+
     def summed(self, kz):
         place = self.place
         total = self.near[0, 0, kz].astype(jnp.float32)
@@ -634,6 +681,31 @@
     def sent_all(self):
         for copy in self.sent:
             copy.wait_send()
+
+
+class FoldRest(Fold):
+    def __init__(self, place, half_ref, far, sems):
+        super().__init__(place, None, None, None, far, sems)
+        self.half_ref = half_ref
+
+    def begin(self):
+        place = self.place
+        for kz in range(place.line):
+            for kf in range(1, place.side):
+                self.send(
+                    self.half_ref.at[kf, kz],
+                    self.far.at[kf - 1, kz],
+                    (place.core, place.chip + place.first[kf]),
+                    self.sems["fs"].at[kf, kz],
+                    self.sems["fr"].at[kf, kz],
+                )
+
+    def summed(self, kz):
+        total = self.half_ref[0, kz].astype(jnp.float32)
+        for kf in range(1, self.place.side):
+            self.arrived(self.far.at[kf - 1, kz], self.sems["fr"].at[kf, kz])
+            total = total + self.far[kf - 1, kz].astype(jnp.float32)
+        return total.astype(self.far.dtype)
 
 
 class FoldLine:
@@ -759,16 +831,16 @@
     cot_ref,
     vec_ref,
     pairs_any,
-    third_line,
-    out_line,
+    third_any,
+    out_any,
     dz_ref,
     dq_ref,
     dk_ref,
     dvec_ref,
     logits_ref,
     outer_ref,
-    third_part,
-    out_part,
+    third_half,
+    out_half,
     squash_ref,
     context_ref,
     ddec_ref,
@@ -788,8 +860,6 @@
     t_near,
     o_stage,
     o_near,
-    t_far,
-    o_far,
     q_s,
     k_s,
     mem_s,
@@ -816,8 +886,6 @@
     fact_sems,
     logit_sems,
     back_sems,
-    sems_t,
-    sems_o,
     sems_ft,
     sems_fo,
 ):
@@ -834,21 +902,22 @@
     place = Place(n_dp)
     core, chip = place.core, place.chip
     other = (1 - core, chip)
-    load = pltpu.make_async_copy(pairs_any, mats_ref, load_sem)
-    load.start()
+    loads = [
+        pltpu.make_async_copy(pairs_any.at[0], mats_ref.at[0], load_sem.at[0]),
+        pltpu.make_async_copy(pairs_any.at[1], mats_ref.at[1], load_sem.at[1]),
+        pltpu.make_async_copy(third_any, third_s, load_sem.at[2]),
+        pltpu.make_async_copy(out_any, out_s, load_sem.at[3]),
+    ]
+    for load in loads:
+        load.start()
     place.greet()
-    third = spread_line(place, third_line, third_s, sems_t)
-    outs = spread_line(place, out_line, out_s, sems_o)
-    third.begin()
-    outs.begin()
     cot_away = remote(
         cot_ref.at[pl.ds((1 - core) * utts, utts)], cot_s, cot_sems.at[0], cot_sems.at[1], other
     )
     cot_away.start()
-    third.stage_one()
-    outs.stage_one()
-    load.wait()
+    loads[0].wait()
     q_s[...] = contract(dec_ref[...], mats_ref[0], 1, 1) + vec_ref[5:6]
+    loads[1].wait()
     k_s[...] = contract(mem_ref[...], mats_ref[1], 1, 1)
     mem_s[...] = mem_ref[...].astype(f32)
     e_s[...] = jnp.zeros_like(e_s)
@@ -869,9 +938,6 @@
 
     for u in range(utts):
         at = u * length
-        if u == utts // 2:
-            third.stage_two()
-            outs.stage_two()
 
         def energy_step(block, sums, at=at):
             base = block * group
@@ -905,8 +971,6 @@
         inside_u = jnp.logical_and(row_u == u, lane_u < frames_ref[u])
         mask = jnp.where(inside_u, 1.0, mask)
     mask = mask[None]
-    third.stage_three()
-    outs.stage_three()
     mono = e_s[0] + ENERGY_OFFSET
     window = e_s[1]
     chosen = jax.nn.sigmoid(mono)
@@ -966,17 +1030,17 @@
         )
     context_ref[...] = ctx_s[...].astype(low)
 
-    third.finish()
-    outs.finish()
-    third_low, third_high = (third_s[s].reshape(width, width) for s in range(2))
+    loads[2].wait()
+    loads[3].wait()
+    third_low, third_high = third_s[0], third_s[1]
     squash = jnp.tanh(
         jnp.dot(dec_ref[...], third_low, preferred_element_type=f32)
         + jnp.dot(context_ref[...], third_high, preferred_element_type=f32)
         + vec_ref[7:8, :width]
     )
     squash_ref[...] = squash.astype(low)
-    pull = contract(gl_ref[0], out_s[0].reshape(width, vocab_pad), 1, 1) + contract(
-        gl_ref[1], out_s[1].reshape(width, vocab_pad), 1, 1
+    pull = contract(gl_ref[0], out_s[0], 1, 1) + contract(
+        gl_ref[1], out_s[1], 1, 1
     )
     dz = (pull * (1.0 - squash * squash)).astype(low)
     dz_ref[...] = dz
@@ -1002,7 +1066,7 @@
         dvec_ref[7:8] += pltpu.roll(row, begin, 1)
         bias = pltpu.roll(vec_ref[7:8], 2 * width - begin, 1)[:, :vocab_pad]
         own_logits[h] = (
-            jnp.dot(squash_ref[...], out_s[h].reshape(width, vocab_pad), preferred_element_type=f32) + bias
+            jnp.dot(squash_ref[...], out_s[h], preferred_element_type=f32) + bias
         ).astype(low)
     logits_kept = pltpu.make_async_copy(own_logits.at[core], logits_ref.at[core], logit_sems.at[0])
     logits_away = remote(
@@ -1034,10 +1098,10 @@
     for block in range(n_dp):
         g_out[block] = total[block * out_rows : (block + 1) * out_rows]
     third_fold = Fold(
-        place, lambda kz, kf, kg: g_third[place.block(kz, kf, kg)].astype(f32), t_stage, t_near, t_far, sems_ft
+        place, lambda kz, kf, kg: g_third[place.block(kz, kf, kg)].astype(f32), t_stage, t_near, None, sems_ft
     )
     out_fold = Fold(
-        place, lambda kz, kf, kg: g_out[place.block(kz, kf, kg)].astype(f32), o_stage, o_near, o_far, sems_fo
+        place, lambda kz, kf, kg: g_out[place.block(kz, kf, kg)].astype(f32), o_stage, o_near, None, sems_fo
     )
     third_fold.stage_a()
     out_fold.stage_a()
@@ -1116,10 +1180,7 @@
             dvec_ref[6:7, columns] += jnp.sum(dw, 0, keepdims=True)
         return dvec
 
-    lax.fori_loop(0, utts // 2, energy_back, 0)
-    third_fold.stage_b()
-    out_fold.stage_b()
-    lax.fori_loop(utts // 2, utts, energy_back, 0)
+    lax.fori_loop(0, utts, energy_back, 0)
     for h in range(2):
         columns = slice(h * width, (h + 1) * width)
         dq_ref[h] = dqa_s[:, columns].astype(low)
@@ -1145,9 +1206,8 @@
     away.start()
     pl.when(mine)(stay.start)
     pl.when(guest)(cross.start)
-    for kz in range(place.line):
-        third_part[kz] = third_fold.summed(kz)
-        out_part[kz] = out_fold.summed(kz)
+    third_fold.stage_half(third_half)
+    out_fold.stage_half(out_half)
     logits_kept.wait()
     logits_away.wait()
     for copy in handed:
@@ -1162,18 +1222,19 @@
 
     arrived(1 - core)
     pl.when(guest)(lambda: arrived(core))
-    for moved in (third, outs, third_fold, out_fold):
+    for moved in (third_fold, out_fold):
         moved.sent_all()
 
 
-def attention(n_dp, frames, labels, memory, decoded, cotangent, vectors, pairs, third_line, out_line):
+def attention(n_dp, frames, labels, memory, decoded, cotangent, vectors, pairs, third, outs):
     rows, width = decoded.shape
     utts = frames.shape[0]
     length = rows // utts
     low, f32 = jnp.bfloat16, jnp.float32
     line, side = DP_LAYOUTS[n_dp][:2]
-    third_block, out_block = third_line.shape[1:], out_line.shape[1:]
-    vocab_half, vocab_pad = cotangent.shape[2], out_block[1]
+    vocab_pad = outs.shape[2]
+    third_block, out_block = (width // n_dp, width), (width // n_dp, vocab_pad)
+    vocab_half = cotangent.shape[2]
     small = (length, 8, LANES)
     diagonal = (2 * length - 1, 8, LANES)
     dma = pltpu.SemaphoreType.DMA
@@ -1186,8 +1247,8 @@
             jax.ShapeDtypeStruct((8, 2 * width), f32),
             jax.ShapeDtypeStruct((2, rows, vocab_pad), low),
             jax.ShapeDtypeStruct((2, utts, length, width), low),
-            jax.ShapeDtypeStruct((line,) + third_block, low),
-            jax.ShapeDtypeStruct((line,) + out_block, low),
+            jax.ShapeDtypeStruct((side, line) + third_block, low),
+            jax.ShapeDtypeStruct((side, line) + out_block, low),
         ),
         in_specs=[SMEM_SPEC] * 2 + [VMEM_SPEC] * 4 + [ANY_SPEC] * 3,
         out_specs=(VMEM_SPEC,) * 8,
@@ -1200,8 +1261,8 @@
             pltpu.VMEM((2, rows, vocab_pad), low),
             pltpu.VMEM((2, rows, vocab_pad), low),
             pltpu.VMEM((2, 2 * width, width), low),
-            pltpu.VMEM((2, n_dp) + third_block, low),
-            pltpu.VMEM((2, n_dp) + out_block, low),
+            pltpu.VMEM((2, width, width), low),
+            pltpu.VMEM((2, width, vocab_pad), low),
             pltpu.VMEM((2, utts, length, width), low),
             pltpu.VMEM((4, rows, width), low),
             pltpu.VMEM((rows, vocab_pad), low),
@@ -1210,7 +1271,6 @@
         ]
         + fold_buffers(line, side, third_block, low)
         + fold_buffers(line, side, out_block, low)
-        + [pltpu.VMEM((side - 1, line) + block, low) for block in (third_block, out_block)]
         + [
             pltpu.VMEM((rows, 2 * width), f32),
             pltpu.VMEM((rows, 2 * width), f32),
@@ -1233,35 +1293,39 @@
             pltpu.VMEM((2,) + small, f32),
             pltpu.VMEM((rows, LANES), f32),
             pltpu.VMEM((2, rows, length * LANES), f32),
-            dma,
+            dma((4,)),
             dma((2,)),
             dma((2, 5)),
             dma((3,)),
             dma((2, 2)),
         ]
-        + [spread_sems(line, side)] * 2
         + [fold_sems(line, side)] * 2,
         compiler_params=pltpu.CompilerParams(
             collective_id=2, has_side_effects=True, vmem_limit_bytes=VMEM_LIMIT
         ),
-    )(frames, labels, memory, decoded, cotangent, vectors, pairs, third_line, out_line)
+    )(frames, labels, memory, decoded, cotangent, vectors, pairs, third, outs)
 
 
 def backward_kernel(
     n_dp,
-    act_ref,
     cell_ref,
     outer_ref,
     dq_ref,
     dk_ref,
     dec_ref,
     mem_ref,
+    third_half,
+    out_half,
+    act_any,
     wt_any,
     ht_ref,
     dpre_ref,
     dpre_other,
     ht_other,
     mats_part,
+    third_sum,
+    out_sum,
+    act_ref,
     wt_ref,
     outer_s,
     state,
@@ -1271,19 +1335,35 @@
     m_stage,
     m_near,
     m_far,
+    t_far,
+    t_parts,
+    t_end,
+    o_far,
+    o_parts,
+    o_end,
     load_sem,
     fact_sems,
     pre_sems,
     ht_sems,
     sems_m,
+    sems_t,
+    sems_o,
 ):
     halves, half, steps, width = outer_ref.shape
     low, f32 = jnp.bfloat16, jnp.float32
     place = Place(n_dp)
-    load = pltpu.make_async_copy(wt_any, wt_ref, load_sem)
-    load.start()
+    loads = [
+        pltpu.make_async_copy(act_any, act_ref, load_sem.at[0]),
+        pltpu.make_async_copy(wt_any, wt_ref, load_sem.at[1]),
+    ]
+    for load in loads:
+        load.start()
     place.greet()
     core = place.core
+    third, outs = FoldRest(place, third_half, t_far, sems_t), FoldRest(place, out_half, o_far, sems_o)
+    third_line, out_line = FoldLine(place, t_parts, t_end, sems_t), FoldLine(place, o_parts, o_end, sems_o)
+    third.begin()
+    outs.begin()
     other = (1 - core, place.chip)
     sources = [dq_ref.at[1 - core], dk_ref.at[1 - core], dec_ref, mem_ref]
     handed = [
@@ -1362,10 +1442,16 @@
     )
     matrices()
     mats.stage_a()
-    load.wait()
+    for load in loads:
+        load.wait()
     lines = list(reversed(range(place.line)))
     lax.fori_loop(0, share, step, 0)
     hand_over(0)
+    for kz in lines:
+        t_parts[kz] = third.summed(kz)
+        o_parts[kz] = outs.summed(kz)
+    third_line.begin()
+    out_line.begin()
     lax.fori_loop(share, 2 * share, step, 0)
     hand_over(1)
     mats.stage_b(*lines[: place.line // 2])
@@ -1376,14 +1462,17 @@
     hand_over(3)
     for kz in lines:
         mats_part[kz] = mats.summed(kz)
+    third_sum[...] = third_line.result()
+    out_sum[...] = out_line.result()
     for copy in handed[4:]:
         copy.wait_recv()
     for copy in handed:
         copy.wait_send()
-    mats.sent_all()
-
-
-def backward(n_dp, act, cell, outer, dq, dk, decoded, memory, weight_t, ht):
+    for fold in (mats, third, outs, third_line, out_line):
+        fold.sent_all()
+
+
+def backward(n_dp, act, cell, outer, dq, dk, decoded, memory, third_half, out_half, weight_t, ht):
     rows = act.shape[0]
     steps, width = outer.shape[2:]
     low, f32 = jnp.bfloat16, jnp.float32
@@ -1398,10 +1487,13 @@
             jax.ShapeDtypeStruct((rows, 2 * width), low),
             jax.ShapeDtypeStruct(ht.shape, low),
             jax.ShapeDtypeStruct((line,) + mats_block, low),
+            jax.ShapeDtypeStruct(third_half.shape[2:], f32),
+            jax.ShapeDtypeStruct(out_half.shape[2:], f32),
         ),
-        in_specs=[VMEM_SPEC] * 7 + [ANY_SPEC] * 2,
-        out_specs=(VMEM_SPEC, VMEM_SPEC, ANY_SPEC, VMEM_SPEC),
+        in_specs=[VMEM_SPEC] * 8 + [ANY_SPEC] * 3,
+        out_specs=(VMEM_SPEC, VMEM_SPEC, ANY_SPEC) + (VMEM_SPEC,) * 3,
         scratch_shapes=[
+            pltpu.VMEM((rows, 4 * width), f32),
             pltpu.VMEM((4, width, width), low),
             pltpu.VMEM((steps, ROWS, width), f32),
             pltpu.VMEM((ROWS, 4 * width), low),
@@ -1411,12 +1503,17 @@
         ]
         + fold_buffers(line, side, mats_block, low)
         + [pltpu.VMEM((side - 1, line) + mats_block, low)]
-        + [dma, dma((2, 4)), dma((2, 4)), dma((2,))]
-        + [fold_sems(line, side)],
+        + [
+            pltpu.VMEM(count + block, low)
+            for block in (third_half.shape[2:], out_half.shape[2:])
+            for count in ((side - 1, line), (line,), (line - 1,))
+        ]
+        + [dma((2,)), dma((2, 4)), dma((2, 4)), dma((2,))]
+        + [fold_sems(line, side)] * 3,
         compiler_params=pltpu.CompilerParams(
             collective_id=3, has_side_effects=True, vmem_limit_bytes=VMEM_LIMIT
         ),
-    )(act, cell, outer, dq, dk, decoded, memory, weight_t, ht)
+    )(cell, outer, dq, dk, decoded, memory, third_half, out_half, act, weight_t, ht)
 
 
 def update_kernel(
@@ -1433,40 +1530,28 @@
     vectors_ref,
     dvec_ref,
     mats_part,
-    third_part,
-    out_part,
     sum_ref,
     gin_ref,
     vec_sum,
     mats_sum,
-    third_sum,
-    out_sum,
     w_s,
     gin_s,
     gin_u,
     vec_s,
     vec_other,
     vec_parts,
-    l_stage,
-    l_near,
     v_stage,
     v_near,
-    l_far,
-    l_end,
     v_far,
     v_parts,
     v_end,
     m_end,
-    t_end,
-    o_end,
     w_sem,
     gin_sems,
     vec_sems,
-    sems_l,
     sems_v,
     sems_m,
-    sems_t,
-    sems_o,
+    *role,
 ):
     width = base_ref.shape[1]
     steps = base_ref.shape[0] // ROWS
@@ -1481,23 +1566,42 @@
     block_rows = sum_ref.shape[0]
     half = pl.ds(pl.multiple_of(core * 2 * width, 2 * width), 2 * width)
 
-    def part(kz, kf, kg):
-        rows = pl.ds(pl.multiple_of(place.block(kz, kf, kg) * block_rows, block_rows), block_rows)
-        return jnp.dot(ht_ref[rows], dpre_ref[:, half], preferred_element_type=f32) + jnp.dot(
-            ht_other[rows], dpre_other[...], preferred_element_type=f32
-        )
-
-    matrix = FoldRole(place, part, l_stage, l_near, l_far, l_end, sems_l)
+    count = max(ROWS, block_rows // FOLDS)
+
+    def part(first):
+        def at(kz, kf, kg):
+            rows = pl.ds(pl.multiple_of(place.block(kz, kf, kg) * block_rows + first, count), count)
+            return jnp.dot(ht_ref[rows], dpre_ref[:, half], preferred_element_type=f32) + jnp.dot(
+                ht_other[rows], dpre_other[...], preferred_element_type=f32
+            )
+
+        return at
+
+    folds = [
+        FoldRole(place, part(n * count), stage, near, far, end, sems)
+        for n, (stage, near, far, end, sems) in enumerate(zip(*(role[k::5] for k in range(5))))
+    ]
+    lines = list(reversed(range(place.line)))
+    items = [(fold, kz) for kz in lines for fold in folds]
     mats = FoldLine(place, mats_part, m_end, sems_m)
-    third = FoldLine(place, third_part, t_end, sems_t)
-    outs = FoldLine(place, out_part, o_end, sems_o)
-    matrix.stage_a()
+    done = 0
+
+    def advance(until):
+        for n in range(done, until):
+            if n < len(items):
+                items[n][0].stage_a(items[n][1])
+            if 0 <= n - LAG < len(items):
+                items[n - LAG][0].stage_b(items[n - LAG][1])
+            if 0 <= n - LAST_LAG < len(items):
+                items[n - LAST_LAG][0].stage_c(items[n - LAST_LAG][1])
+        return max(done, until)
+
+    done = advance(LAG + 1)
     mats.begin()
-    third.begin()
-    outs.begin()
 
     load.wait()
     gin_s[...] = contract(dpre_ref[...], w_s[...], 1, 1)
+    done = advance(LAG + 2)
     input_grad = gin_s[...]
     scaled = base_ref[...]
     vec_s[...] = dvec_ref[...]
@@ -1523,11 +1627,11 @@
             )
         )
 
-    turned = gin_s[...].reshape(steps, ROWS, width)
     half_batch = batch // 2
+    done = advance(LAG + 3)
     for u in range(batch):
         straight = outer_ref[u // half_batch, u % half_batch].astype(f32)
-        gin_u[u] = turned[:, u, :] + jnp.where(encoder, straight, 0.0)
+        gin_u[u] = gin_s[...].reshape(steps, ROWS, width)[:, u, :] + jnp.where(encoder, straight, 0.0)
     kept = pltpu.make_async_copy(gin_u, gin_ref, gin_sems.at[0])
     handed = remote(gin_u, gin_ref, gin_sems.at[1], gin_sems.at[2], (1 - core, place.chip + place.along[1]))
 
@@ -1556,22 +1660,17 @@
     vecs = Fold(place, lambda kz, kf, kg: vec_parts[place.block(kz, kf, kg)], v_stage, v_near, v_far, sems_v)
     vec_line = FoldLine(place, v_parts, v_end, sems_v)
     vecs.stage_a()
-    lines = list(reversed(range(place.line)))
-    matrix.stage_b(lines[0])
-    for n, kz in enumerate(lines[1:]):
-        if n == place.line // 2 - 1:
-            vecs.stage_b()
-        matrix.stage_b(kz)
-        matrix.stage_c(lines[n])
+    done = advance(len(items) - 2)
+    vecs.stage_b()
+    done = advance(len(items) + LAG)
     for n in lines:
         v_parts[n] = vecs.summed(n)
     vec_line.begin()
-    matrix.stage_c(lines[-1])
+    done = advance(len(items) + LAST_LAG)
     mats_sum[...] = mats.result()
-    third_sum[...] = third.result()
-    out_sum[...] = outs.result()
     vec_sum[...] = vec_line.result()
-    matrix.result(sum_ref)
+    for n, fold in enumerate(folds):
+        fold.result(sum_ref.at[n * count : (n + 1) * count])
 
     @pl.when(mine)
     def _():
@@ -1582,17 +1681,17 @@
         handed.wait()
 
     trade.wait_send()
-    for fold in (matrix, vecs, vec_line, mats, third, outs):
+    for fold in (*folds, vecs, vec_line, mats):
         fold.sent_all()
 
 
-def update(n_dp, batch, ht, ht_other, dpre, dpre_other, weight, base, spread, outer, vectors, dvec, *parts):
+def update(n_dp, batch, ht, ht_other, dpre, dpre_other, weight, base, spread, outer, vectors, dvec, mats_part):
     rows, width = base.shape
     steps = rows // ROWS
     low, f32 = jnp.bfloat16, jnp.float32
     line, side = DP_LAYOUTS[n_dp][:2]
     block_rows = 2 * width // n_dp
-    block = (block_rows, 2 * width)
+    block = (max(ROWS, block_rows // FOLDS), 2 * width)
     dma = pltpu.SemaphoreType.DMA
     return pl.pallas_call(
         functools.partial(update_kernel, n_dp, batch),
@@ -1600,10 +1699,10 @@
             jax.ShapeDtypeStruct((block_rows, 4 * width), f32),
             jax.ShapeDtypeStruct((batch, steps, width), f32),
             jax.ShapeDtypeStruct((8, LANES), f32),
-        )
-        + tuple(jax.ShapeDtypeStruct(part.shape[1:], f32) for part in parts),
-        in_specs=[VMEM_SPEC] * 4 + [ANY_SPEC] + [VMEM_SPEC] * 8,
-        out_specs=(VMEM_SPEC, ANY_SPEC) + (VMEM_SPEC,) * 4,
+            jax.ShapeDtypeStruct(mats_part.shape[1:], f32),
+        ),
+        in_specs=[VMEM_SPEC] * 4 + [ANY_SPEC] + [VMEM_SPEC] * 6,
+        out_specs=(VMEM_SPEC, ANY_SPEC) + (VMEM_SPEC,) * 2,
         scratch_shapes=[
             pltpu.VMEM((width, 4 * width), low),
             pltpu.VMEM((rows, width), f32),
@@ -1612,22 +1711,28 @@
             pltpu.VMEM((8, width), f32),
             pltpu.VMEM((n_dp, 8, LANES), f32),
         ]
-        + fold_buffers(line, side, block, low)
         + fold_buffers(line, side, (8, LANES), f32)
         + [
-            pltpu.VMEM((side - 1, line) + block, low),
-            pltpu.VMEM((2, line // 2) + block, low),
             pltpu.VMEM((side - 1, line, 8, LANES), f32),
             pltpu.VMEM((line, 8, LANES), f32),
             pltpu.VMEM((line - 1, 8, LANES), f32),
+            pltpu.VMEM((line - 1,) + mats_part.shape[1:], low),
         ]
-        + [pltpu.VMEM((line - 1,) + part.shape[1:], low) for part in parts]
         + [dma, dma((3,)), dma((2,))]
-        + [fold_sems(line, side)] * 5,
+        + [fold_sems(line, side)] * 2
+        + (
+            fold_buffers(line, side, block, low)
+            + [
+                pltpu.VMEM((side - 1, line) + block, low),
+                pltpu.VMEM((2, line // 2) + block, low),
+                fold_sems(line, side),
+            ]
+        )
+        * (block_rows // block[0]),
         compiler_params=pltpu.CompilerParams(
             collective_id=4, has_side_effects=True, vmem_limit_bytes=VMEM_LIMIT
         ),
-    )(ht, ht_other, dpre, dpre_other, weight, base, spread, outer, vectors, dvec, *parts)
+    )(ht, ht_other, dpre, dpre_other, weight, base, spread, outer, vectors, dvec, mats_part)
 
 
 STEP = 5
@@ -1688,19 +1793,21 @@
     mats_block = jnp.swapaxes(mats_copy, 1, 2)
     out_block = jnp.pad(out_copy, ((0, 0), (0, vocab_pad - vocab_half)))
     vec_block = jnp.pad(vec_master.astype(low).astype(f32), ((0, 0), (0, LANES - piece)))
-    act, cell, ht, base, spread, vectors, pair, weight, weight_t, pairs, third_line, out_line = forward(
+    act, cell, ht, base, spread, vectors, pair, weight, weight_t, pairs, third, outs = forward(
         n_dp, inputs[0], lstm_copy[0], mats_block, out_block, vec_block
     )
     memory, decoded = pair.reshape(2, half * length, model_width)
     pairs = pairs.reshape(2, 2 * model_width, model_width)
-    dz, dq, dk, vec_rows, logits, outer, third_part, out_part = attention(
-        n_dp, frames, labels, memory, decoded, cotangent, vectors, pairs, third_line, out_line
+    third = third.reshape(2, model_width, model_width)
+    outs = outs.reshape(2, model_width, vocab_pad)
+    dz, dq, dk, vec_rows, logits, outer, third_half, out_half = attention(
+        n_dp, frames, labels, memory, decoded, cotangent, vectors, pairs, third, outs
     )
     logits = logits.reshape(batch_size, length, vocab_pad)[..., :vocab_half]
-    dpre, dpre_other, ht_other, mats_part = backward(
-        n_dp, act, cell, outer, dq, dk, decoded, memory, weight_t, ht
-    )
-    lstm_sum, inputs_grad, vec_sum, mats_sum, third_sum, out_sum = update(
+    dpre, dpre_other, ht_other, mats_part, third_sum, out_sum = backward(
+        n_dp, act, cell, outer, dq, dk, decoded, memory, third_half, out_half, weight_t, ht
+    )
+    lstm_sum, inputs_grad, vec_sum, mats_sum = update(
         n_dp,
         batch_size,
         ht,
@@ -1714,8 +1821,6 @@
         vectors,
         vec_rows,
         mats_part,
-        third_part,
-        out_part,
     )
     mats_sum = jnp.concatenate([mats_sum.reshape(2, -1, model_width), third_sum[None]], 0)
     mats_sum = jnp.swapaxes(mats_sum, 1, 2)

time: 431 us -> 384 us (0.89)
  Pallas kernels: 403 us -> 356 us
    pallas_call x1, Pallas kernels: 87.2 us -> 57.1 us  [attention(): pl.pallas_call(functools.partial(attention_kernel, n_dp), out_shape=(jax....]
    pallas_call x1, Pallas kernels: 104 us -> 88.3 us  [update(): pl.pallas_call(functools.partial(update_kernel, n_dp, batch), out_shape=(...]
    pallas_call x1, Pallas kernels: 154 us -> 149 us  [forward(): pl.pallas_call(functools.partial(forward_kernel, n_dp), out_shape=(jax.Sh...]
  transfers between devices with their start and end apart: 1 -> 1, of which waited for: 0 -> 0; matrix products, arithmetic and copies ran while one was open for 1% -> 1% of each run, Pallas kernels for 36% -> 40%
where the time goes in v5:
time: 384 us; the launch traced here: 377 us
  Pallas kernels  356 us (93%)
  other arithmetic  14 us (4%)
  local copies, waits for them, and re-layouts  5.19 us (1%)
    pallas_call x1, Pallas kernels, forward(): pl.pallas_call(functools.partial(forward_kernel, n_dp), out_shape=(jax.Sh...  149 us
    pallas_call x1, Pallas kernels, update(): pl.pallas_call(functools.partial(update_kernel, n_dp, batch), out_shape=(...  88.3 us
    pallas_call x1, Pallas kernels, backward(): pl.pallas_call(functools.partial(backward_kernel, n_dp), out_shape=(jax.S...  61.9 us
    pallas_call x1, Pallas kernels, attention(): pl.pallas_call(functools.partial(attention_kernel, n_dp), out_shape=(jax....  57.1 us
  transfers between devices with their start and end apart: 1, of which 0 were waited for; matrix products, arithmetic and copies ran while one was open for 1% of the time, Pallas kernels for 40%

profile of v5, /device:TPU:0, one launch (start us, length us, event | category | flops | bytes accessed | tf_op | source)
XLA Modules:
  0.0 377.4 jit_solution(7683566676054510197)
XLA Ops:
  0.7 0.0 copy-start.13
  0.7 0.8 fusion.6
  1.5 0.5 collective-permute-start
  1.9 0.7 convert_element_type.17
  2.6 0.6 pad_convert_fusion.vec_ref
  3.2 1.5 pad.10.out_ref
  4.7 149.1 %shard_map.305 = (f32[384,4096]{1,0:T(8,128)}, f32[400,1024]{1,0:T(8,128)}, bf16[2048,384]{1,0:T(8,128)(2,1)}, f32[24,16,1024]{2,1,0:T(8,128)}, f32[24,16,128]{2...) custom-call(bf16[12,24,1024]{2,1,0:T(8,128)(2,1)} %bitcast.49, ...), custom_call_target="tpu_custom_call" | custom-call | tf_op jit(solution)/shard_map/pallas_call | solution.py:574
  153.8 1.9 fusion.14
  155.7 0.0 collective-permute-done
  155.7 0.0 copy-done.13
  155.7 0.6 broadcast_select_fusion.2
  156.3 57.1 %shard_map.306 = (bf16[144,1024]{1,0:T(8,128)(2,1)}, bf16[2,144,1024]{2,1,0:T(8,128)(2,1)}, bf16[2,144,1024]{2,1,0:T(8,128)(2,1)}, f32[8,2048]{1,0:T(8,128)}, bf...) custom-call(s32[6]{0:T(128)} %get-tuple-element.93.frames_ref, ...), custom_call_target="tpu_custom_call" | custom-call | tf_op jit(solution)/shard_map/pallas_call | solution.py:1241
  213.4 61.9 %shard_map.307 = (bf16[384,4096]{1,0:T(8,128)(2,1)}, bf16[384,2048]{1,0:T(8,128)(2,1)}, bf16[2048,384]{1,0:T(8,128)(2,1)}, bf16[4,128,1024]{2,1,0:T(8,128)(2,1)}, f32[64,1024]{1,0:T(8,128)}, /*index=5*/f32[64,512]{1,0:T(8,128)}) custom-call(f32[400,1024]{1,0:T(8,128)} %get-tuple-element.53.cell_ref, bf16[2,6,24,1024]{3,2,1,0:T(8,128)(2,1)} %get-tuple-element.54.outer_ref, ...), custom_call_target="tpu_custom_call" | custom-call | tf_op jit(solution)/shard_map/pallas_call | solution.py:1483
  275.3 0.0 copy-start.12
  275.3 0.0 copy-start.14
  275.3 0.0 copy-start.15
  275.3 0.0 copy-start.8
  275.4 0.0 copy-start.9
  275.4 0.0 copy-start.10
  275.4 0.0 copy-start.11
  275.4 0.0 copy-start
  275.4 88.3 %shard_map.308 = (f32[128,4096]{1,0:T(8,128)}, f32[12,24,1024]{2,1,0:T(8,128)}, f32[8,128]{1,0:T(8,128)}, f32[128,1024]{1,0:T(8,128)}) custom-call(bf16[2048,384]{1,0:T(8,128)(2,1)} %get-tuple-element.52.ht_ref, bf16[2048,384]{1,0:T(8,128)(2,1)} %get-tuple-element.61.ht_other, bf16[384,4096]{1,0:T(8,128)(2,1)} %get-tuple-element.62.dpre_ref, ...), custom_call_target="tpu_custom_call" | custom-call | tf_op jit(solution)/shard_map/pallas_call | solution.py:1696
  363.7 0.0 copy-done.12
  363.7 0.0 copy-done.14
  363.8 1.3 multiply_subtract_fusion.3
  365.1 0.0 copy-done.11
  365.1 0.8 fusion.8
  365.9 7.3 %fusion.12 = (bf16[1,128,4096]{2,1,0:T(8,128)(2,1)}, f32[1,128,4096]{2,1,0:T(8,128)}, f32[1,128,4096]{2,1,0:T(8,128)}, f32[1,128,4096]{2,1,0:T(8,128)}) fusion(f32[1,128,4096]{2,1,0:T(8,128)S(1)} %copy-done, f32[128,4096]{1,0:T(8,128)} %get-tuple-element.70, f32[1,128,4096]{2,1,0:T(8,128)} %param.23, f32[1,128,4096]{2,1,0:T(8,128)} %param.24), kind=kLoop, calls=%fused_computation.27 | loop fusion | flops 8388608 | bytes 15728640 | tf_op jit(solution)/shard_map/convert_element_type | solution.py:1845
  373.2 0.0 copy-done.2
  373.3 2.0 fusion.10
  375.2 0.7 copy.37
  375.9 1.0 copy.38
  (18 shorter events, 0.0 us)
Async XLA Ops:
  0.7 155.1 %copy-start.13 = (s32[1,12]{1,0:T(1,128)S(1)}, s32[1,12]{1,0:T(1,128)}, u32[]{:S(2)}) copy-start(s32[1,12]{1,0:T(1,128)} %param.19) | copy-start | bytes 148
  1.5 154.2 %collective-permute-start = (s32[6]{0:T(128)S(1)}, s32[6]{0:T(128)S(1)}, u32[]{:S(2)}, u32[]{:S(2)}) collective-permute-start(s32[6]{0:T(128)S(1)} %fusion.6), channel_id=1, source_target_pairs={{0,16},{16,0},{1,17},{17,1},{2,18},{18,2},{3,19},{19,3},{4,20},{20... | collective-permute-start | bytes 80 | tf_op jit(solution)/shard_map/ppermute | solution.py:1790
  275.3 88.4 %copy-start.12 = (f32[8,64]{1,0:T(8,128)S(1)}, f32[8,64]{1,0:T(8,128)}, u32[]{:S(2)}) copy-start(f32[8,64]{1,0:T(8,128)} %param.33) | copy-start | bytes 6148
  275.3 88.4 %copy-start.14 = (f32[8,64]{1,0:T(8,128)S(1)}, f32[8,64]{1,0:T(8,128)}, u32[]{:S(2)}) copy-start(f32[8,64]{1,0:T(8,128)} %param.34) | copy-start | bytes 6148
  275.3 88.4 %copy-start.15 = (f32[8,64]{1,0:T(8,128)S(1)}, f32[8,64]{1,0:T(8,128)}, u32[]{:S(2)}) copy-start(f32[8,64]{1,0:T(8,128)} %param.35) | copy-start | bytes 6148
  275.3 89.7 %copy-start.8 = (f32[64,500]{1,0:T(8,128)S(1)}, f32[64,500]{1,0:T(8,128)}, u32[]{:S(2)}) copy-start(f32[64,500]{1,0:T(8,128)} %param.29) | copy-start | bytes 384004
  275.4 89.7 %copy-start.9 = (f32[64,500]{1,0:T(8,128)S(1)}, f32[64,500]{1,0:T(8,128)}, u32[]{:S(2)}) copy-start(f32[64,500]{1,0:T(8,128)} %param.31) | copy-start | bytes 384004
  275.4 89.7 %copy-start.10 = (f32[64,500]{1,0:T(8,128)S(1)}, f32[64,500]{1,0:T(8,128)}, u32[]{:S(2)}) copy-start(f32[64,500]{1,0:T(8,128)} %param.32) | copy-start | bytes 384004
  275.4 89.7 %copy-start.11 = (f32[64,512]{1,0:T(8,128)S(1)}, f32[64,512]{1,0:T(8,128)}, u32[]{:S(2)}) copy-start(f32[64,512]{1,0:T(8,128)} %get-tuple-element.73) | copy-start | bytes 393220
  275.4 90.5 %copy-start = (f32[1,128,4096]{2,1,0:T(8,128)S(1)}, f32[1,128,4096]{2,1,0:T(8,128)}, u32[]{:S(2)}) copy-start(f32[1,128,4096]{2,1,0:T(8,128)} %param.21) | copy-start | bytes 6291460
  365.9 7.3 %copy-start.2 = (f32[3,1024,64]{1,2,0:T(8,128)S(1)}, f32[3,1024,64]{1,2,0:T(8,128)}, u32[]{:S(2)}) copy-start(f32[3,1024,64]{1,2,0:T(8,128)} %param.25) | copy-start | bytes 2359300
  365.9 7.3 %copy-start.3 = (f32[3,1024,64]{1,2,0:T(8,128)S(1)}, f32[3,1024,64]{1,2,0:T(8,128)}, u32[]{:S(2)}) copy-start(f32[3,1024,64]{1,2,0:T(8,128)} %param.27) | copy-start | bytes 2359300
  365.9 7.3 %copy-start.4 = (f32[3,1024,64]{1,2,0:T(8,128)S(1)}, f32[3,1024,64]{1,2,0:T(8,128)}, u32[]{:S(2)}) copy-start(f32[3,1024,64]{1,2,0:T(8,128)} %param.28) | copy-start | bytes 2359300
  365.9 7.3 %copy-start.5 = (f32[128,1024]{1,0:T(8,128)S(1)}, f32[128,1024]{1,0:T(8,128)}, u32[]{:S(2)}) copy-start(f32[128,1024]{1,0:T(8,128)} %get-tuple-element.71) | copy-start | bytes 1572868
  365.9 7.3 %copy-start.7 = (f32[64,1024]{1,0:T(8,128)S(1)}, f32[64,1024]{1,0:T(8,128)}, u32[]{:S(2)}) copy-start(f32[64,1024]{1,0:T(8,128)} %get-tuple-element.72) | copy-start | bytes 786436
  373.2 2.0 copy-start.6
  373.2 2.7 copy-start.1

commit v6 on v5

--- a/solution.py
+++ b/solution.py
@@ -343,8 +343,8 @@
     seq_ref,
     shard_ref,
     mats_ref,
-    out_ref,
-    vec_ref,
+    out_part,
+    vec_part,
     act_out,
     cell_ref,
     ht_ref,
@@ -357,6 +357,8 @@
     mats_out,
     third_out,
     out_out,
+    out_ref,
+    vec_ref,
     act_ref,
     seq_s,
     result_s,
@@ -382,6 +384,11 @@
     mine = core == place.role
     guest = jnp.logical_not(mine)
     encoder = place.role == 0
+    piece = vec_part.shape[1]
+    vec_ref[...] = jnp.zeros_like(vec_ref)
+    vec_ref[:, :piece] = vec_part[...].astype(low).astype(f32)
+    out_ref[...] = jnp.zeros_like(out_ref)
+    out_ref[:, : out_part.shape[1]] = out_part[...]
     place.greet()
     rows = shard_ref.shape[0]
     count = max(ROWS, rows // CHUNKS)
@@ -435,7 +442,6 @@
         spread_ref[:, u, :] = jnp.broadcast_to(spread, (steps, LANES))
     vecs.stage_three()
     vecs.finish()
-    piece = 2 * width // (2 * n_dp)
     per_tile = LANES // piece
     for m in range(2 * width // LANES):
         tile = jnp.zeros((8, LANES), f32)
@@ -570,6 +576,7 @@
     low, f32 = jnp.bfloat16, jnp.float32
     line, side = DP_LAYOUTS[n_dp][:2]
     columns = mats_block.shape[1]
+    out_shape = (out_block.shape[0], -(-out_block.shape[1] // LANES) * LANES)
     dma = pltpu.SemaphoreType.DMA
     return pl.pallas_call(
         functools.partial(forward_kernel, n_dp),
@@ -585,11 +592,13 @@
             jax.ShapeDtypeStruct((4, width, width), low),
             jax.ShapeDtypeStruct((2, 2, n_dp, columns, width), low),
             jax.ShapeDtypeStruct((2, n_dp, columns, width), low),
-            jax.ShapeDtypeStruct((2, n_dp) + out_block.shape, low),
+            jax.ShapeDtypeStruct((2, n_dp) + out_shape, low),
         ),
-        in_specs=[VMEM_SPEC, ANY_SPEC, ANY_SPEC, ANY_SPEC, VMEM_SPEC],
+        in_specs=[VMEM_SPEC, ANY_SPEC, ANY_SPEC, VMEM_SPEC, VMEM_SPEC],
         out_specs=(ANY_SPEC,) + (VMEM_SPEC,) * 6 + (ANY_SPEC,) * 5,
         scratch_shapes=[
+            pltpu.VMEM(out_shape, low),
+            pltpu.VMEM((8, LANES), f32),
             pltpu.VMEM((rows, 4 * width), f32),
             pltpu.VMEM((batch, steps, width), low),
             pltpu.VMEM((batch, steps, width), low),
@@ -631,8 +640,11 @@
         for kz in steps or reversed(range(place.line)):
             for kg in range(1, place.side):
                 for kf in reversed(range(place.side)):
-                    source = self.stage.at[kg - 1, kf, kz]
-                    source[...] = self.part(kz, kf, kg).astype(source.dtype)
+                    if callable(self.stage):
+                        source = self.stage(kz, kf, kg)
+                    else:
+                        source = self.stage.at[kg - 1, kf, kz]
+                        source[...] = self.part(kz, kf, kg).astype(source.dtype)
                     self.send(
                         source,
                         self.near.at[kg - 1, kf, kz],
@@ -737,6 +749,69 @@
     def sent_all(self):
         for kz in range(1, self.place.line):
             self.copy(kz).wait_send()
+
+
+class FoldFirst(Fold):
+    def __init__(self, place, term, ends, near, far, sems):
+        super().__init__(place, None, term, near, far, sems)
+        self.ends = ends
+
+    def begin(self):
+        place = self.place
+        for kz in reversed(range(1, place.line)):
+            for kg in reversed(range(place.side)):
+                for kf in reversed(range(place.side)):
+                    self.send(
+                        self.stage(kz, kf, kg),
+                        self.ends.at[kz - 1, kg, kf],
+                        (place.core, place.chip + place.along[kz]),
+                        self.sems["ls"].at[kg, kf, kz],
+                        self.sems["lr"].at[kg, kf, kz],
+                    )
+
+    def stage_line(self):
+        place = self.place
+        for kg in reversed(range(place.side)):
+            for kf in reversed(range(place.side)):
+                total = self.stage(0, kf, kg)[...].astype(jnp.float32)
+                for kz in range(1, place.line):
+                    self.arrived(self.ends.at[kz - 1, kg, kf], self.sems["lr"].at[kg, kf, kz])
+                    total = total + self.ends[kz - 1, kg, kf].astype(jnp.float32)
+                source = self.ends.at[0, kg, kf]
+                source[...] = total.astype(source.dtype)
+                if kg:
+                    self.send(
+                        source,
+                        self.near.at[kg - 1, kf],
+                        (place.core, place.chip + place.second[kg]),
+                        self.sems["gs"].at[kg, kf, 0],
+                        self.sems["gr"].at[kg, kf, 0],
+                    )
+
+    def stage_second(self):
+        place = self.place
+        for kf in reversed(range(place.side)):
+            total = self.ends[0, 0, kf].astype(jnp.float32)
+            for kg in range(1, place.side):
+                self.arrived(self.near.at[kg - 1, kf], self.sems["gr"].at[kg, kf, 0])
+                total = total + self.near[kg - 1, kf].astype(jnp.float32)
+            source = self.near.at[0, kf]
+            source[...] = total.astype(source.dtype)
+            if kf:
+                self.send(
+                    source,
+                    self.far.at[kf - 1],
+                    (place.core, place.chip + place.first[kf]),
+                    self.sems["fs"].at[kf, 0],
+                    self.sems["fr"].at[kf, 0],
+                )
+
+    def result(self):
+        total = self.near[0, 0].astype(jnp.float32)
+        for kf in range(1, self.place.side):
+            self.arrived(self.far.at[kf - 1], self.sems["fr"].at[kf, 0])
+            total = total + self.far[kf - 1].astype(jnp.float32)
+        return total
 
 
 class FoldRole(Fold):
@@ -802,9 +877,10 @@
             self.cross.wait_send()
 
 
-def fold_sems(line, side):
+def fold_sems(line, side, first=False):
     dma = pltpu.SemaphoreType.DMA
-    return {
+    ends = {"ls": dma((side, side, line)), "lr": dma((side, side, line))}
+    return (ends if first else {}) | {
         "gs": dma((side, side, line)),
         "gr": dma((side, side, line)),
         "fs": dma((side, line)),
@@ -826,8 +902,7 @@
     n_dp,
     frames_ref,
     labels_ref,
-    mem_ref,
-    dec_ref,
+    pair_ref,
     cot_ref,
     vec_ref,
     pairs_any,
@@ -889,6 +964,7 @@
     sems_ft,
     sems_fo,
 ):
+    mem_ref, dec_ref = pair_ref.at[0], pair_ref.at[1]
     rows, width = dec_ref.shape
     utts = frames_ref.shape[0]
     length = rows // utts
@@ -1226,8 +1302,8 @@
         moved.sent_all()
 
 
-def attention(n_dp, frames, labels, memory, decoded, cotangent, vectors, pairs, third, outs):
-    rows, width = decoded.shape
+def attention(n_dp, frames, labels, pair, cotangent, vectors, pairs, third, outs):
+    rows, width = pair.shape[1:]
     utts = frames.shape[0]
     length = rows // utts
     low, f32 = jnp.bfloat16, jnp.float32
@@ -1250,7 +1326,7 @@
             jax.ShapeDtypeStruct((side, line) + third_block, low),
             jax.ShapeDtypeStruct((side, line) + out_block, low),
         ),
-        in_specs=[SMEM_SPEC] * 2 + [VMEM_SPEC] * 4 + [ANY_SPEC] * 3,
+        in_specs=[SMEM_SPEC] * 2 + [VMEM_SPEC] * 3 + [ANY_SPEC] * 3,
         out_specs=(VMEM_SPEC,) * 8,
         scratch_shapes=[
             pltpu.VMEM((rows, width), low),
@@ -1303,81 +1379,117 @@
         compiler_params=pltpu.CompilerParams(
             collective_id=2, has_side_effects=True, vmem_limit_bytes=VMEM_LIMIT
         ),
-    )(frames, labels, memory, decoded, cotangent, vectors, pairs, third, outs)
+    )(frames, labels, pair, cotangent, vectors, pairs, third, outs)
 
 
 def backward_kernel(
     n_dp,
     cell_ref,
     outer_ref,
-    dq_ref,
-    dk_ref,
-    dec_ref,
-    mem_ref,
+    pair_ref,
     third_half,
     out_half,
+    spread_ref,
+    vectors_ref,
+    dvec_ref,
+    dq_any,
+    dk_any,
     act_any,
     wt_any,
-    ht_ref,
-    dpre_ref,
-    dpre_other,
-    ht_other,
-    mats_part,
+    ht_any,
+    w_any,
+    base_any,
+    sum_ref,
+    gin_ref,
+    vec_sum,
+    mats_sum,
     third_sum,
     out_sum,
     act_ref,
     wt_ref,
+    ht_ref,
+    ht_other,
+    dpre_ref,
+    dpre_other,
     outer_s,
     state,
     held,
     facts,
+    own,
     g_mats,
-    m_stage,
+    k_ends,
+    k_near,
+    k_far,
     m_near,
     m_far,
+    m_parts,
+    m_end,
     t_far,
     t_parts,
     t_end,
     o_far,
     o_parts,
     o_end,
+    vec_s,
+    vec_other,
+    vec_parts,
+    v_stage,
+    v_near,
+    v_far,
+    v_parts,
+    v_end,
     load_sem,
     fact_sems,
     pre_sems,
     ht_sems,
+    gin_sems,
+    vec_sems,
+    sems_k,
     sems_m,
     sems_t,
     sems_o,
+    sems_v,
+    *role,
 ):
-    halves, half, steps, width = outer_ref.shape
+    halves, half_batch, steps, width = outer_ref.shape
+    batch = halves * half_batch
     low, f32 = jnp.bfloat16, jnp.float32
+    mem_ref, dec_ref = pair_ref.at[0], pair_ref.at[1]
     place = Place(n_dp)
     loads = [
         pltpu.make_async_copy(act_any, act_ref, load_sem.at[0]),
         pltpu.make_async_copy(wt_any, wt_ref, load_sem.at[1]),
+        pltpu.make_async_copy(ht_any, ht_ref, load_sem.at[2]),
     ]
-    for load in loads:
+    core = place.core
+    own_loads = [
+        pltpu.make_async_copy(source.at[core], own.at[n], load_sem.at[8 + n])
+        for n, source in enumerate((dq_any, dk_any))
+    ]
+    for load in own_loads + loads:
         load.start()
     place.greet()
-    core = place.core
+    other = (1 - core, place.chip)
+    encoder = place.role == 0
+    mine = core == place.role
     third, outs = FoldRest(place, third_half, t_far, sems_t), FoldRest(place, out_half, o_far, sems_o)
     third_line, out_line = FoldLine(place, t_parts, t_end, sems_t), FoldLine(place, o_parts, o_end, sems_o)
+    mats_line = FoldLine(place, m_parts, m_end, sems_m)
     third.begin()
     outs.begin()
-    other = (1 - core, place.chip)
-    sources = [dq_ref.at[1 - core], dk_ref.at[1 - core], dec_ref, mem_ref]
+    sources = [dq_any.at[1 - core], dk_any.at[1 - core], dec_ref, mem_ref]
     handed = [
         remote(source, facts.at[n], fact_sems.at[0, n], fact_sems.at[1, n], other)
         for n, source in enumerate(sources)
     ]
-    handed.append(remote(ht_ref, ht_other, ht_sems.at[0], ht_sems.at[1], other))
+    handed.append(remote(ht_any, ht_other, ht_sems.at[0], ht_sems.at[1], other))
     for copy in handed:
         copy.start()
     state[...] = jnp.zeros_like(state)
     held[...] = jnp.zeros_like(held)
-    outer_s[:, halves * half :] = jnp.zeros((steps, ROWS - halves * half, width), f32)
-    for u in range(halves * half):
-        outer_s[:, u, :] = outer_ref[u // half, u % half].astype(f32)
+    outer_s[:, batch:] = jnp.zeros((steps, ROWS - batch, width), f32)
+    for u in range(batch):
+        outer_s[:, u, :] = outer_ref[u // half_batch, u % half_batch].astype(f32)
 
     def step(k, carry):
         t = steps - 1 - k
@@ -1421,30 +1533,39 @@
         copy.start()
         handed.append(copy)
 
-    part_rows = g_mats.shape[1] // 2
+    part_rows = g_mats.shape[2]
 
     def matrices():
         for copy in handed[:4]:
             copy.wait_recv()
+        for load in own_loads:
+            load.wait()
         pairs = [
-            (dq_ref[core], dec_ref[...], facts[0], facts[2]),
-            (dk_ref[core], mem_ref[...], facts[1], facts[3]),
+            (own[0], dec_ref[...], facts[0], facts[2]),
+            (own[1], mem_ref[...], facts[1], facts[3]),
         ]
         for m, (a, b, c, d) in enumerate(pairs):
             total = (contract(a, b, 0, 0) + contract(c, d, 0, 0)).astype(low)
             for block in range(n_dp):
-                g_mats[block, m * part_rows : (m + 1) * part_rows] = total[
-                    block * part_rows : (block + 1) * part_rows
-                ]
+                g_mats[m, block] = total[block * part_rows : (block + 1) * part_rows]
 
     mats = Fold(
-        place, lambda kz, kf, kg: g_mats[place.block(kz, kf, kg)].astype(f32), m_stage, m_near, m_far, sems_m
-    )
+        place,
+        lambda kz, kf, kg: g_mats[0, place.block(kz, kf, kg)].astype(f32),
+        lambda kz, kf, kg: g_mats.at[0, place.block(kz, kf, kg)],
+        m_near,
+        m_far,
+        sems_m,
+    )
+    keys = FoldFirst(
+        place, lambda kz, kf, kg: g_mats.at[1, place.block(kz, kf, kg)], k_ends, k_near, k_far, sems_k
+    )
+    lines = list(reversed(range(place.line)))
     matrices()
+    keys.begin()
     mats.stage_a()
     for load in loads:
         load.wait()
-    lines = list(reversed(range(place.line)))
     lax.fori_loop(0, share, step, 0)
     hand_over(0)
     for kz in lines:
@@ -1457,115 +1578,19 @@
     mats.stage_b(*lines[: place.line // 2])
     lax.fori_loop(2 * share, 3 * share, step, 0)
     hand_over(2)
-    mats.stage_b(*lines[place.line // 2 :])
     lax.fori_loop(3 * share, steps, step, 0)
     hand_over(3)
-    for kz in lines:
-        mats_part[kz] = mats.summed(kz)
-    third_sum[...] = third_line.result()
-    out_sum[...] = out_line.result()
-    for copy in handed[4:]:
-        copy.wait_recv()
-    for copy in handed:
-        copy.wait_send()
-    for fold in (mats, third, outs, third_line, out_line):
-        fold.sent_all()
-
-
-def backward(n_dp, act, cell, outer, dq, dk, decoded, memory, third_half, out_half, weight_t, ht):
-    rows = act.shape[0]
-    steps, width = outer.shape[2:]
-    low, f32 = jnp.bfloat16, jnp.float32
-    line, side = DP_LAYOUTS[n_dp][:2]
-    utt_rows = decoded.shape[0]
-    mats_block = (2 * width // n_dp, width)
-    dma = pltpu.SemaphoreType.DMA
-    return pl.pallas_call(
-        functools.partial(backward_kernel, n_dp),
-        out_shape=(
-            jax.ShapeDtypeStruct((rows, 4 * width), low),
-            jax.ShapeDtypeStruct((rows, 2 * width), low),
-            jax.ShapeDtypeStruct(ht.shape, low),
-            jax.ShapeDtypeStruct((line,) + mats_block, low),
-            jax.ShapeDtypeStruct(third_half.shape[2:], f32),
-            jax.ShapeDtypeStruct(out_half.shape[2:], f32),
-        ),
-        in_specs=[VMEM_SPEC] * 8 + [ANY_SPEC] * 3,
-        out_specs=(VMEM_SPEC, VMEM_SPEC, ANY_SPEC) + (VMEM_SPEC,) * 3,
-        scratch_shapes=[
-            pltpu.VMEM((rows, 4 * width), f32),
-            pltpu.VMEM((4, width, width), low),
-            pltpu.VMEM((steps, ROWS, width), f32),
-            pltpu.VMEM((ROWS, 4 * width), low),
-            pltpu.VMEM((ROWS, width), f32),
-            pltpu.VMEM((4, utt_rows, width), low),
-            pltpu.VMEM((n_dp,) + mats_block, low),
-        ]
-        + fold_buffers(line, side, mats_block, low)
-        + [pltpu.VMEM((side - 1, line) + mats_block, low)]
-        + [
-            pltpu.VMEM(count + block, low)
-            for block in (third_half.shape[2:], out_half.shape[2:])
-            for count in ((side - 1, line), (line,), (line - 1,))
-        ]
-        + [dma((2,)), dma((2, 4)), dma((2, 4)), dma((2,))]
-        + [fold_sems(line, side)] * 3,
-        compiler_params=pltpu.CompilerParams(
-            collective_id=3, has_side_effects=True, vmem_limit_bytes=VMEM_LIMIT
-        ),
-    )(cell, outer, dq, dk, decoded, memory, third_half, out_half, act, weight_t, ht)
-
-
-def update_kernel(
-    n_dp,
-    batch,
-    ht_ref,
-    ht_other,
-    dpre_ref,
-    dpre_other,
-    w_ref,
-    base_ref,
-    spread_ref,
-    outer_ref,
-    vectors_ref,
-    dvec_ref,
-    mats_part,
-    sum_ref,
-    gin_ref,
-    vec_sum,
-    mats_sum,
-    w_s,
-    gin_s,
-    gin_u,
-    vec_s,
-    vec_other,
-    vec_parts,
-    v_stage,
-    v_near,
-    v_far,
-    v_parts,
-    v_end,
-    m_end,
-    w_sem,
-    gin_sems,
-    vec_sems,
-    sems_v,
-    sems_m,
-    *role,
-):
-    width = base_ref.shape[1]
-    steps = base_ref.shape[0] // ROWS
-    low, f32 = jnp.bfloat16, jnp.float32
-    place = Place(n_dp)
-    load = pltpu.make_async_copy(w_ref, w_s, w_sem)
-    load.start()
-    place.greet()
-    core = place.core
-    encoder = place.role == 0
-    mine = core == place.role
+
+    late = [pltpu.make_async_copy(base_any, act_ref.at[:, :width], load_sem.at[3])]
+    for q in range(4):
+        late.append(
+            pltpu.make_async_copy(w_any.at[:, q * width : (q + 1) * width], wt_ref.at[q], load_sem.at[4 + q])
+        )
+    for load in late:
+        load.start()
+    base_columns, gin_columns = slice(0, width), slice(width, 2 * width)
     block_rows = sum_ref.shape[0]
     half = pl.ds(pl.multiple_of(core * 2 * width, 2 * width), 2 * width)
-
     count = max(ROWS, block_rows // FOLDS)
 
     def part(first):
@@ -1581,9 +1606,7 @@
         FoldRole(place, part(n * count), stage, near, far, end, sems)
         for n, (stage, near, far, end, sems) in enumerate(zip(*(role[k::5] for k in range(5))))
     ]
-    lines = list(reversed(range(place.line)))
     items = [(fold, kz) for kz in lines for fold in folds]
-    mats = FoldLine(place, mats_part, m_end, sems_m)
     done = 0
 
     def advance(until):
@@ -1596,44 +1619,55 @@
                 items[n - LAST_LAG][0].stage_c(items[n - LAST_LAG][1])
         return max(done, until)
 
+    for copy in handed[4:]:
+        copy.wait_recv()
+    done = advance(LAG)
+    mats.stage_b(*lines[place.line // 2 :])
     done = advance(LAG + 1)
-    mats.begin()
-
-    load.wait()
-    gin_s[...] = contract(dpre_ref[...], w_s[...], 1, 1)
+    for load in late:
+        load.wait()
+    chunks = [slice(at, at + LANES) for at in range(0, steps * ROWS, LANES)]
+    for rows in chunks:
+        act_ref[rows, gin_columns] = contract(dpre_ref[rows, :width], wt_ref[0], 1, 1)
+        for q in range(1, 4):
+            act_ref[rows, gin_columns] += contract(dpre_ref[rows, q * width : (q + 1) * width], wt_ref[q], 1, 1)
     done = advance(LAG + 2)
-    input_grad = gin_s[...]
-    scaled = base_ref[...]
+    for kz in lines:
+        m_parts[kz] = mats.summed(kz)
+    mats_line.begin()
     vec_s[...] = dvec_ref[...]
-    vec_s[4:5, :width] = jnp.where(encoder, jnp.sum(input_grad * scaled, 0, keepdims=True), 0.0)
-    vec_s[4:5, width:] = jnp.where(encoder, jnp.sum(input_grad, 0, keepdims=True), 0.0)
+    vec_s[4:5] = jnp.zeros((1, 2 * width), f32)
+    for rows in chunks:
+        input_grad = jnp.where(encoder, act_ref[rows, gin_columns], 0.0)
+        vec_s[4:5, :width] += jnp.sum(input_grad * act_ref[rows, base_columns], 0, keepdims=True)
+        vec_s[4:5, width:] += jnp.sum(input_grad, 0, keepdims=True)
     for q in range(4):
         columns = slice((q % 2) * width, (q % 2 + 1) * width)
         bias = jnp.sum(dpre_ref[:, q * width : (q + 1) * width].astype(f32), 0, keepdims=True)
-        for role in range(2):
-            row = 2 * role + q // 2
-            vec_s[row : row + 1, columns] = jnp.where(place.role == role, bias, 0.0)
+        for role_index in range(2):
+            row = 2 * role_index + q // 2
+            vec_s[row : row + 1, columns] = jnp.where(place.role == role_index, bias, 0.0)
 
     @pl.when(encoder)
     def _():
-        grads = gin_s[...] * vectors_ref[4:5, :width]
-        values = base_ref[...]
-        gin_s[...] = (
-            spread_ref[:, :1]
-            * (
+        for rows in chunks:
+            grads = act_ref[rows, gin_columns] * vectors_ref[4:5, :width]
+            values = act_ref[rows, base_columns]
+            act_ref[rows, gin_columns] = spread_ref[rows, :1] * (
                 grads
                 - jnp.mean(grads, -1, keepdims=True)
                 - values * jnp.mean(grads * values, -1, keepdims=True)
             )
-        )
-
-    half_batch = batch // 2
+
     done = advance(LAG + 3)
+    gin_u = act_ref.at[: batch * steps, 2 * width : 3 * width]
     for u in range(batch):
         straight = outer_ref[u // half_batch, u % half_batch].astype(f32)
-        gin_u[u] = gin_s[...].reshape(steps, ROWS, width)[:, u, :] + jnp.where(encoder, straight, 0.0)
+        gin_u[u * steps : (u + 1) * steps] = act_ref[:, gin_columns].reshape(steps, ROWS, width)[
+            :, u, :
+        ] + jnp.where(encoder, straight, 0.0)
     kept = pltpu.make_async_copy(gin_u, gin_ref, gin_sems.at[0])
-    handed = remote(gin_u, gin_ref, gin_sems.at[1], gin_sems.at[2], (1 - core, place.chip + place.along[1]))
+    away = remote(gin_u, gin_ref, gin_sems.at[1], gin_sems.at[2], (1 - core, place.chip + place.along[1]))
 
     @pl.when(mine)
     def _():
@@ -1641,13 +1675,11 @@
 
     @pl.when(jnp.logical_not(mine))
     def _():
-        handed.start()
+        away.start()
 
     own_half = pl.ds(pl.multiple_of(core * width, width), width)
     other_half = pl.ds(pl.multiple_of((1 - core) * width, width), width)
-    trade = remote(
-        vec_s.at[:, other_half], vec_other, vec_sems.at[0], vec_sems.at[1], (1 - core, place.chip)
-    )
+    trade = remote(vec_s.at[:, other_half], vec_other, vec_sems.at[0], vec_sems.at[1], other)
     trade.start()
     trade.wait_recv()
     total = vec_s[:, own_half] + vec_other[...]
@@ -1660,14 +1692,20 @@
     vecs = Fold(place, lambda kz, kf, kg: vec_parts[place.block(kz, kf, kg)], v_stage, v_near, v_far, sems_v)
     vec_line = FoldLine(place, v_parts, v_end, sems_v)
     vecs.stage_a()
+    done = advance(LAG + 5)
+    keys.stage_line()
     done = advance(len(items) - 2)
+    keys.stage_second()
     vecs.stage_b()
     done = advance(len(items) + LAG)
     for n in lines:
         v_parts[n] = vecs.summed(n)
     vec_line.begin()
+    third_sum[...] = third_line.result()
+    out_sum[...] = out_line.result()
     done = advance(len(items) + LAST_LAG)
-    mats_sum[...] = mats.result()
+    mats_sum[:part_rows] = mats_line.result()
+    mats_sum[part_rows:] = keys.result()
     vec_sum[...] = vec_line.result()
     for n, fold in enumerate(folds):
         fold.result(sum_ref.at[n * count : (n + 1) * count])
@@ -1678,48 +1716,90 @@
 
     @pl.when(jnp.logical_not(mine))
     def _():
-        handed.wait()
+        away.wait()
 
     trade.wait_send()
-    for fold in (*folds, vecs, vec_line, mats):
+    for copy in handed:
+        copy.wait_send()
+    for fold in (*folds, vecs, vec_line, mats, mats_line, keys, third, outs, third_line, out_line):
         fold.sent_all()
 
 
-def update(n_dp, batch, ht, ht_other, dpre, dpre_other, weight, base, spread, outer, vectors, dvec, mats_part):
+def backward(
+    n_dp,
+    act,
+    cell,
+    outer,
+    dq,
+    dk,
+    pair,
+    third_half,
+    out_half,
+    weight_t,
+    ht,
+    weight,
+    base,
+    spread,
+    vectors,
+    dvec,
+):
     rows, width = base.shape
-    steps = rows // ROWS
+    half_batch, steps = outer.shape[1:3]
+    batch = 2 * half_batch
     low, f32 = jnp.bfloat16, jnp.float32
     line, side = DP_LAYOUTS[n_dp][:2]
+    utt_rows = pair.shape[1]
+    mats_block = (width // n_dp, width)
+    third_block, out_block = third_half.shape[2:], out_half.shape[2:]
     block_rows = 2 * width // n_dp
     block = (max(ROWS, block_rows // FOLDS), 2 * width)
     dma = pltpu.SemaphoreType.DMA
+    rest = ((side - 1, line), (line,), (line - 1,))
     return pl.pallas_call(
-        functools.partial(update_kernel, n_dp, batch),
+        functools.partial(backward_kernel, n_dp),
         out_shape=(
             jax.ShapeDtypeStruct((block_rows, 4 * width), f32),
-            jax.ShapeDtypeStruct((batch, steps, width), f32),
+            jax.ShapeDtypeStruct((batch * steps, width), f32),
             jax.ShapeDtypeStruct((8, LANES), f32),
-            jax.ShapeDtypeStruct(mats_part.shape[1:], f32),
+            jax.ShapeDtypeStruct((2 * mats_block[0], width), f32),
+            jax.ShapeDtypeStruct(third_block, f32),
+            jax.ShapeDtypeStruct(out_block, f32),
         ),
-        in_specs=[VMEM_SPEC] * 4 + [ANY_SPEC] + [VMEM_SPEC] * 6,
-        out_specs=(VMEM_SPEC, ANY_SPEC) + (VMEM_SPEC,) * 2,
+        in_specs=[VMEM_SPEC] * 8 + [ANY_SPEC] * 7,
+        out_specs=(VMEM_SPEC, ANY_SPEC) + (VMEM_SPEC,) * 4,
         scratch_shapes=[
-            pltpu.VMEM((width, 4 * width), low),
-            pltpu.VMEM((rows, width), f32),
-            pltpu.VMEM((batch, steps, width), f32),
+            pltpu.VMEM((rows, 4 * width), f32),
+            pltpu.VMEM((4, width, width), low),
+            pltpu.VMEM((2 * width, rows), low),
+            pltpu.VMEM((2 * width, rows), low),
+            pltpu.VMEM((rows, 4 * width), low),
+            pltpu.VMEM((rows, 2 * width), low),
+            pltpu.VMEM((steps, ROWS, width), f32),
+            pltpu.VMEM((ROWS, 4 * width), low),
+            pltpu.VMEM((ROWS, width), f32),
+            pltpu.VMEM((4, utt_rows, width), low),
+            pltpu.VMEM((2, utt_rows, width), low),
+            pltpu.VMEM((2, n_dp) + mats_block, low),
+            pltpu.VMEM((line - 1, side, side) + mats_block, low),
+            pltpu.VMEM((side - 1, side) + mats_block, low),
+            pltpu.VMEM((side - 1,) + mats_block, low),
+            pltpu.VMEM((side - 1, side, line) + mats_block, low),
+        ]
+        + [
+            pltpu.VMEM(shape + size, low)
+            for size in (mats_block, third_block, out_block)
+            for shape in rest
+        ]
+        + [
             pltpu.VMEM((8, 2 * width), f32),
             pltpu.VMEM((8, width), f32),
             pltpu.VMEM((n_dp, 8, LANES), f32),
         ]
         + fold_buffers(line, side, (8, LANES), f32)
-        + [
-            pltpu.VMEM((side - 1, line, 8, LANES), f32),
-            pltpu.VMEM((line, 8, LANES), f32),
-            pltpu.VMEM((line - 1, 8, LANES), f32),
-            pltpu.VMEM((line - 1,) + mats_part.shape[1:], low),
-        ]
-        + [dma, dma((3,)), dma((2,))]
-        + [fold_sems(line, side)] * 2
+        + [pltpu.VMEM(shape + (8, LANES), f32) for shape in rest]
+        + [dma((10,)), dma((2, 4)), dma((2, 4)), dma((2,)), dma((3,)), dma((2,))]
+        + [fold_sems(line, side, first=True)]
+        + [fold_sems(line, side)] * 4
         + (
             fold_buffers(line, side, block, low)
             + [
@@ -1730,9 +1810,25 @@
         )
         * (block_rows // block[0]),
         compiler_params=pltpu.CompilerParams(
-            collective_id=4, has_side_effects=True, vmem_limit_bytes=VMEM_LIMIT
+            collective_id=3, has_side_effects=True, vmem_limit_bytes=VMEM_LIMIT
         ),
-    )(ht, ht_other, dpre, dpre_other, weight, base, spread, outer, vectors, dvec, mats_part)
+    )(
+        cell,
+        outer,
+        pair,
+        third_half,
+        out_half,
+        spread,
+        vectors,
+        dvec,
+        dq,
+        dk,
+        act,
+        weight_t,
+        ht,
+        weight,
+        base,
+    )
 
 
 STEP = 5
@@ -1791,36 +1887,34 @@
     frames, labels = jnp.where(on_first, kept, other), jnp.where(on_first, other, kept)
 
     mats_block = jnp.swapaxes(mats_copy, 1, 2)
-    out_block = jnp.pad(out_copy, ((0, 0), (0, vocab_pad - vocab_half)))
-    vec_block = jnp.pad(vec_master.astype(low).astype(f32), ((0, 0), (0, LANES - piece)))
     act, cell, ht, base, spread, vectors, pair, weight, weight_t, pairs, third, outs = forward(
-        n_dp, inputs[0], lstm_copy[0], mats_block, out_block, vec_block
-    )
-    memory, decoded = pair.reshape(2, half * length, model_width)
+        n_dp, inputs[0], lstm_copy[0], mats_block, out_copy, vec_master
+    )
+    pair = pair.reshape(2, half * length, model_width)
     pairs = pairs.reshape(2, 2 * model_width, model_width)
     third = third.reshape(2, model_width, model_width)
     outs = outs.reshape(2, model_width, vocab_pad)
     dz, dq, dk, vec_rows, logits, outer, third_half, out_half = attention(
-        n_dp, frames, labels, memory, decoded, cotangent, vectors, pairs, third, outs
+        n_dp, frames, labels, pair, cotangent, vectors, pairs, third, outs
     )
     logits = logits.reshape(batch_size, length, vocab_pad)[..., :vocab_half]
-    dpre, dpre_other, ht_other, mats_part, third_sum, out_sum = backward(
-        n_dp, act, cell, outer, dq, dk, decoded, memory, third_half, out_half, weight_t, ht
-    )
-    lstm_sum, inputs_grad, vec_sum, mats_sum = update(
+    lstm_sum, inputs_grad, vec_sum, mats_sum, third_sum, out_sum = backward(
         n_dp,
-        batch_size,
+        act,
+        cell,
+        outer,
+        dq,
+        dk,
+        pair,
+        third_half,
+        out_half,
+        weight_t,
         ht,
-        ht_other,
-        dpre,
-        dpre_other,
         weight,
         base.reshape(-1, model_width),
         spread.reshape(-1, LANES),
-        outer,
         vectors,
         vec_rows,
-        mats_part,
     )
     mats_sum = jnp.concatenate([mats_sum.reshape(2, -1, model_width), third_sum[None]], 0)
     mats_sum = jnp.swapaxes(mats_sum, 1, 2)
@@ -1838,7 +1932,7 @@
     )
     return (
         logits,
-        inputs_grad[None],
+        inputs_grad.reshape(inputs.shape),
         lstm_new,
         lstm_first_new,
         lstm_second_new,

time: 384 us -> 369 us (0.961)
  Pallas kernels: 356 us -> 345 us
    pallas_call x1 -> x0, Pallas kernels: 88.3 us -> none  [update(): pl.pallas_call(functools.partial(update_kernel, n_dp, batch), out_shape=(...]
    pallas_call x1, Pallas kernels: 61.9 us -> 139 us  [backward(): pl.pallas_call(functools.partial(backward_kernel, n_dp), out_shape=(jax.S...]
  transfers between devices with their start and end apart: 1 -> 1, of which waited for: 0 -> 0; matrix products, arithmetic and copies ran while one was open for 1% -> 0% of each run, Pallas kernels for 40% -> 41%
where the time goes in v6:
time: 369 us; the launch traced here: 362 us
  Pallas kernels  345 us (93%)
  other arithmetic  13.6 us (4%)
    pallas_call x1, Pallas kernels, forward(): pl.pallas_call(functools.partial(forward_kernel, n_dp), out_shape=(jax.Sh...  149 us
    pallas_call x1, Pallas kernels, backward(): pl.pallas_call(functools.partial(backward_kernel, n_dp), out_shape=(jax.S...  139 us
    pallas_call x1, Pallas kernels, attention(): pl.pallas_call(functools.partial(attention_kernel, n_dp), out_shape=(jax....  57.2 us
  transfers between devices with their start and end apart: 1, of which 0 were waited for; matrix products, arithmetic and copies ran while one was open for 0% of the time, Pallas kernels for 41%

profile of v6, /device:TPU:0, one launch (start us, length us, event | category | flops | bytes accessed | tf_op | source)
XLA Modules:
  0.0 362.4 jit_solution(1937981681480904149)
XLA Ops:
  0.7 0.0 copy-start.12
  0.7 0.8 fusion.6
  1.5 0.5 collective-permute-start
  1.9 149.2 %shard_map.305 = (f32[384,4096]{1,0:T(8,128)}, f32[400,1024]{1,0:T(8,128)}, bf16[2048,384]{1,0:T(8,128)(2,1)}, f32[24,16,1024]{2,1,0:T(8,128)}, f32[24,16,128]{2...) custom-call(bf16[12,24,1024]{2,1,0:T(8,128)(2,1)} %bitcast.46, ...), custom_call_target="tpu_custom_call" | custom-call | tf_op jit(solution)/shard_map/pallas_call | solution.py:581
  151.2 0.0 collective-permute-done
  151.2 0.0 copy-done.12
  151.2 0.6 broadcast_select_fusion.2
  151.8 57.2 %shard_map.306 = (bf16[144,1024]{1,0:T(8,128)(2,1)}, bf16[2,144,1024]{2,1,0:T(8,128)(2,1)}, bf16[2,144,1024]{2,1,0:T(8,128)(2,1)}, f32[8,2048]{1,0:T(8,128)}, bf...) custom-call(s32[6]{0:T(128)} %get-tuple-element.83.frames_ref, ...), custom_call_target="tpu_custom_call" | custom-call | tf_op jit(solution)/shard_map/pallas_call | solution.py:1317
  209.0 0.0 copy-start.11
  209.0 0.0 copy-start.13
  209.0 0.0 copy-start.14
  209.0 0.0 copy-start.8
  209.0 0.0 copy-start.9
  209.1 0.0 copy-start.10
  209.1 0.0 copy-start
  209.1 138.8 %shard_map.307 = (f32[128,4096]{1,0:T(8,128)}, f32[288,1024]{1,0:T(8,128)}, f32[8,128]{1,0:T(8,128)}, f32[128,1024]{1,0:T(8,128)}, f32[64,1024]{1,0:T(8,128)}, /*index=5*/f32[64,512]{1,0:T(8,128)}) custom-call(f32[400,1024]{1,0:T(8,128)} %get-tuple-element.48.cell_ref, bf16[2,6,24,1024]{3,2,1,0:T(8,128)(2,1)} %get-tuple-element.49.outer_ref, ...), custom_call_target="tpu_custom_call" | custom-call | tf_op jit(solution)/shard_map/pallas_call | solution.py:1758
  347.9 0.0 copy-done.11
  347.9 0.0 copy-done.13
  347.9 1.3 multiply_subtract_fusion.3
  349.2 1.7 fusion.8
  350.9 0.0 copy-start.4
  351.0 0.0 copy-start.5
  351.0 0.0 copy-start.7
  351.0 7.3 %fusion.12 = (bf16[1,128,4096]{2,1,0:T(8,128)(2,1)}, f32[1,128,4096]{2,1,0:T(8,128)}, f32[1,128,4096]{2,1,0:T(8,128)}, f32[1,128,4096]{2,1,0:T(8,128)}) fusion(f32[1,128,4096]{2,1,0:T(8,128)S(1)} %copy-done, f32[128,4096]{1,0:T(8,128)} %get-tuple-element.62, f32[1,128,4096]{2,1,0:T(8,128)} %param.23, f32[1,128,4096]{2,1,0:T(8,128)} %param.24), kind=kLoop, calls=%fused_computation.26 | loop fusion | flops 8388608 | bytes 15728640 | tf_op jit(solution)/shard_map/convert_element_type | solution.py:1939
  358.2 0.0 copy-done.4
  358.2 0.0 copy-done.5
  358.3 0.0 copy-done.7
  358.3 0.0 copy-start.6
  358.3 0.0 copy-start.1
  358.3 2.0 fusion.10
  360.3 0.7 copy.37
  361.0 1.0 copy.38
  (11 shorter events, 0.0 us)
Async XLA Ops:
  0.7 150.5 %copy-start.12 = (s32[1,12]{1,0:T(1,128)S(1)}, s32[1,12]{1,0:T(1,128)}, u32[]{:S(2)}) copy-start(s32[1,12]{1,0:T(1,128)} %param.19) | copy-start | bytes 148
  1.5 149.7 %collective-permute-start = (s32[6]{0:T(128)S(1)}, s32[6]{0:T(128)S(1)}, u32[]{:S(2)}, u32[]{:S(2)}) collective-permute-start(s32[6]{0:T(128)S(1)} %fusion.6), channel_id=1, source_target_pairs={{0,16},{16,0},{1,17},{17,1},{2,18},{18,2},{3,19},{19,3},{4,20},{20... | collective-permute-start | bytes 80 | tf_op jit(solution)/shard_map/ppermute | solution.py:1886
  209.0 138.9 %copy-start.11 = (f32[8,64]{1,0:T(8,128)S(1)}, f32[8,64]{1,0:T(8,128)}, u32[]{:S(2)}) copy-start(f32[8,64]{1,0:T(8,128)} %vec_part.1) | copy-start | bytes 6148
  209.0 138.9 %copy-start.13 = (f32[8,64]{1,0:T(8,128)S(1)}, f32[8,64]{1,0:T(8,128)}, u32[]{:S(2)}) copy-start(f32[8,64]{1,0:T(8,128)} %param.34) | copy-start | bytes 6148
  209.0 138.9 %copy-start.14 = (f32[8,64]{1,0:T(8,128)S(1)}, f32[8,64]{1,0:T(8,128)}, u32[]{:S(2)}) copy-start(f32[8,64]{1,0:T(8,128)} %param.35) | copy-start | bytes 6148
  209.0 140.2 %copy-start.8 = (f32[64,500]{1,0:T(8,128)S(1)}, f32[64,500]{1,0:T(8,128)}, u32[]{:S(2)}) copy-start(f32[64,500]{1,0:T(8,128)} %param.29) | copy-start | bytes 384004
  209.0 140.2 %copy-start.9 = (f32[64,500]{1,0:T(8,128)S(1)}, f32[64,500]{1,0:T(8,128)}, u32[]{:S(2)}) copy-start(f32[64,500]{1,0:T(8,128)} %param.31) | copy-start | bytes 384004
  209.1 140.2 %copy-start.10 = (f32[64,500]{1,0:T(8,128)S(1)}, f32[64,500]{1,0:T(8,128)}, u32[]{:S(2)}) copy-start(f32[64,500]{1,0:T(8,128)} %param.32) | copy-start | bytes 384004
  209.1 141.9 %copy-start = (f32[1,128,4096]{2,1,0:T(8,128)S(1)}, f32[1,128,4096]{2,1,0:T(8,128)}, u32[]{:S(2)}) copy-start(f32[1,128,4096]{2,1,0:T(8,128)} %param.21) | copy-start | bytes 6291460
  350.9 7.3 %copy-start.2 = (f32[3,1024,64]{1,2,0:T(8,128)S(1)}, f32[3,1024,64]{1,2,0:T(8,128)}, u32[]{:S(2)}) copy-start(f32[3,1024,64]{1,2,0:T(8,128)} %param.25) | copy-start | bytes 2359300
  350.9 7.3 %copy-start.3 = (f32[3,1024,64]{1,2,0:T(8,128)S(1)}, f32[3,1024,64]{1,2,0:T(8,128)}, u32[]{:S(2)}) copy-start(f32[3,1024,64]{1,2,0:T(8,128)} %param.27) | copy-start | bytes 2359300
  350.9 7.3 %copy-start.4 = (f32[3,1024,64]{1,2,0:T(8,128)S(1)}, f32[3,1024,64]{1,2,0:T(8,128)}, u32[]{:S(2)}) copy-start(f32[3,1024,64]{1,2,0:T(8,128)} %param.28) | copy-start | bytes 2359300
  351.0 7.3 %copy-start.5 = (f32[128,1024]{1,0:T(8,128)S(1)}, f32[128,1024]{1,0:T(8,128)}, u32[]{:S(2)}) copy-start(f32[128,1024]{1,0:T(8,128)} %get-tuple-element.63) | copy-start | bytes 1572868
  351.0 7.3 %copy-start.7 = (f32[64,1024]{1,0:T(8,128)S(1)}, f32[64,1024]{1,0:T(8,128)}, u32[]{:S(2)}) copy-start(f32[64,1024]{1,0:T(8,128)} %get-tuple-element.64) | copy-start | bytes 786436
  358.3 2.0 copy-start.6
  358.3 2.7 copy-start.1
